TPU v7x, 32 devices: a whole 2x2x4 slice. The times are simulated.
32 devices in a mesh: groups: 2 (over y), segment: 8 (over z, x), template: 2 (over core).
Axes of the slice: x: 2, y: 2, z: 4, core: 2. Of those that a mesh axis runs over, the one named last changes fastest.
Arguments:
- strain_frames: bfloat16 [64, 16384], P('segment'), may hold values from -6 to 6
- frame_slot: int32 [8, 8], replicated, may hold values from 0 to 7, as said below
- templates: bfloat16 [4, 2, 131072], P(('groups', 'template'), None, 'segment'), parts along dimension 0, may hold values from -6 to 6
- bin_edges: int32 [4, 3], P(('groups', 'template')), parts along dimension 0, may hold values from 16384 to 114687, as said below
Outputs:
- snr_series: bfloat16 [8, 4, 131072], P('segment', ('groups', 'template')), parts along dimension 1
- chisq_series: bfloat16 [8, 4, 131072], P('segment', ('groups', 'template')), parts along dimension 1
- peak_newsnr: float32 [8, 4], P('segment', ('groups', 'template')), parts along dimension 1
There are 2 independent parts, one for each index of `groups`. A program takes and returns all parts, laid end to end along the dimension named above; an argument that names none is the same for every part. Nothing has to cross between parts.
Inputs may be any that keep to these rules, and one draw needn't show every extreme that they name: Each column frame_slot[:, j] is a permutation of 0 to 7. `bin_edges`: edge number e of a template lies in [(2 e + 1) * 16384, (2 e + 3) * 16384), so the edges rise.
All inputs are finite; a program needn't handle non-finite values.
Results may differ from a plain program's by a relative error of at most 0.011.
Values may be sent and summed in bfloat16 or wider, within the bound.
No kernel may reach another device: no remote copies, remote signals or barrier semaphores. Data moves between devices by JAX's collectives and lax.ppermute only.
A program may use at most 64 MiB of HBM per device.

v0:
```python
import math

import jax
import jax.numpy as jnp
from jax import lax
from jax.sharding import PartitionSpec as P

RADIX_A = 64
RADIX_B = 32
RADIX_C = 128


def dft_table(length, orient):
    counter = jnp.arange(length, dtype=jnp.int32)
    product = counter[:, None] * counter[None, :] % length
    angles = orient * 2.0 * math.pi / length * product.astype(jnp.float32)
    cosine = jnp.cos(angles)
    sine = jnp.sin(angles)
    upper = jnp.stack([cosine, -sine], axis=1)
    lower = jnp.stack([sine, cosine], axis=1)
    return jnp.stack([upper, lower], axis=0).astype(jnp.bfloat16)


def rotate(values, phase_index, modulus, orient):
    angles = orient * 2.0 * math.pi / modulus * (phase_index % modulus).astype(jnp.float32)
    cosine = jnp.cos(angles)
    sine = jnp.sin(angles)
    real_part = values[0] * cosine - values[1] * sine
    imag_part = values[0] * sine + values[1] * cosine
    return jnp.stack([real_part, imag_part]).astype(jnp.bfloat16)


def later_passes(level_one, orient, table_three):
    length = RADIX_A * RADIX_B * RADIX_C
    inner = RADIX_B * RADIX_C
    grid_one = (
        jnp.arange(RADIX_A, dtype=jnp.int32)[:, None] * jnp.arange(inner, dtype=jnp.int32)[None, :]
    )
    turned = rotate(level_one, grid_one, length, orient).reshape(2, RADIX_A, RADIX_B, RADIX_C)
    level_two = jnp.einsum(
        "cjdp,dkpr->ckjr", dft_table(RADIX_B, orient), turned, preferred_element_type=jnp.float32
    )
    grid_two = (
        jnp.arange(RADIX_B, dtype=jnp.int32)[:, None]
        * jnp.arange(RADIX_C, dtype=jnp.int32)[None, :]
    )
    turned_two = rotate(level_two, grid_two, inner, orient)
    level_three = jnp.einsum(
        "cldr,dkjr->ckjl", table_three, turned_two, preferred_element_type=jnp.float32
    )
    rows = table_three.shape[1]
    return jnp.transpose(level_three, (0, 3, 2, 1)).reshape(2, rows * inner * RADIX_A // RADIX_C)


def forward_spectrum(real_signal):
    inner = RADIX_B * RADIX_C
    start = real_signal.reshape(RADIX_A, inner)
    table_one = dft_table(RADIX_A, -1.0)[:, :, 0, :]
    level_one = jnp.einsum("ckp,pq->ckq", table_one, start, preferred_element_type=jnp.float32)
    table_three = dft_table(RADIX_C, -1.0)[:, : RADIX_C // 2]
    return later_passes(level_one, -1.0, table_three)


def inverse_kept(masked):
    inner = RADIX_B * RADIX_C
    start = masked.reshape(2, RADIX_A // 2, inner)
    table_one = dft_table(RADIX_A, 1.0)[:, :, :, : RADIX_A // 2]
    level_one = jnp.einsum("ckdp,dpq->ckq", table_one, start, preferred_element_type=jnp.float32)
    table_three = dft_table(RADIX_C, 1.0)[:, RADIX_C // 4 : RADIX_C // 4 + RADIX_C // 2]
    return later_passes(level_one, 1.0, table_three)


def filter_template(spectrum, template, edges):
    length = RADIX_A * RADIX_B * RADIX_C
    kept = length // 2
    temp_real = template[0].astype(jnp.float32)
    temp_imag = template[1].astype(jnp.float32)
    corr_real = spectrum[0] * temp_real + spectrum[1] * temp_imag
    corr_imag = spectrum[1] * temp_real - spectrum[0] * temp_imag
    power = temp_real * temp_real + temp_imag * temp_imag
    total = jnp.sum(power)
    bin_index = jnp.arange(kept, dtype=jnp.int32)
    label = (
        (bin_index >= edges[0]).astype(jnp.int32)
        + (bin_index >= edges[1]).astype(jnp.int32)
        + (bin_index >= edges[2]).astype(jnp.int32)
    )
    pieces = []
    shares = []
    for number in range(4):
        inside = (label == number).astype(jnp.float32)
        shares.append(jnp.sum(power * inside) / total)
        masked = jnp.stack([corr_real * inside, corr_imag * inside]).astype(jnp.bfloat16)
        pieces.append(inverse_kept(masked) / length)
    summed = pieces[0] + pieces[1] + pieces[2] + pieces[3]
    scale = length / total
    snr = jnp.sqrt((summed[0] * summed[0] + summed[1] * summed[1]) * scale)
    chisq = jnp.zeros_like(snr)
    for number in range(4):
        diff_real = pieces[number][0] - shares[number] * summed[0]
        diff_imag = pieces[number][1] - shares[number] * summed[1]
        chisq = chisq + diff_real * diff_real + diff_imag * diff_imag
    chisq = chisq * scale
    reduced = chisq / 6.0
    weighted = snr * ((1.0 + reduced * reduced * reduced) / 2.0) ** (-1.0 / 6.0)
    newsnr = jnp.where(reduced > 1.0, weighted, snr)
    return (snr.astype(jnp.bfloat16), chisq.astype(jnp.bfloat16), jnp.max(newsnr))


def local(strain_frames, frame_slot, templates, bin_edges):
    segments_count = lax.axis_size("segment")
    position = lax.axis_index("segment")
    frame_length = strain_frames.shape[1]
    length = RADIX_A * RADIX_B * RADIX_C
    kept = length // 2
    counter = jnp.arange(segments_count, dtype=jnp.int32)
    slot_now = lax.dynamic_slice_in_dim(frame_slot, position, 1, 1)[:, 0]
    next_index = jnp.minimum(position + 1, segments_count - 1)
    slot_next = lax.dynamic_slice_in_dim(frame_slot, next_index, 1, 1)[:, 0]

    def arrange(slots, frames):
        selector = (counter[:, None] == slots[None, :]).astype(jnp.bfloat16)
        return (
            jnp.dot(selector, frames, preferred_element_type=jnp.float32)
            .astype(jnp.bfloat16)
            .reshape(kept)
        )

    following_rows = jnp.concatenate(
        [strain_frames[1:], jnp.zeros((1, frame_length), jnp.bfloat16)], axis=0
    )
    outgoing = jnp.stack([strain_frames, following_rows], axis=1)
    received = lax.all_to_all(outgoing, "segment", split_axis=0, concat_axis=0, tiled=True)
    leading = arrange(slot_now, received[:, 0])
    trailing = arrange(slot_next, received[:, 1])
    segment_data = jnp.concatenate([leading, trailing])
    whole_templates = lax.all_gather(templates, "segment", axis=2, tiled=True)
    spectrum = forward_spectrum(segment_data)
    snr_one, chisq_one, peak_one = filter_template(spectrum, whole_templates[0], bin_edges[0])
    snr_rows = [snr_one]
    chisq_rows = [chisq_one]
    peak_rows = [peak_one]
    snr_series = jnp.stack(snr_rows)[None]
    chisq_series = jnp.stack(chisq_rows)[None]
    peak_newsnr = jnp.stack(peak_rows)[None]
    return (snr_series, chisq_series, peak_newsnr)


def solution(mesh):
    in_specs = (
        P("segment", None),
        P(),
        P(("groups", "template"), None, "segment"),
        P(("groups", "template"), None),
    )
    out_specs = (
        P("segment", ("groups", "template"), None),
        P("segment", ("groups", "template"), None),
        P("segment", ("groups", "template")),
    )
    return jax.shard_map(local, mesh=mesh, in_specs=in_specs, out_specs=out_specs, check_vma=False)
```

profile of v0, /device:TPU:0, one launch (start us, length us, event | category | flops | bytes accessed | tf_op | source)
XLA Modules:
  0.0 121.7 jit_solution(296445114597201190)
XLA Ops:
  0.6 1.0 slice.196
  1.7 1.0 pad_maximum_fusion
  2.7 1.3 %copy.65 = bf16[8,2,16384]{2,1,0:T(2,128)(2,1)} copy(bf16[8,2,16384]{2,0,1:T(8,128)(2,1)S(1)} %pad_maximum_fusion) | data formatting | bytes 1048576 | tf_op jit(solution)/shard_map/stack | solution.py:132
  4.1 7.3 %all-to-all-start = ((bf16[8,2,16384]{2,1,0:T(2,128)(2,1)}), bf16[8,2,16384]{2,1,0:T(2,128)(2,1)S(1)}, u32[]{:S(2)}, u32[]{:S(2)}) async-start(bf16[8,2,16384]{2,1,0:T(2,128)(2,1)} %copy.65), calls=%async_computation | async-start | bytes 1048576 | tf_op jit(solution)/shard_map/all_to_all | solution.py:133
  14.4 35.5 %all_gather.3 = bf16[1,2,131072]{2,1,0:T(2,128)(2,1)S(1)} all-gather(bf16[1,2,16384]{2,1,0:T(2,128)(2,1)S(1)} %copy-done.3), channel_id=1, replica_groups=mesh['groups'=2,'segment'=8,'template'=2] {'segment'}, dimensions={2}, use_global_device_ids=true | all-gather | bytes 589824 | tf_op jit(solution)/shard_map/all_gather | solution.py:137
  49.9 4.1 %fusion.81 = (f32[131072]{0:T(1024)S(1)}, f32[131072]{0:T(1024)S(1)}, f32[]{:T(128)}, f32[1,1,131072]{2,1,0:T(1,128)S(1)}) fusion(bf16[1,2,131072]{2,1,0:T(2,128)(2,1)S(1)} %all_gather.3), kind=kLoop, calls=%fused_computation.186 | loop fusion | flops 786431 | bytes 2097156 | tf_op jit(solution)/shard_map/convert_element_type | solution.py:76
  54.0 2.9 %select_reduce_fusion.3 = (f32[]{:T(128)}, f32[]{:T(128)}, f32[]{:T(128)}, f32[]{:T(128)}) fusion(f32[131072]{0:T(1024)S(1)} %bitcast.310, s32[]{:T(128)} %bitcast.4, s32[]{:T(128)} %bitcast.3, s32[]{:T(128)} %bitcast.2), kind=kLoop, calls=%fused_computation.155 | loop fusion | flops 2621436 | bytes 524316 | tf_op jit(solution)/shard_map/reduce_sum | solution.py:92
  67.9 4.8 %fusion.79 = (bf16[8,8,32,128]{3,1,2,0:T(8,128)(2,1)S(1)}, bf16[8,8,32,128]{3,1,2,0:T(8,128)(2,1)S(1)}) fusion(f32[2,64,4096]{2,1,0:T(8,128)S(1)} %fusion.57), kind=kLoop, calls=%fused_computation.184 | loop fusion | flops 5767168 | bytes 3145728
  74.3 1.1 copy.71
  75.8 1.1 copy.70
  77.3 3.3 %select_convert_fusion.5 = (bf16[1,32,4096]{2,1,0:T(8,128)(2,1)S(1)}, bf16[1,32,4096]{2,1,0:T(8,128)(2,1)S(1)}, bf16[1,32,4096]{2,1,0:T(8,128)(2,1)S(1)}, bf16[1,32,4096]{2,1,0:T(8,128)(2,1)S(1)}) fusion(s32[]{:T(128)} %bitcast.4, s32[]{:T(128)} %bitcast.3, s32[]{:T(128)} %bitcast.2, f32[1,32,4096]{2,1,0:T(8,128)S(1)} %squeeze.55, ...), kind=kLoop, calls=%fused_computation.170 | loop fusion | flops 2752512 | bytes 3145740 | tf_op jit(solution)/shard_map/convert.25
  80.5 2.3 %select_convert_fusion.6 = (bf16[1,32,4096]{2,1,0:T(8,128)(2,1)S(1)}, bf16[1,32,4096]{2,1,0:T(8,128)(2,1)S(1)}, bf16[1,32,4096]{2,1,0:T(8,128)(2,1)S(1)}, bf16[1...) fusion(bf16[1,32,4096]{2,1,0:T(8,128)(2,1)S(1)} %get-tuple-element.42, ...), kind=kLoop, calls=%fused_computation.171 | loop fusion | flops 2490368 | bytes 2097164 | tf_op jit(solution)/shard_map/convert.50
  83.3 4.6 %fusion.49 = (bf16[8,8,32,128]{3,1,2,0:T(8,128)(2,1)S(1)}, bf16[8,8,32,128]{3,1,2,0:T(8,128)(2,1)S(1)}) fusion(f32[2,64,4096]{2,1,0:T(8,128)S(1)} %convolution_bitcast_fusion.3), kind=kLoop, calls=%fused_computation.114 | loop fusion | flops 5767168 | bytes 3145728
  88.6 4.6 %fusion.51 = (bf16[8,8,32,128]{3,1,2,0:T(8,128)(2,1)S(1)}, bf16[8,8,32,128]{3,1,2,0:T(8,128)(2,1)S(1)}) fusion(f32[2,64,4096]{2,1,0:T(8,128)S(1)} %convolution_bitcast_fusion.2), kind=kLoop, calls=%fused_computation.116 | loop fusion | flops 5767168 | bytes 3145728
  94.0 4.6 %fusion.53 = (bf16[8,8,32,128]{3,1,2,0:T(8,128)(2,1)S(1)}, bf16[8,8,32,128]{3,1,2,0:T(8,128)(2,1)S(1)}) fusion(f32[2,64,4096]{2,1,0:T(8,128)S(1)} %convolution_bitcast_fusion.1), kind=kLoop, calls=%fused_computation.118 | loop fusion | flops 5767168 | bytes 3145728
  99.3 4.8 %fusion.55 = (bf16[8,8,32,128]{3,1,2,0:T(8,128)(2,1)S(1)}, bf16[8,8,32,128]{3,1,2,0:T(8,128)(2,1)S(1)}) fusion(f32[2,64,4096]{2,1,0:T(8,128)S(1)} %convolution_bitcast_fusion), kind=kLoop, calls=%fused_computation.120 | loop fusion | flops 5767168 | bytes 3145728
  106.3 1.3 %subtract_convert_fusion.4 = (bf16[1,64,32,128]{3,2,0,1:T(8,128)(2,1)S(1)}, bf16[1,64,32,128]{3,2,0,1:T(8,128)(2,1)S(1)}, bf16[1,64,32,128]{3,2,0,1:T(8,128)(2,1...) fusion(f32[2,64,32,128]{3,2,0,1:T(8,128)S(1)} %convolution_bitc, ...), kind=kLoop, calls=%fused_computation.90 | loop fusion | flops 8388608 | bytes 12615680 | tf_op jit(solution)/shard_map/convert.19
  109.5 2.4 %broadcast_multiply_fusion = (f32[1,64,32,64]{1,2,0,3:T(8,128)S(1)}, bf16[1,64,32,64]{1,2,0,3:T(8,128)(2,1)}, bf16[1,64,32,64]{1,2,0,3:T(8,128)(2,1)}, f32[1,64,32,64]{1,2,0,3:T(8,128)S(1)}) fusion(f32[]{:T(128)S(6)} %div.55, f32[2,64,32,64]{1,2,0,3:T(8,128)S(1)} %get-tuple-element.79, f32[]{:T(128)S(6)} %div.59, f32[2,64,32,64]{1,2,0,3:T(8,128)S(1)} %fusion.1, ...), kind=kLoop, calls=%fused_computation.151 | loop fusion | flops 5111808 | bytes 6815764 | tf_op jit(solution)/shard_map/div | solution.py:104
  112.0 1.1 copy.86
  114.0 2.1 %copy.85 = bf16[1,64,32,64]{3,2,1,0:T(8,128)(2,1)S(1)} copy(bf16[1,64,32,64]{1,2,0,3:T(8,128)(2,1)} %get-tuple-element.12) | data formatting | bytes 524288 | tf_op jit(solution)/shard_map/convert_element_type | solution.py:107
  116.2 1.1 reshape.1302
  117.3 1.1 copy.84
  118.3 1.1 sqrt.17
  119.4 1.1 copy.87
  (90 shorter events, 19.3 us)
Async XLA Ops:
  1.6 12.1 %copy-start.5 = (s32[1,3]{1,0:T(1,128)S(1)}, s32[1,3]{1,0:T(1,128)}, u32[]{:S(2)}) copy-start(s32[1,3]{1,0:T(1,128)} %param.7) | copy-start | bytes 40
  1.7 12.7 %copy-start.3 = (bf16[1,2,16384]{2,1,0:T(2,128)(2,1)S(1)}, bf16[1,2,16384]{2,1,0:T(2,128)(2,1)}, u32[]{:S(2)}) copy-start(bf16[1,2,16384]{2,1,0:T(2,128)(2,1)} %param.6) | copy-start | bytes 196612
  4.1 61.2 %all-to-all-start = ((bf16[8,2,16384]{2,1,0:T(2,128)(2,1)}), bf16[8,2,16384]{2,1,0:T(2,128)(2,1)S(1)}, u32[]{:S(2)}, u32[]{:S(2)}) async-start(bf16[8,2,16384]{2,1,0:T(2,128)(2,1)} %copy.65), calls=%async_computation | async-start | bytes 1048576 | tf_op jit(solution)/shard_map/all_to_all | solution.py:133
  49.9 14.7 %copy-start.4 = (s32[8,8]{1,0:T(8,128)S(1)}, s32[8,8]{1,0:T(8,128)}, u32[]{:S(2)}) copy-start(s32[8,8]{1,0:T(8,128)} %param.5) | copy-start | bytes 772
  75.8 1.5 %copy-start = (f32[1,32,4096]{2,1,0:T(8,128)S(1)}, f32[1,32,4096]{2,1,0:T(8,128)}, u32[]{:S(2)}) copy-start(f32[1,32,4096]{2,1,0:T(8,128)} %reshape.1209) | copy-start | bytes 1572868
  113.0 4.2 %copy-start.1 = (bf16[1,64,32,64]{1,2,0,3:T(8,128)(2,1)S(1)}, bf16[1,64,32,64]{1,2,0,3:T(8,128)(2,1)}, u32[]{:S(2)}) copy-start(bf16[1,64,32,64]{1,2,0,3:T(8,128)(2,1)} %get-tuple-element.31) | copy-start | bytes 786436
  119.4 1.3 %copy-start.2 = (f32[131072]{0:T(1024)S(1)}, f32[131072]{0:T(1024)}, u32[]{:S(2)}) copy-start(f32[131072]{0:T(1024)} %reshape.1304) | copy-start | bytes 1572868
where the time goes:
time: 122 us
  other arithmetic  44.6 us (37%)
  blocking collectives  35.5 us (29%)
  local copies, waits for them, and re-layouts  19.4 us (16%)
  matrix products  7.79 us (6%)
  starting transfers between devices  7.25 us (6%)
  between operations  7.15 us (6%)
    all_gather x1, blocking collectives, local(): whole_templates = lax.all_gather(templates, 'segment', axis=2, tiled=True)  35.5 us
    unnamed x5, other arithmetic  23.3 us
    another operation x19, other arithmetic  9.6 us
    all_to_all x1, starting transfers between devices, local(): lax.all_to_all(outgoing, 'segment', split_axis=0, concat_axis=0, tiled=True)  7.25 us
    convert_element_type x1, other arithmetic, filter_template(): temp_real = template[0].astype(jnp.float32)  4.07 us
    convert_element_type x2, local copies, waits for them, and re-layouts, filter_template(): chisq.astype(jnp.bfloat16)  3.2 us
    reduce_sum x1, other arithmetic, filter_template(): shares.append(jnp.sum(power * inside) / total)  2.89 us
  transfers between devices with their start and end apart: 1, of which 0 were waited for; matrix products, arithmetic and copies ran while one was open for 10% of the time, Pallas kernels for 0%

commit v1 on v0

v1 whole, which is shorter than its diff:
```python
import math

import jax
import jax.numpy as jnp
import ml_dtypes
import numpy as np
from jax import lax
from jax.experimental import pallas as pl
from jax.experimental.pallas import tpu as pltpu
from jax.sharding import PartitionSpec as P

SIDE = 512
HALF = SIDE // 2
LENGTH = SIDE * SIDE
AXES = ("groups", "segment", "template")
MIB = 1 << 20
BIN_LOW = (0, 32, 96, 128)


def turn(rows, columns, modulus):
    product = np.outer(rows, columns) % modulus
    angles = 2.0 * math.pi / modulus * product.astype(np.float64)
    return np.cos(angles), np.sin(angles)


def tables():
    digit = np.arange(SIDE)
    cosine, sine = turn(digit, digit, SIDE)
    first = np.concatenate([cosine, -sine], axis=0)
    low = slice(0, HALF)
    second = np.block([[cosine[:, low], -sine[:, low]], [sine[:, low], cosine[:, low]]])
    third = []
    column = np.arange(HALF // 2)
    for start in BIN_LOW:
        chosen = np.where(column >= start, column, column + HALF // 2)
        third.append(
            np.block([[cosine[chosen], sine[chosen]], [-sine[chosen], cosine[chosen]]])
        )
    kept = slice(HALF // 2, HALF // 2 + HALF)
    fourth = np.block([[cosine[kept], -sine[kept]], [sine[kept], cosine[kept]]])
    phase_cos, phase_sin = turn(digit, digit, LENGTH)
    phase = np.stack([phase_cos, phase_sin]).astype(np.float32)


    narrow = [x.astype(np.float32).astype(ml_dtypes.bfloat16) for x in (first, second, np.stack(third), fourth)]
    return (*narrow, phase)


def in_vmem(*arrays):
    return [pltpu.with_memory_space_constraint(x, pltpu.VMEM) for x in arrays]


def split_frames(frames):
    count, samples = frames.shape
    rows = samples // SIDE
    tiles = SIDE // 128

    def body(frames_ref, out_ref, wide):
        core = lax.axis_index("template")
        wide[:, count * rows :, :] = jnp.zeros((tiles, rows, 128), jnp.float32)
        for row in range(rows):
            for tile in range(tiles):
                place = (row * tiles + tile) * 128
                wide[tile, pl.ds(row, count, stride=rows), :] = frames_ref[
                    :, place : place + 128
                ].astype(jnp.float32)
        for tile in range(tiles):
            moved = wide[tile, pl.ds(pl.multiple_of(core * rows, rows), count * rows), :]
            out_ref[:, :, tile * 128 : tile * 128 + 128] = moved.astype(jnp.bfloat16).reshape(
                count, rows, 128
            )

    return pl.pallas_call(
        body,
        out_shape=pltpu.VMEM((count, rows, SIDE), jnp.bfloat16),
        in_specs=[pl.BlockSpec(memory_space=pltpu.VMEM)],
        out_specs=pl.BlockSpec(memory_space=pltpu.VMEM),
        scratch_shapes=[pltpu.VMEM((tiles, (count + 1) * rows, 128), jnp.float32)],
        compiler_params=pltpu.CompilerParams(vmem_limit_bytes=16 * MIB),
        name="split_frames",
    )(frames)


def forward_body(signal, first, second, phase, spectrum, turned):
    rows = SIDE // 2

    def chunk(index, carry):
        here = pl.ds(pl.multiple_of(index * rows, rows), rows)
        there = pl.ds(pl.multiple_of(SIDE + index * rows, rows), rows)
        real = jnp.dot(first[here, :], signal[...], preferred_element_type=jnp.float32)
        imag = jnp.dot(first[there, :], signal[...], preferred_element_type=jnp.float32)
        cosine, sine = phase[0, here, :], phase[1, here, :]
        turned[here, :SIDE] = (real * cosine + imag * sine).astype(jnp.bfloat16)
        turned[here, SIDE:] = (imag * cosine - real * sine).astype(jnp.bfloat16)
        spectrum[here, :] = jnp.dot(
            turned[here, :], second[...], preferred_element_type=jnp.float32
        )
        return carry

    lax.fori_loop(0, SIDE // rows, chunk, 0)


def forward_received(own, other, frame_slot, first, second, phase):
    count, rows, _ = own.shape

    def body(own_ref, other_ref, slot_ref, first_ref, second_ref, phase_ref, spectrum, signal, turned):
        segment = lax.axis_index("segment")
        core = lax.axis_index("template")
        for part, frames in ((core, own_ref), (1 - core, other_ref)):
            half = jnp.minimum(segment + part, count - 1)
            for source in range(count):
                start = part * HALF + slot_ref[source, half] * rows
                signal[pl.ds(pl.multiple_of(start, rows), rows), :] = frames[source]
        forward_body(signal, first_ref, second_ref, phase_ref, spectrum, turned)

    vmem = pl.BlockSpec(memory_space=pltpu.VMEM)
    return pl.pallas_call(
        body,
        out_shape=pltpu.VMEM((SIDE, SIDE), jnp.float32),
        in_specs=[vmem, vmem, pl.BlockSpec(memory_space=pltpu.SMEM), vmem, vmem, vmem],
        out_specs=vmem,
        scratch_shapes=[
            pltpu.VMEM((SIDE, SIDE), jnp.bfloat16),
            pltpu.VMEM((SIDE, 2 * SIDE), jnp.bfloat16),
        ],
        compiler_params=pltpu.CompilerParams(vmem_limit_bytes=32 * MIB),
        cost_estimate=pl.CostEstimate(
            flops=4 * SIDE**3 * 2, bytes_accessed=6 * MIB, transcendentals=0
        ),
        name="forward",
    )(own, other, frame_slot, *in_vmem(first, second, phase))


def forward_arranged(signal, first, second, phase):
    def body(signal_ref, first_ref, second_ref, phase_ref, spectrum, turned):
        forward_body(signal_ref, first_ref, second_ref, phase_ref, spectrum, turned)

    vmem = pl.BlockSpec(memory_space=pltpu.VMEM)
    return pl.pallas_call(
        body,
        out_shape=pltpu.VMEM((SIDE, SIDE), jnp.float32),
        in_specs=[vmem] * 4,
        out_specs=vmem,
        scratch_shapes=[pltpu.VMEM((SIDE, 2 * SIDE), jnp.bfloat16)],
        compiler_params=pltpu.CompilerParams(vmem_limit_bytes=32 * MIB),
        name="forward",
    )(signal, *in_vmem(first, second, phase))


def owners_of(segment, core, doubled):
    if not doubled:
        return [[0]]
    near, far = 2 - core, 1 + core
    masks = [[0], [4], [near, near ^ 4], [far, far ^ 4, far ^ near, far ^ near ^ 4]]
    return [[segment ^ mask for mask in block] for block in masks]


def inverse(spectrum, blocks, edges, third, fourth, phase, doubled):
    n_blocks = len(blocks)
    shard = blocks[0].shape[2]
    quarter = HALF // 2
    rows = SIDE // 2
    wide = SIDE // 2

    def body(*refs):
        spectrum_ref, block_refs = refs[0], refs[1 : 1 + n_blocks]
        edge_ref, third_ref, fourth_ref, phase_ref = refs[1 + n_blocks : 5 + n_blocks]
        snr_ref, chisq_ref, peak_ref = refs[5 + n_blocks : 8 + n_blocks]
        gathered, flipped, masked, turned, sums = refs[8 + n_blocks :]
        segment = lax.axis_index("segment")
        core = lax.axis_index("template")
        for block, owners in zip(block_refs, owners_of(segment, core, doubled), strict=True):
            for place, owner in enumerate(owners):
                here = pl.ds(pl.multiple_of(owner * shard, shard), shard)
                for part in range(2):
                    gathered[part, here, :] = block[place, part]
        for part in range(2):
            flipped[:, part * HALF : (part + 1) * HALF] = gathered[part].T
        edge = [edge_ref[0, number] for number in range(3)]
        sums[...] = jnp.zeros_like(sums)
        step = 32

        def correlate(index, carry):
            here = pl.ds(pl.multiple_of(index * step, step), step)
            spec_real = [spectrum_ref[here, q * quarter : (q + 1) * quarter] for q in range(2)]
            spec_imag = [spectrum_ref[here, (q + 2) * quarter : (q + 3) * quarter] for q in range(2)]
            temp_real = [
                flipped[here, q * quarter : (q + 1) * quarter].astype(jnp.float32) for q in range(2)
            ]
            temp_imag = [
                flipped[here, (q + 2) * quarter : (q + 3) * quarter].astype(jnp.float32)
                for q in range(2)
            ]
            lane = lax.broadcasted_iota(jnp.int32, (step, quarter), 1)
            base = lane * SIDE + lax.broadcasted_iota(jnp.int32, (step, quarter), 0) + index * step
            zero = jnp.zeros((step, quarter), jnp.float32)
            corr, above, power = [], [], []
            for q in range(2):
                corr.append(
                    (
                        spec_real[q] * temp_real[q] + spec_imag[q] * temp_imag[q],
                        spec_imag[q] * temp_real[q] - spec_real[q] * temp_imag[q],
                    )
                )
                power.append(temp_real[q] * temp_real[q] + temp_imag[q] * temp_imag[q])
                bins = base + q * quarter * SIDE
                above.append([bins >= edge[number] for number in range(3)])
            inside = [
                [~above[0][0], None],
                [above[0][0] & ~above[0][1], ~above[1][1]],
                [above[0][1] & ~above[0][2], above[1][1] & ~above[1][2]],
                [None, above[1][2]],
            ]
            inside[1][1] = ~above[1][1] & above[1][0]
            for number in range(4):
                first_half, second_half = inside[number]
                if second_half is None:
                    chosen = [jnp.where(first_half, corr[0][part], zero) for part in range(2)]
                    strength = jnp.where(first_half, power[0], zero)
                elif first_half is None:
                    chosen = [jnp.where(second_half, corr[1][part], zero) for part in range(2)]
                    strength = jnp.where(second_half, power[1], zero)
                else:
                    chosen = [
                        jnp.where(
                            first_half, corr[0][part], jnp.where(second_half, corr[1][part], zero)
                        )
                        for part in range(2)
                    ]
                    strength = jnp.where(first_half, power[0], zero) + jnp.where(
                        second_half, power[1], zero
                    )
                for part in range(2):
                    masked[number, here, part * quarter : (part + 1) * quarter] = chosen[
                        part
                    ].astype(jnp.bfloat16)
                folded = strength[0:8]
                for start in range(8, step, 8):
                    folded = folded + strength[start : start + 8]
                sums[number] += folded
            return carry

        lax.fori_loop(0, SIDE // step, correlate, 0)

        def first_pass(index, carry):
            number, part = index // (SIDE // rows), index % (SIDE // rows)
            here = pl.ds(pl.multiple_of(part * rows, rows), rows)
            there = pl.ds(pl.multiple_of(SIDE + part * rows, rows), rows)
            product = jnp.dot(
                masked[number, here, :], third_ref[number], preferred_element_type=jnp.float32
            )
            real, imag = product[:, :SIDE], product[:, SIDE:]
            cosine, sine = phase_ref[0, here, :], phase_ref[1, here, :]
            turned[number, here, :] = (real * cosine - imag * sine).astype(jnp.bfloat16)
            turned[number, there, :] = (real * sine + imag * cosine).astype(jnp.bfloat16)
            return carry

        lax.fori_loop(0, 4 * (SIDE // rows), first_pass, 0)

        bin_power = [jnp.sum(sums[number]) for number in range(4)]
        total = (bin_power[0] + bin_power[1]) + (bin_power[2] + bin_power[3])
        total_row = jnp.full((1, wide), total, jnp.float32)
        shares = [jnp.full((1, wide), bin_power[number], jnp.float32) / total_row for number in range(4)]
        scale = (1.0 / LENGTH) / total_row

        def second_pass(index, peak):
            columns = pl.ds(pl.multiple_of(index * wide, wide), wide)
            pieces = [
                jnp.dot(
                    fourth_ref[...], turned[number, :, columns], preferred_element_type=jnp.float32
                )
                for number in range(4)
            ]
            real = [piece[:HALF] for piece in pieces]
            imag = [piece[HALF:] for piece in pieces]
            sum_real = (real[0] + real[1]) + (real[2] + real[3])
            sum_imag = (imag[0] + imag[1]) + (imag[2] + imag[3])
            snr = jnp.sqrt((sum_real * sum_real + sum_imag * sum_imag) * scale)
            chisq = jnp.zeros_like(snr)
            for number in range(4):
                diff_real = real[number] - shares[number] * sum_real
                diff_imag = imag[number] - shares[number] * sum_imag
                chisq = chisq + (diff_real * diff_real + diff_imag * diff_imag)
            chisq = chisq * scale
            reduced = chisq / 6.0
            inner = (1.0 + reduced * reduced * reduced) / 2.0
            weighted = snr * jnp.exp(jnp.log(inner) * (-1.0 / 6.0))
            newsnr = jnp.where(reduced > 1.0, weighted, snr)
            snr_ref[:, columns] = snr.astype(jnp.bfloat16)
            chisq_ref[:, columns] = chisq.astype(jnp.bfloat16)
            return jnp.maximum(peak, jnp.max(newsnr, axis=0, keepdims=True))

        peak = lax.fori_loop(
            0, SIDE // wide, second_pass, jnp.zeros((1, wide), jnp.float32)
        )
        peak_ref[...] = jnp.max(peak, axis=1, keepdims=True)

    vmem = pl.BlockSpec(memory_space=pltpu.VMEM)
    return pl.pallas_call(
        body,
        out_shape=(
            jax.ShapeDtypeStruct((HALF, SIDE), jnp.bfloat16),
            jax.ShapeDtypeStruct((HALF, SIDE), jnp.bfloat16),
            jax.ShapeDtypeStruct((1, 1), jnp.float32),
        ),
        in_specs=[vmem] * (1 + n_blocks) + [pl.BlockSpec(memory_space=pltpu.SMEM)] + [vmem] * 3,
        out_specs=(vmem, vmem, vmem),
        scratch_shapes=[
            pltpu.VMEM((2, HALF, SIDE), jnp.bfloat16),
            pltpu.VMEM((SIDE, SIDE), jnp.bfloat16),
            pltpu.VMEM((4, SIDE, HALF), jnp.bfloat16),
            pltpu.VMEM((4, 2 * SIDE, SIDE), jnp.bfloat16),
            pltpu.VMEM((4, 8, quarter), jnp.float32),
        ],
        compiler_params=pltpu.CompilerParams(vmem_limit_bytes=48 * MIB),
        name="inverse",
    )(spectrum, *blocks, edges, *in_vmem(third, fourth, phase))


def partner(mesh_shape, mask_of):
    groups, segments, cores = (mesh_shape[name] for name in AXES)
    pairs = []
    for group in range(groups):
        for segment in range(segments):
            for core in range(cores):
                here = (group * segments + segment) * cores + core
                other = segment ^ mask_of(core)
                pairs.append((here, (group * segments + other) * cores + core))
    return pairs


def gather_doubling(shard, mesh_shape):
    across = lax.ppermute(shard, AXES, partner(mesh_shape, lambda core: 4))
    pair = jnp.concatenate([shard, across])
    near = lax.ppermute(pair, AXES, partner(mesh_shape, lambda core: 2 - core))
    four = jnp.concatenate([pair, near])
    far = lax.ppermute(four, AXES, partner(mesh_shape, lambda core: 1 + core))
    return [shard, across, near, far]


def arrange_plain(strain_frames, frame_slot):
    count = lax.axis_size("segment")
    position = lax.axis_index("segment")
    frame_length = strain_frames.shape[1]
    counter = jnp.arange(count, dtype=jnp.int32)
    slot_now = lax.dynamic_slice_in_dim(frame_slot, position, 1, 1)[:, 0]
    next_index = jnp.minimum(position + 1, count - 1)
    slot_next = lax.dynamic_slice_in_dim(frame_slot, next_index, 1, 1)[:, 0]

    def arrange(slots, frames):
        selector = (counter[:, None] == slots[None, :]).astype(jnp.bfloat16)
        placed = jnp.dot(selector, frames, preferred_element_type=jnp.float32)
        return placed.astype(jnp.bfloat16).reshape(HALF, SIDE)

    following_rows = jnp.concatenate(
        [strain_frames[1:], jnp.zeros((1, frame_length), jnp.bfloat16)], axis=0
    )
    outgoing = jnp.stack([strain_frames, following_rows], axis=1)
    received = lax.all_to_all(outgoing, "segment", split_axis=0, concat_axis=0, tiled=True)
    leading = arrange(slot_now, received[:, 0])
    trailing = arrange(slot_next, received[:, 1])
    return jnp.concatenate([leading, trailing])


def local(mesh_shape, strain_frames, frame_slot, templates, bin_edges):
    first, second, third, fourth, phase = tables()
    count = mesh_shape["segment"]
    rows = strain_frames.shape[1] // SIDE
    staged = count == 8 and mesh_shape["template"] == 2 and rows % 16 == 0
    if staged:
        shard = templates.reshape(1, 2, -1, SIDE)
        blocks = gather_doubling(shard, mesh_shape)
        outgoing = split_frames(strain_frames)
        own = lax.all_to_all(outgoing, "segment", split_axis=0, concat_axis=0, tiled=True)
        other = lax.ppermute(own, "template", [(0, 1), (1, 0)])
        spectrum = forward_received(own, other, frame_slot, first, second, phase)
    else:
        signal = arrange_plain(strain_frames, frame_slot)
        whole = lax.all_gather(templates, "segment", axis=2, tiled=True)
        blocks = [whole.reshape(1, 2, HALF, SIDE)]
        spectrum = forward_arranged(signal, first, second, phase)
    snr, chisq, peak = inverse(spectrum, blocks, bin_edges, third, fourth, phase, staged)
    return snr.reshape(1, 1, LENGTH // 2), chisq.reshape(1, 1, LENGTH // 2), peak


def solution(mesh):
    mesh_shape = dict(mesh.shape)

    def step(strain_frames, frame_slot, templates, bin_edges):
        return local(mesh_shape, strain_frames, frame_slot, templates, bin_edges)

    in_specs = (
        P("segment", None),
        P(),
        P(("groups", "template"), None, "segment"),
        P(("groups", "template"), None),
    )
    out_specs = (
        P("segment", ("groups", "template"), None),
        P("segment", ("groups", "template"), None),
        P("segment", ("groups", "template")),
    )
    return jax.shard_map(step, mesh=mesh, in_specs=in_specs, out_specs=out_specs, check_vma=False)
```

time: 122 us -> 48 us (0.39)
  other arithmetic: 44.6 us -> 0.04 us
  blocking collectives: 35.5 us -> 0 us
  Pallas kernels: 0 us -> 13.3 us
  waiting for transfers between devices: 0.01 us -> 12.7 us
  local copies, waits for them, and re-layouts: 19.4 us -> 8.93 us
  matrix products: 7.79 us -> 0 us
  between operations: 7.15 us -> 0.7 us
  starting transfers between devices: 7.25 us -> 11.9 us
    all_gather x1 -> x0, blocking collectives: 35.5 us -> none  [local(): whole_templates = lax.all_gather(templates, 'segment', axis=2, tiled=True)]
    unnamed x5 -> x0, other arithmetic: 23.3 us -> none
    pallas_call x0 -> x3, Pallas kernels: none -> 13.3 us  [the longest x1 9.52 us: inverse(): pl.pallas_call(body, out_shape=(jax.ShapeDtypeStruct((HALF, SIDE), jnp.bf...]
    ppermute x0 -> x4, waiting for transfers between devices: none -> 12.7 us  [the longest x1 7.89 us: gather_doubling(): across = lax.ppermute(shard, AXES, partner(mesh_shape, lambda core: 4))]
    another operation x26 -> x0, other arithmetic: 10.7 us -> none
    dot_general x17 -> x0, matrix products: 7.79 us -> none  [the longest x5 2.37 us: later_passes(): jnp.einsum('cjdp,dkpr->ckjr', dft_table(RADIX_B, orient), turned, preferr...]
    unnamed x22 -> x23, local copies, waits for them, and re-layouts: 0.93 us -> 7.09 us
    convert_element_type x4 -> x0, local copies, waits for them, and re-layouts: 4.97 us -> none  [the longest x2 3.2 us: filter_template(): chisq.astype(jnp.bfloat16)]
  transfers between devices with their start and end apart: 1 -> 5, of which waited for: 0 -> 2; matrix products, arithmetic and copies ran while one was open for 10% -> 2% of each run, Pallas kernels for 0% -> 5%
where the time goes in v1:
time: 48 us; the launch traced here: 47.6 us
  Pallas kernels  13.3 us (28%)
  waiting for transfers between devices  12.7 us (26%)
  starting transfers between devices  11.9 us (25%)
  local copies, waits for them, and re-layouts  8.93 us (19%)
  between operations  0.7 us (1%)
    pallas_call x1, Pallas kernels, inverse(): pl.pallas_call(body, out_shape=(jax.ShapeDtypeStruct((HALF, SIDE), jnp.bf...  9.52 us
    ppermute x1, waiting for transfers between devices, gather_doubling(): across = lax.ppermute(shard, AXES, partner(mesh_shape, lambda core: 4))  7.89 us
    all_to_all x1, starting transfers between devices, local(): lax.all_to_all(outgoing, 'segment', split_axis=0, concat_axis=0, tiled=True)  7.25 us
    unnamed x23, local copies, waits for them, and re-layouts  7.09 us
    ppermute x1, waiting for transfers between devices, gather_doubling(): near = lax.ppermute(pair, AXES, partner(mesh_shape, lambda core: 2 - core))  4.83 us
    ppermute x1, starting transfers between devices, gather_doubling(): across = lax.ppermute(shard, AXES, partner(mesh_shape, lambda core: 4))  2.99 us
    pallas_call x1, Pallas kernels, forward_received(): pl.pallas_call(body, out_shape=pltpu.VMEM((SIDE, SIDE), jnp.float32), in_...  2.51 us
    ppermute x1, starting transfers between devices, gather_doubling(): far = lax.ppermute(four, AXES, partner(mesh_shape, lambda core: 1 + core))  1.48 us
  transfers between devices with their start and end apart: 5, of which 2 were waited for; matrix products, arithmetic and copies ran while one was open for 2% of the time, Pallas kernels for 5%

profile of v1, /device:TPU:0, one launch (start us, length us, event | category | flops | bytes accessed | tf_op | source)
XLA Modules:
  0.0 47.6 jit_solution(9069177579560445524)
XLA Ops:
  0.6 0.0 copy-start.4
  0.6 0.0 copy-start.7
  0.7 1.0 %copy-done.7 = bf16[8,16384]{1,0:T(8,128)(2,1)S(1)} copy-done((bf16[8,16384]{1,0:T(8,128)(2,1)S(1)}, bf16[8,16384]{1,0:T(8,128)(2,1)}, u32[]{:S(2)}) %copy-start.7) | copy-done | bytes 262168
  1.7 1.2 %split_frames.1 = bf16[8,32,512]{2,1,0:T(8,128)(2,1)} custom-call(bf16[8,16384]{1,0:T(8,128)(2,1)S(1)} %copy-done.7), custom_call_target="tpu_custom_call" | custom-call | tf_op jit(solution)/shard_map/split_frames/pallas_call | solution.py:73
  2.9 7.3 %all-to-all-start = ((bf16[8,32,512]{2,1,0:T(8,128)(2,1)}), bf16[8,32,512]{2,1,0:T(8,128)(2,1)S(1)}, u32[]{:S(2)}, u32[]{:S(2)}) async-start(bf16[8,32,512]{2,1,0:T(8,128)(2,1)} %split_frames.1), calls=%async_computation | async-start | bytes 524288 | tf_op jit(solution)/shard_map/all_to_all | solution.py:374
  10.2 0.8 %copy.14 = bf16[1,2,32,512]{3,2,1,0:T(8,128)(2,1)S(1)} copy(bf16[1,2,32,512]{3,1,2,0:T(2,128)(2,1)} %bitcast.6) | data formatting | bytes 131072
  11.0 3.0 %collective-permute-start.1 = (bf16[1,2,32,512]{3,2,1,0:T(8,128)(2,1)S(1)}, bf16[1,2,32,512]{3,2,1,0:T(8,128)(2,1)S(1)}, u32[]{:S(2)}, u32[]{:S(2)}) collective-permute-start(bf16[1,2,32,512]{3,2,1,0:T(8,128)(2,1)S(1)} %copy.14), channel_id=1, source_target_pairs={{0,8},{1,9},{2,10},{3,11},{4,12},{5,13},{6,14},{7,15},{8,0},{9,1},... | collective-permute-start | bytes 196616 | tf_op jit(solution)/shard_map/ppermute | solution.py:333
  14.0 7.9 %collective-permute-done.1.refs_2_ = bf16[1,2,32,512]{3,2,1,0:T(8,128)(2,1)S(1)} collective-permute-done((bf16[1,2,32,512]{3,2,1,0:T(8,128)(2,1)S(1)}, bf16[1,2,32,512]{3,2,1,0:T(8,128)(2,1)S(1)}, u32[]{:S(2)}, u32[]{:S(2)}) %collective-permute-start.1) | collective-permute-done | bytes 65568 | tf_op jit(solution)/shard_map/ppermute | solution.py:333
  21.9 0.1 collective-permute-start.2
  22.0 0.0 all-to-all-done.own_ref
  22.0 0.1 collective-permute-start
  22.1 4.8 %collective-permute-done.2.refs_3_ = bf16[2,2,32,512]{3,2,1,0:T(8,128)(2,1)S(1)} collective-permute-done((bf16[2,2,32,512]{3,2,1,0:T(8,128)(2,1)S(1)}, bf16[2,2,32,512]{3,2,1,0:T(8,128)(2,1)S(1)}, u32[]{:S(2)}, u32[]{:S(2)}) %collective-permute-start.2) | collective-permute-done | bytes 131104 | tf_op jit(solution)/shard_map/ppermute | solution.py:335
  27.0 1.5 %collective-permute-start.3 = (bf16[4,2,32,512]{3,2,1,0:T(8,128)(2,1)S(1)}, bf16[4,2,32,512]{3,2,1,0:T(8,128)(2,1)S(1)}, u32[]{:S(2)}, u32[]{:S(2)}) collective-permute-start(bf16[4,2,32,512]{3,2,1,0:T(8,128)(2,1)S(1)} %pad_maximum_fusion), channel_id=1, source_target_pairs={{0,2},{1,5},{2,0},{3,7},{4,6},{5,1},{6,4},{7,3},{8,10},{9,13},{10,... | collective-permute-start | bytes 786440 | tf_op jit(solution)/shard_map/ppermute | solution.py:337
  28.5 0.0 collective-permute-done.other_ref
  28.5 1.6 %copy-done = f32[2,512,512]{2,1,0:T(8,128)S(1)} copy-done((f32[2,512,512]{2,1,0:T(8,128)S(1)}, f32[2,512,512]{2,1,0:T(8,128)}, u32[]{:S(2)}) %copy-start) | copy-done | bytes 2097176
  30.1 1.2 %copy-done.5 = bf16[1024,512]{1,0:T(8,128)(2,1)S(1)} copy-done((bf16[1024,512]{1,0:T(8,128)(2,1)S(1)}, bf16[1024,512]{1,0:T(8,128)(2,1)}, u32[]{:S(2)}) %copy-start.5) | copy-done | bytes 1048600
  31.3 0.7 %copy-done.8 = s32[8,8]{1,0:T(8,128)S(1)} copy-done((s32[8,8]{1,0:T(8,128)S(1)}, s32[8,8]{1,0:T(8,128)}, u32[]{:S(2)}) %copy-start.8) | copy-done | bytes 280
  32.0 2.5 %forward.1.refs_0_ = f32[512,512]{1,0:T(8,128)S(1)} custom-call(bf16[8,32,512]{2,1,0:T(8,128)(2,1)S(1)} %all-to-all-done.own_ref, bf16[8,32,512]{2,1,0:T(8,128)(2,1)S(1)} %collective-permute-done.other_ref, s32[8,8]{1,0:T(8,128)S(1)} %copy-done.8, bf16[1024,512]{1,0:T(8,128)(2,1)S(1)} %copy-done.5, bf16[1024,512]{1,0:T(8,128)(2,1)S(1)} %copy-done.4, ...), custom_call_target="tpu_custom_call" | custom-call | flops 1073741824 | bytes 6291456 | tf_op jit(solution)/shard_map/forward/pallas_call | solution.py:117
  34.5 1.0 %copy-done.2 = f32[512,512]{1,0:T(8,128)} copy-done((f32[512,512]{1,0:T(8,128)}, f32[512,512]{1,0:T(8,128)S(1)}, u32[]{:S(2)}) %copy-start.2) | copy-done | bytes 1048600
  35.5 0.0 collective-permute-done.3.refs_4_
  35.5 0.7 %copy-done.10 = bf16[4,2,32,512]{3,2,1,0:T(8,128)(2,1)} copy-done((bf16[4,2,32,512]{3,2,1,0:T(8,128)(2,1)}, bf16[4,2,32,512]{3,2,1,0:T(8,128)(2,1)S(1)}, u32[]{:S(2)}) %copy-start.10) | copy-done | bytes 262168
  36.2 9.5 %inverse.1 = (bf16[256,512]{1,0:T(8,128)(2,1)S(1)}, bf16[256,512]{1,0:T(8,128)(2,1)S(1)}, f32[1,1]{1,0:T(1,128)}) custom-call(f32[512,512]{1,0:T(8,128)} %copy-done.2, bf16[1,2,32,512]{3,2,1,0:T(8,128)(2,1)S(1)} %copy.14, bf16[1,2,32,512]{3,2,1,0:T(8,128)(2,1)S(1)} %collective-permute-done.1.refs_2_, ...), custom_call_target="tpu_custom_call" | custom-call | tf_op jit(solution)/shard_map/inverse/pallas_call | solution.py:299
  45.7 0.9 %reshape.16 = bf16[1,1,131072]{2,1,0:T(2,128)(2,1)} reshape(bf16[256,512]{1,0:T(8,128)(2,1)S(1)} %get-tuple-element.6) | data formatting | bytes 524288 | tf_op jit(solution)/shard_map/reshape | solution.py:383
  46.6 0.9 %reshape.17 = bf16[1,1,131072]{2,1,0:T(2,128)(2,1)} reshape(bf16[256,512]{1,0:T(8,128)(2,1)S(1)} %get-tuple-element.7) | data formatting | bytes 524288 | tf_op jit(solution)/shard_map/reshape | solution.py:383
  (16 shorter events, 0.1 us)
Async XLA Ops:
  0.6 27.8 %copy-start.4 = (bf16[1024,512]{1,0:T(8,128)(2,1)S(1)}, bf16[1024,512]{1,0:T(8,128)(2,1)}, u32[]{:S(2)}) copy-start(bf16[1024,512]{1,0:T(8,128)(2,1)} %constant.11.clone.second_ref) | copy-start | bytes 3145732
  0.6 1.0 %copy-start.7 = (bf16[8,16384]{1,0:T(8,128)(2,1)S(1)}, bf16[8,16384]{1,0:T(8,128)(2,1)}, u32[]{:S(2)}) copy-start(bf16[8,16384]{1,0:T(8,128)(2,1)} %frames_ref.1) | copy-start | bytes 786436
  2.9 19.1 %all-to-all-start = ((bf16[8,32,512]{2,1,0:T(8,128)(2,1)}), bf16[8,32,512]{2,1,0:T(8,128)(2,1)S(1)}, u32[]{:S(2)}, u32[]{:S(2)}) async-start(bf16[8,32,512]{2,1,0:T(8,128)(2,1)} %split_frames.1), calls=%async_computation | async-start | bytes 524288 | tf_op jit(solution)/shard_map/all_to_all | solution.py:374
  11.0 10.9 %collective-permute-start.1 = (bf16[1,2,32,512]{3,2,1,0:T(8,128)(2,1)S(1)}, bf16[1,2,32,512]{3,2,1,0:T(8,128)(2,1)S(1)}, u32[]{:S(2)}, u32[]{:S(2)}) collective-permute-start(bf16[1,2,32,512]{3,2,1,0:T(8,128)(2,1)S(1)} %copy.14), channel_id=1, source_target_pairs={{0,8},{1,9},{2,10},{3,11},{4,12},{5,13},{6,14},{7,15},{8,0},{9,1},... | collective-permute-start | bytes 196616 | tf_op jit(solution)/shard_map/ppermute | solution.py:333
  21.9 5.0 %collective-permute-start.2 = (bf16[2,2,32,512]{3,2,1,0:T(8,128)(2,1)S(1)}, bf16[2,2,32,512]{3,2,1,0:T(8,128)(2,1)S(1)}, u32[]{:S(2)}, u32[]{:S(2)}) collective-permute-start(bf16[2,2,32,512]{3,2,1,0:T(8,128)(2,1)S(1)} %pad_maximum_fusion.1), channel_id=1, source_target_pairs={{0,4},{1,3},{2,6},{3,1},{4,0},{5,7},{6,2},{7,5},{8,12},{9,11},{10,... | collective-permute-start | bytes 393224 | tf_op jit(solution)/shard_map/ppermute | solution.py:335
  22.0 6.5 %collective-permute-start = (bf16[8,32,512]{2,1,0:T(8,128)(2,1)S(1)}, bf16[8,32,512]{2,1,0:T(8,128)(2,1)S(1)}, u32[]{:S(2)}, u32[]{:S(2)}) collective-permute-start(bf16[8,32,512]{2,1,0:T(8,128)(2,1)S(1)} %all-to-all-done.own_ref), channel_id=1, source_target_pairs={{0,1},{1,0},{2,3},{3,2},{4,5},{5,4},{6,7},{7,6},{8,9},{9,8},{10,11... | collective-permute-start | bytes 786440 | tf_op jit(solution)/shard_map/ppermute | solution.py:375
  26.9 9.2 %copy-start.9 = (s32[1,3]{1,0:T(1,128)S(1)}, s32[1,3]{1,0:T(1,128)}, u32[]{:S(2)}) copy-start(s32[1,3]{1,0:T(1,128)} %refs_5_.1) | copy-start | bytes 40
  27.0 8.5 %collective-permute-start.3 = (bf16[4,2,32,512]{3,2,1,0:T(8,128)(2,1)S(1)}, bf16[4,2,32,512]{3,2,1,0:T(8,128)(2,1)S(1)}, u32[]{:S(2)}, u32[]{:S(2)}) collective-permute-start(bf16[4,2,32,512]{3,2,1,0:T(8,128)(2,1)S(1)} %pad_maximum_fusion), channel_id=1, source_target_pairs={{0,2},{1,5},{2,0},{3,7},{4,6},{5,1},{6,4},{7,3},{8,10},{9,13},{10,... | collective-permute-start | bytes 786440 | tf_op jit(solution)/shard_map/ppermute | solution.py:337
  28.5 1.6 %copy-start = (f32[2,512,512]{2,1,0:T(8,128)S(1)}, f32[2,512,512]{2,1,0:T(8,128)}, u32[]{:S(2)}) copy-start(f32[2,512,512]{2,1,0:T(8,128)} %constant.12.clone.phase_ref.refs_8_) | copy-start | bytes 6291460
  30.1 1.2 %copy-start.5 = (bf16[1024,512]{1,0:T(8,128)(2,1)S(1)}, bf16[1024,512]{1,0:T(8,128)(2,1)}, u32[]{:S(2)}) copy-start(bf16[1024,512]{1,0:T(8,128)(2,1)} %constant.10.clone.first_ref) | copy-start | bytes 3145732
  31.3 0.7 %copy-start.8 = (s32[8,8]{1,0:T(8,128)S(1)}, s32[8,8]{1,0:T(8,128)}, u32[]{:S(2)}) copy-start(s32[8,8]{1,0:T(8,128)} %slot_ref.1) | copy-start | bytes 772
  32.0 4.2 %copy-start.1 = (f32[2,512,512]{2,1,0:T(8,128)S(1)}, f32[2,512,512]{2,1,0:T(8,128)}, u32[]{:S(2)}) copy-start(f32[2,512,512]{2,1,0:T(8,128)} %constant.12.clone.phase_ref.refs_8_) | copy-start | bytes 6291460
  32.0 4.2 %copy-start.3 = (bf16[4,256,1024]{2,1,0:T(8,128)(2,1)S(1)}, bf16[4,256,1024]{2,1,0:T(8,128)(2,1)}, u32[]{:S(2)}) copy-start(bf16[4,256,1024]{2,1,0:T(8,128)(2,1)} %constant.13.clone.refs_6_) | copy-start | bytes 6291460
  32.0 4.2 %copy-start.6 = (bf16[512,1024]{1,0:T(8,128)(2,1)S(1)}, bf16[512,1024]{1,0:T(8,128)(2,1)}, u32[]{:S(2)}) copy-start(bf16[512,1024]{1,0:T(8,128)(2,1)} %constant.14.clone.refs_7_) | copy-start | bytes 3145732
  34.5 1.0 %copy-start.2 = (f32[512,512]{1,0:T(8,128)}, f32[512,512]{1,0:T(8,128)S(1)}, u32[]{:S(2)}) copy-start(f32[512,512]{1,0:T(8,128)S(1)} %forward.1.refs_0_) | copy-start | bytes 3145732
  35.5 0.7 %copy-start.10 = (bf16[4,2,32,512]{3,2,1,0:T(8,128)(2,1)}, bf16[4,2,32,512]{3,2,1,0:T(8,128)(2,1)S(1)}, u32[]{:S(2)}) copy-start(bf16[4,2,32,512]{3,2,1,0:T(8,128)(2,1)S(1)} %collective-permute-done.3.refs_4_) | copy-start | bytes 786436

commit v2 on v1

--- a/solution.py
+++ b/solution.py
@@ -1,3 +1,4 @@
+import functools
 import math
 
 import jax
@@ -15,6 +16,13 @@
 AXES = ("groups", "segment", "template")
 MIB = 1 << 20
 BIN_LOW = (0, 32, 96, 128)
+ROUNDS = 4
+
+
+def strain_mask(step, core):
+    if isinstance(core, int):
+        return (step + 1) % ROUNDS if core == 0 else step + ROUNDS
+    return jnp.where(core == 0, (step + 1) % ROUNDS, step + ROUNDS)
 
 
 def turn(rows, columns, modulus):
@@ -36,49 +44,121 @@
         third.append(
             np.block([[cosine[chosen], sine[chosen]], [-sine[chosen], cosine[chosen]]])
         )
-    kept = slice(HALF // 2, HALF // 2 + HALF)
-    fourth = np.block([[cosine[kept], -sine[kept]], [sine[kept], cosine[kept]]])
+    fourth = []
+    for parity in range(2):
+        kept = slice(HALF // 2 + parity, HALF // 2 + HALF, 2)
+        fourth.append(
+            np.block(
+                [[cosine[kept, low], -sine[kept, low]], [sine[kept, low], cosine[kept, low]]]
+            )
+        )
     phase_cos, phase_sin = turn(digit, digit, LENGTH)
     phase = np.stack([phase_cos, phase_sin]).astype(np.float32)
 
 
-    narrow = [x.astype(np.float32).astype(ml_dtypes.bfloat16) for x in (first, second, np.stack(third), fourth)]
+    narrow = [x.astype(np.float32).astype(ml_dtypes.bfloat16) for x in (first, second, np.stack(third), np.stack(fourth))]
     return (*narrow, phase)
 
 
-def in_vmem(*arrays):
-    return [pltpu.with_memory_space_constraint(x, pltpu.VMEM) for x in arrays]
-
-
-def split_frames(frames):
+def spread(source, wide, count, rows):
+    tiles = SIDE // 128
+    for row in range(rows):
+        for tile in range(tiles):
+            place = (row * tiles + tile) * 128
+            wide[tile, pl.ds(row, count, stride=rows), :] = source[:, place : place + 128].astype(
+                jnp.float32
+            )
+
+
+def split_frames(frames, shard):
     count, samples = frames.shape
     rows = samples // SIDE
     tiles = SIDE // 128
 
-    def body(frames_ref, out_ref, wide):
+    def body(frames_ref, shard_ref, *refs):
+        outs, unpacked, wide, narrow = refs[: ROUNDS + 1], *refs[ROUNDS + 1 :]
+        segment = lax.axis_index("segment")
         core = lax.axis_index("template")
         wide[:, count * rows :, :] = jnp.zeros((tiles, rows, 128), jnp.float32)
-        for row in range(rows):
+        spread(frames_ref, wide, count, rows)
+        for step, out_ref in enumerate(outs):
+            mask = strain_mask(step, core) if step < ROUNDS else 0
+            start = pl.multiple_of((segment ^ mask) * rows, rows)
             for tile in range(tiles):
-                place = (row * tiles + tile) * 128
-                wide[tile, pl.ds(row, count, stride=rows), :] = frames_ref[
-                    :, place : place + 128
-                ].astype(jnp.float32)
-        for tile in range(tiles):
-            moved = wide[tile, pl.ds(pl.multiple_of(core * rows, rows), count * rows), :]
-            out_ref[:, :, tile * 128 : tile * 128 + 128] = moved.astype(jnp.bfloat16).reshape(
-                count, rows, 128
-            )
-
+                out_ref[:, :, tile * 128 : tile * 128 + 128] = (
+                    wide[tile, pl.ds(start, 2 * rows), :].astype(jnp.bfloat16).reshape(2, rows, 128)
+                )
+        unpack(shard_ref, narrow, unpacked.at[0])
+
+    vmem = pl.BlockSpec(memory_space=pltpu.VMEM)
     return pl.pallas_call(
         body,
-        out_shape=pltpu.VMEM((count, rows, SIDE), jnp.bfloat16),
-        in_specs=[pl.BlockSpec(memory_space=pltpu.VMEM)],
-        out_specs=pl.BlockSpec(memory_space=pltpu.VMEM),
-        scratch_shapes=[pltpu.VMEM((tiles, (count + 1) * rows, 128), jnp.float32)],
-        compiler_params=pltpu.CompilerParams(vmem_limit_bytes=16 * MIB),
+        out_shape=[pltpu.VMEM((2, rows, SIDE), jnp.bfloat16)] * (ROUNDS + 1)
+        + [pltpu.VMEM((1, 2, rows, SIDE), jnp.bfloat16)],
+        in_specs=[vmem, vmem],
+        out_specs=[vmem] * (ROUNDS + 2),
+        scratch_shapes=[
+            pltpu.VMEM((tiles, (count + 1) * rows, 128), jnp.float32),
+            pltpu.VMEM((tiles, 2 * rows, 128), jnp.float32),
+        ],
+        compiler_params=pltpu.CompilerParams(vmem_limit_bytes=4 * MIB),
         name="split_frames",
-    )(frames)
+    )(frames, shard)
+
+
+def unpack(shard_ref, narrow, out_ref):
+    rows = out_ref.shape[1]
+    spread(shard_ref.at[0], narrow, 2, rows)
+    for tile in range(SIDE // 128):
+        out_ref[:, :, tile * 128 : tile * 128 + 128] = (
+            narrow[tile].astype(jnp.bfloat16).reshape(2, rows, 128)
+        )
+
+
+def pair_shards(unpacked, across):
+    rows = unpacked.shape[2]
+
+    def body(unpacked_ref, across_ref, out_ref, narrow):
+        out_ref[0] = unpacked_ref[0]
+        unpack(across_ref, narrow, out_ref.at[1])
+
+    vmem = pl.BlockSpec(memory_space=pltpu.VMEM)
+    return pl.pallas_call(
+        body,
+        out_shape=pltpu.VMEM((2, 2, rows, SIDE), jnp.bfloat16),
+        in_specs=[vmem, vmem],
+        out_specs=vmem,
+        scratch_shapes=[pltpu.VMEM((SIDE // 128, 2 * rows, 128), jnp.float32)],
+        compiler_params=pltpu.CompilerParams(vmem_limit_bytes=4 * MIB),
+        name="pair_shards",
+    )(unpacked, across)
+
+
+def load_tables(arrays, after):
+    count = len(arrays)
+
+    def body(*refs):
+        sources, outs, arrived = refs[:count], refs[count + 1 : 2 * count + 1], refs[-1]
+        copies = [
+            pltpu.make_async_copy(source, out, arrived.at[place])
+            for place, (source, out) in enumerate(zip(sources, outs, strict=True))
+        ]
+        for copy in copies:
+            copy.start()
+        for copy in copies:
+            copy.wait()
+
+    hbm = pl.BlockSpec(memory_space=pl.ANY)
+    return pl.pallas_call(
+        body,
+        out_shape=[pltpu.VMEM(x.shape, x.dtype) for x in arrays],
+        in_specs=[hbm] * (count + 1),
+        out_specs=[pl.BlockSpec(memory_space=pltpu.VMEM)] * count,
+        scratch_shapes=[pltpu.SemaphoreType.DMA((count,))],
+        compiler_params=pltpu.CompilerParams(vmem_limit_bytes=1 * MIB),
+        cost_estimate=pl.CostEstimate(flops=0, bytes_accessed=12 * MIB, transcendentals=0),
+        name="load_tables",
+    )(*(pltpu.with_memory_space_constraint(x, pltpu.HBM) for x in arrays), after)
 
 
 def forward_body(signal, first, second, phase, spectrum, turned):
@@ -100,35 +180,43 @@
     lax.fori_loop(0, SIDE // rows, chunk, 0)
 
 
-def forward_received(own, other, frame_slot, first, second, phase):
-    count, rows, _ = own.shape
-
-    def body(own_ref, other_ref, slot_ref, first_ref, second_ref, phase_ref, spectrum, signal, turned):
+def forward_received(received, other, mine, frame_slot, first, second, phase):
+    rows = mine.shape[1]
+
+    def body(*refs):
+        received_refs, other_ref, mine_ref, slot_ref = refs[:ROUNDS], *refs[ROUNDS : ROUNDS + 3]
+        first_ref, second_ref, phase_ref, spectrum, signal, turned = refs[ROUNDS + 3 :]
         segment = lax.axis_index("segment")
         core = lax.axis_index("template")
-        for part, frames in ((core, own_ref), (1 - core, other_ref)):
-            half = jnp.minimum(segment + part, count - 1)
-            for source in range(count):
+        following = jnp.minimum(segment + 1, slot_ref.shape[1] - 1)
+
+        def place(source, frames):
+            for part, half in enumerate((segment, following)):
                 start = part * HALF + slot_ref[source, half] * rows
-                signal[pl.ds(pl.multiple_of(start, rows), rows), :] = frames[source]
+                signal[pl.ds(pl.multiple_of(start, rows), rows), :] = frames[part]
+
+        for step in range(ROUNDS):
+            place(segment ^ strain_mask(step, core), received_refs[step])
+            place(segment ^ strain_mask(step, 1 - core), other_ref.at[step])
+        place(segment, mine_ref)
         forward_body(signal, first_ref, second_ref, phase_ref, spectrum, turned)
 
     vmem = pl.BlockSpec(memory_space=pltpu.VMEM)
     return pl.pallas_call(
         body,
         out_shape=pltpu.VMEM((SIDE, SIDE), jnp.float32),
-        in_specs=[vmem, vmem, pl.BlockSpec(memory_space=pltpu.SMEM), vmem, vmem, vmem],
+        in_specs=[vmem] * (ROUNDS + 2) + [pl.BlockSpec(memory_space=pltpu.SMEM)] + [vmem] * 3,
         out_specs=vmem,
         scratch_shapes=[
             pltpu.VMEM((SIDE, SIDE), jnp.bfloat16),
             pltpu.VMEM((SIDE, 2 * SIDE), jnp.bfloat16),
         ],
-        compiler_params=pltpu.CompilerParams(vmem_limit_bytes=32 * MIB),
+        compiler_params=pltpu.CompilerParams(vmem_limit_bytes=12 * MIB),
         cost_estimate=pl.CostEstimate(
             flops=4 * SIDE**3 * 2, bytes_accessed=6 * MIB, transcendentals=0
         ),
         name="forward",
-    )(own, other, frame_slot, *in_vmem(first, second, phase))
+    )(*received, other, mine, frame_slot, first, second, phase)
 
 
 def forward_arranged(signal, first, second, phase):
@@ -142,16 +230,16 @@
         in_specs=[vmem] * 4,
         out_specs=vmem,
         scratch_shapes=[pltpu.VMEM((SIDE, 2 * SIDE), jnp.bfloat16)],
-        compiler_params=pltpu.CompilerParams(vmem_limit_bytes=32 * MIB),
+        compiler_params=pltpu.CompilerParams(vmem_limit_bytes=12 * MIB),
         name="forward",
-    )(signal, *in_vmem(first, second, phase))
+    )(signal, first, second, phase)
 
 
 def owners_of(segment, core, doubled):
     if not doubled:
         return [[0]]
     near, far = 2 - core, 1 + core
-    masks = [[0], [4], [near, near ^ 4], [far, far ^ 4, far ^ near, far ^ near ^ 4]]
+    masks = [[0, 4], [near, near ^ 4], [far, far ^ 4, far ^ near, far ^ near ^ 4]]
     return [[segment ^ mask for mask in block] for block in masks]
 
 
@@ -159,14 +247,13 @@
     n_blocks = len(blocks)
     shard = blocks[0].shape[2]
     quarter = HALF // 2
-    rows = SIDE // 2
     wide = SIDE // 2
 
     def body(*refs):
         spectrum_ref, block_refs = refs[0], refs[1 : 1 + n_blocks]
         edge_ref, third_ref, fourth_ref, phase_ref = refs[1 + n_blocks : 5 + n_blocks]
         snr_ref, chisq_ref, peak_ref = refs[5 + n_blocks : 8 + n_blocks]
-        gathered, flipped, masked, turned, sums = refs[8 + n_blocks :]
+        gathered, flipped, masked, turned, sums, series = refs[8 + n_blocks :]
         segment = lax.axis_index("segment")
         core = lax.axis_index("template")
         for block, owners in zip(block_refs, owners_of(segment, core, doubled), strict=True):
@@ -242,20 +329,27 @@
 
         lax.fori_loop(0, SIDE // step, correlate, 0)
 
-        def first_pass(index, carry):
-            number, part = index // (SIDE // rows), index % (SIDE // rows)
-            here = pl.ds(pl.multiple_of(part * rows, rows), rows)
-            there = pl.ds(pl.multiple_of(SIDE + part * rows, rows), rows)
-            product = jnp.dot(
-                masked[number, here, :], third_ref[number], preferred_element_type=jnp.float32
-            )
-            real, imag = product[:, :SIDE], product[:, SIDE:]
-            cosine, sine = phase_ref[0, here, :], phase_ref[1, here, :]
-            turned[number, here, :] = (real * cosine - imag * sine).astype(jnp.bfloat16)
-            turned[number, there, :] = (real * sine + imag * cosine).astype(jnp.bfloat16)
+        def first_pass(number, carry):
+            for tile in range(SIDE // wide):
+                here = slice(tile * wide, (tile + 1) * wide)
+                there = slice(SIDE + tile * wide, SIDE + (tile + 1) * wide)
+                real = jnp.dot(
+                    masked[number], third_ref[number, :, here], preferred_element_type=jnp.float32
+                )
+                imag = jnp.dot(
+                    masked[number], third_ref[number, :, there], preferred_element_type=jnp.float32
+                )
+                cosine, sine = phase_ref[0, :, here], phase_ref[1, :, here]
+                new_real = real * cosine - imag * sine
+                new_imag = real * sine + imag * cosine
+                for part, value in enumerate((new_real, new_imag)):
+                    rows = slice(part * HALF, (part + 1) * HALF)
+                    upper, lower = value[:HALF], value[HALF:]
+                    turned[number, 0, rows, here] = (upper + lower).astype(jnp.bfloat16)
+                    turned[number, 1, rows, here] = (upper - lower).astype(jnp.bfloat16)
             return carry
 
-        lax.fori_loop(0, 4 * (SIDE // rows), first_pass, 0)
+        lax.fori_loop(0, 4, first_pass, 0, unroll=True)
 
         bin_power = [jnp.sum(sums[number]) for number in range(4)]
         total = (bin_power[0] + bin_power[1]) + (bin_power[2] + bin_power[3])
@@ -263,44 +357,59 @@
         shares = [jnp.full((1, wide), bin_power[number], jnp.float32) / total_row for number in range(4)]
         scale = (1.0 / LENGTH) / total_row
 
-        def second_pass(index, peak):
-            columns = pl.ds(pl.multiple_of(index * wide, wide), wide)
-            pieces = [
+        def second_pass(index, parity):
+            columns = slice(index * wide, (index + 1) * wide)
+            return [
                 jnp.dot(
-                    fourth_ref[...], turned[number, :, columns], preferred_element_type=jnp.float32
+                    fourth_ref[parity],
+                    turned[number, parity, :, columns],
+                    preferred_element_type=jnp.float32,
                 )
                 for number in range(4)
             ]
-            real = [piece[:HALF] for piece in pieces]
-            imag = [piece[HALF:] for piece in pieces]
+
+        def finish(index, parity, pieces):
+            real = [piece[:quarter] for piece in pieces]
+            imag = [piece[quarter:] for piece in pieces]
             sum_real = (real[0] + real[1]) + (real[2] + real[3])
             sum_imag = (imag[0] + imag[1]) + (imag[2] + imag[3])
             snr = jnp.sqrt((sum_real * sum_real + sum_imag * sum_imag) * scale)
-            chisq = jnp.zeros_like(snr)
+            chisq = None
             for number in range(4):
                 diff_real = real[number] - shares[number] * sum_real
                 diff_imag = imag[number] - shares[number] * sum_imag
-                chisq = chisq + (diff_real * diff_real + diff_imag * diff_imag)
+                term = diff_real * diff_real + diff_imag * diff_imag
+                chisq = term if chisq is None else chisq + term
             chisq = chisq * scale
-            reduced = chisq / 6.0
-            inner = (1.0 + reduced * reduced * reduced) / 2.0
-            weighted = snr * jnp.exp(jnp.log(inner) * (-1.0 / 6.0))
+            reduced = chisq * (1.0 / 6.0)
+            inner = 0.5 + 0.5 * (reduced * reduced * reduced)
+            weighted = snr * jnp.exp2(jnp.log2(inner) * (-1.0 / 6.0))
             newsnr = jnp.where(reduced > 1.0, weighted, snr)
-            snr_ref[:, columns] = snr.astype(jnp.bfloat16)
-            chisq_ref[:, columns] = chisq.astype(jnp.bfloat16)
-            return jnp.maximum(peak, jnp.max(newsnr, axis=0, keepdims=True))
-
-        peak = lax.fori_loop(
-            0, SIDE // wide, second_pass, jnp.zeros((1, wide), jnp.float32)
-        )
+            for tile in range(wide // 128):
+                lanes = slice(tile * 128, (tile + 1) * 128)
+                start = parity * (SIDE // 128) + index * (wide // 128) + tile
+                rows = pl.ds(start, quarter, stride=2 * SIDE // 128)
+                series[0, rows, :] = snr[:, lanes]
+                series[1, rows, :] = chisq[:, lanes]
+            return jnp.max(newsnr, axis=0, keepdims=True)
+
+        peak = jnp.zeros((1, wide), jnp.float32)
+        steps = [(index, parity) for index in range(SIDE // wide) for parity in range(2)]
+        pieces = second_pass(*steps[0])
+        for place, step in enumerate(steps):
+            ahead = second_pass(*steps[place + 1]) if place + 1 < len(steps) else None
+            peak = jnp.maximum(peak, finish(*step, pieces))
+            pieces = ahead
+        for kind, out_ref in enumerate((snr_ref, chisq_ref)):
+            out_ref[0] = series[kind].reshape(1, LENGTH // 2).astype(jnp.bfloat16)
         peak_ref[...] = jnp.max(peak, axis=1, keepdims=True)
 
     vmem = pl.BlockSpec(memory_space=pltpu.VMEM)
     return pl.pallas_call(
         body,
         out_shape=(
-            jax.ShapeDtypeStruct((HALF, SIDE), jnp.bfloat16),
-            jax.ShapeDtypeStruct((HALF, SIDE), jnp.bfloat16),
+            jax.ShapeDtypeStruct((1, 1, LENGTH // 2), jnp.bfloat16),
+            jax.ShapeDtypeStruct((1, 1, LENGTH // 2), jnp.bfloat16),
             jax.ShapeDtypeStruct((1, 1), jnp.float32),
         ),
         in_specs=[vmem] * (1 + n_blocks) + [pl.BlockSpec(memory_space=pltpu.SMEM)] + [vmem] * 3,
@@ -309,33 +418,26 @@
             pltpu.VMEM((2, HALF, SIDE), jnp.bfloat16),
             pltpu.VMEM((SIDE, SIDE), jnp.bfloat16),
             pltpu.VMEM((4, SIDE, HALF), jnp.bfloat16),
-            pltpu.VMEM((4, 2 * SIDE, SIDE), jnp.bfloat16),
+            pltpu.VMEM((4, 2, SIDE, SIDE), jnp.bfloat16),
             pltpu.VMEM((4, 8, quarter), jnp.float32),
+            pltpu.VMEM((2, LENGTH // 256, 128), jnp.float32),
         ],
-        compiler_params=pltpu.CompilerParams(vmem_limit_bytes=48 * MIB),
+        compiler_params=pltpu.CompilerParams(vmem_limit_bytes=20 * MIB),
         name="inverse",
-    )(spectrum, *blocks, edges, *in_vmem(third, fourth, phase))
-
-
-def partner(mesh_shape, mask_of):
+    )(spectrum, *blocks, edges, third, fourth, phase)
+
+
+def exchange(value, mesh_shape, mask_of):
     groups, segments, cores = (mesh_shape[name] for name in AXES)
     pairs = []
     for group in range(groups):
         for segment in range(segments):
             for core in range(cores):
-                here = (group * segments + segment) * cores + core
-                other = segment ^ mask_of(core)
-                pairs.append((here, (group * segments + other) * cores + core))
-    return pairs
-
-
-def gather_doubling(shard, mesh_shape):
-    across = lax.ppermute(shard, AXES, partner(mesh_shape, lambda core: 4))
-    pair = jnp.concatenate([shard, across])
-    near = lax.ppermute(pair, AXES, partner(mesh_shape, lambda core: 2 - core))
-    four = jnp.concatenate([pair, near])
-    far = lax.ppermute(four, AXES, partner(mesh_shape, lambda core: 1 + core))
-    return [shard, across, near, far]
+                if mask_of(core):
+                    here = (group * segments + segment) * cores + core
+                    other = segment ^ mask_of(core)
+                    pairs.append((here, (group * segments + other) * cores + core))
+    return lax.ppermute(value, AXES, pairs)
 
 
 def arrange_plain(strain_frames, frame_slot):
@@ -363,24 +465,32 @@
 
 
 def local(mesh_shape, strain_frames, frame_slot, templates, bin_edges):
-    first, second, third, fourth, phase = tables()
+    constants = tables()
     count = mesh_shape["segment"]
     rows = strain_frames.shape[1] // SIDE
     staged = count == 8 and mesh_shape["template"] == 2 and rows % 16 == 0
     if staged:
-        shard = templates.reshape(1, 2, -1, SIDE)
-        blocks = gather_doubling(shard, mesh_shape)
-        outgoing = split_frames(strain_frames)
-        own = lax.all_to_all(outgoing, "segment", split_axis=0, concat_axis=0, tiled=True)
-        other = lax.ppermute(own, "template", [(0, 1), (1, 0)])
-        spectrum = forward_received(own, other, frame_slot, first, second, phase)
+        across = exchange(templates, mesh_shape, lambda core: 4)
+        *outgoing, mine, unpacked = split_frames(strain_frames, templates)
+        pair = pair_shards(unpacked, across)
+        *late, pair = lax.optimization_barrier((*outgoing[2:], pair))
+        received = [
+            exchange(value, mesh_shape, functools.partial(strain_mask, step))
+            for step, value in enumerate([*outgoing[:2], *late])
+        ]
+        near = exchange(pair, mesh_shape, lambda core: 2 - core)
+        first, second, third, fourth, phase = load_tables(constants, pair)
+        other = lax.ppermute(jnp.stack(received), "template", [(0, 1), (1, 0)])
+        far = exchange(jnp.concatenate([pair, near]), mesh_shape, lambda core: 1 + core)
+        blocks = [pair, near, far]
+        spectrum = forward_received(received, other, mine, frame_slot, first, second, phase)
     else:
+        first, second, third, fourth, phase = constants
         signal = arrange_plain(strain_frames, frame_slot)
         whole = lax.all_gather(templates, "segment", axis=2, tiled=True)
         blocks = [whole.reshape(1, 2, HALF, SIDE)]
         spectrum = forward_arranged(signal, first, second, phase)
-    snr, chisq, peak = inverse(spectrum, blocks, bin_edges, third, fourth, phase, staged)
-    return snr.reshape(1, 1, LENGTH // 2), chisq.reshape(1, 1, LENGTH // 2), peak
+    return inverse(spectrum, blocks, bin_edges, third, fourth, phase, staged)
 
 
 def solution(mesh):

time: 48 us -> 34.9 us (0.73)
  waiting for transfers between devices: 12.7 us -> 2.93 us
  local copies, waits for them, and re-layouts: 8.93 us -> 1.8 us
  starting transfers between devices: 11.9 us -> 15.5 us
    ppermute x4 -> x8, starting transfers between devices: 4.65 us -> 15.5 us  [the longest x7 11.6 us: exchange(): return lax.ppermute(value, AXES, pairs)]
    ppermute x4 -> x8, waiting for transfers between devices: 12.7 us -> 2.93 us  [the longest x7 2.93 us: exchange(): return lax.ppermute(value, AXES, pairs)]
    all_to_all x1 -> x0, starting transfers between devices: 7.25 us -> none  [local(): lax.all_to_all(outgoing, 'segment', split_axis=0, concat_axis=0, tiled=True)]
    unnamed x23 -> x8, local copies, waits for them, and re-layouts: 7.09 us -> 1.8 us
    reshape x2 -> x0, local copies, waits for them, and re-layouts: 1.84 us -> none  [the longest x1 0.92 us: local(): snr.reshape(1, 1, LENGTH // 2)]
    pallas_call x2 -> x4, Pallas kernels: 10.8 us -> 11.2 us  [the longest x1 7.39 us: inverse(): pl.pallas_call(body, out_shape=(jax.ShapeDtypeStruct((1, 1, LENGTH // 2),...]
  transfers between devices with their start and end apart: 5 -> 8, of which waited for: 2 -> 2; matrix products, arithmetic and copies ran while one was open for 2% -> 0% of each run, Pallas kernels for 5% -> 18%
where the time goes in v2:
time: 34.9 us; the launch traced here: 34.7 us
  starting transfers between devices  15.5 us (44%)
  Pallas kernels  13.7 us (39%)
  waiting for transfers between devices  2.93 us (8%)
  local copies, waits for them, and re-layouts  1.8 us (5%)
  between operations  0.73 us (2%)
    ppermute x7, starting transfers between devices, exchange(): return lax.ppermute(value, AXES, pairs)  11.6 us
    pallas_call x1, Pallas kernels, inverse(): pl.pallas_call(body, out_shape=(jax.ShapeDtypeStruct((1, 1, LENGTH // 2),...  7.39 us
    ppermute x1, starting transfers between devices, local(): other = lax.ppermute(jnp.stack(received), 'template', [(0, 1), (1, 0)])  3.89 us
    pallas_call x1, Pallas kernels, load_tables(): pl.pallas_call(body, out_shape=[pltpu.VMEM(x.shape, x.dtype) for x in arr...  3.07 us
    ppermute x7, waiting for transfers between devices, exchange(): return lax.ppermute(value, AXES, pairs)  2.93 us
    pallas_call x1, Pallas kernels, forward_received(): pl.pallas_call(body, out_shape=pltpu.VMEM((SIDE, SIDE), jnp.float32), in_...  2.53 us
    unnamed x8, local copies, waits for them, and re-layouts  1.8 us
  transfers between devices with their start and end apart: 8, of which 2 were waited for; matrix products, arithmetic and copies ran while one was open for 0% of the time, Pallas kernels for 18%

profile of v2, /device:TPU:0, one launch (start us, length us, event | category | flops | bytes accessed | tf_op | source)
XLA Modules:
  0.0 34.7 jit_solution(13799525091480763260)
XLA Ops:
  0.6 4.1 %collective-permute-start.2 = (bf16[1,2,16384]{2,1,0:T(2,128)(2,1)}, bf16[1,2,16384]{2,1,0:T(2,128)(2,1)S(1)}, u32[]{:S(2)}, u32[]{:S(2)}) collective-permute-start(bf16[1,2,16384]{2,1,0:T(2,128)(2,1)} %shard_ref.1), channel_id=1, source_target_pairs={{0,8},{1,9},{2,10},{3,11},{4,12},{5,13},{6,14},{7,15},{8,0},{9,1},... | collective-permute-start | bytes 196616 | tf_op jit(solution)/shard_map/ppermute | solution.py:440
  4.7 0.9 %copy-done = bf16[8,16384]{1,0:T(8,128)(2,1)S(1)} copy-done((bf16[8,16384]{1,0:T(8,128)(2,1)S(1)}, bf16[8,16384]{1,0:T(8,128)(2,1)}, u32[]{:S(2)}) %copy-start) | copy-done | bytes 262168
  5.7 0.8 %copy-done.1 = bf16[1,2,16384]{2,1,0:T(2,128)(2,1)S(1)} copy-done((bf16[1,2,16384]{2,1,0:T(2,128)(2,1)S(1)}, bf16[1,2,16384]{2,1,0:T(2,128)(2,1)}, u32[]{:S(2)}) %copy-start.1) | copy-done | bytes 65560
  6.5 0.6 %split_frames.1 = (bf16[2,32,512]{2,1,0:T(8,128)(2,1)S(1)}, bf16[2,32,512]{2,1,0:T(8,128)(2,1)S(1)}, bf16[2,32,512]{2,1,0:T(8,128)(2,1)S(1)}, bf16[2,32,512]{2,1...) custom-call(bf16[8,16384]{1,0:T(8,128)(2,1)S(1)} %copy-done, ...), custom_call_target="tpu_custom_call" | custom-call | tf_op jit(solution)/shard_map/split_frames/pallas_call | solution.py:94
  7.2 1.6 %collective-permute-start = (bf16[2,32,512]{2,1,0:T(8,128)(2,1)S(1)}, bf16[2,32,512]{2,1,0:T(8,128)(2,1)S(1)}, u32[]{:S(2)}, u32[]{:S(2)}) collective-permute-start(bf16[2,32,512]{2,1,0:T(8,128)(2,1)S(1)} %get-tuple-element.17), channel_id=1, source_target_pairs={{0,2},{1,9},{2,0},{3,11},{4,6},{5,13},{6,4},{7,15},{8,10},{9,1},{1... | collective-permute-start | bytes 196616 | tf_op jit(solution)/shard_map/ppermute | solution.py:440
  8.7 1.6 %collective-permute-start.1 = (bf16[2,32,512]{2,1,0:T(8,128)(2,1)S(1)}, bf16[2,32,512]{2,1,0:T(8,128)(2,1)S(1)}, u32[]{:S(2)}, u32[]{:S(2)}) collective-permute-start(bf16[2,32,512]{2,1,0:T(8,128)(2,1)S(1)} %get-tuple-element.18), channel_id=1, source_target_pairs={{0,4},{1,11},{2,6},{3,9},{4,0},{5,15},{6,2},{7,13},{8,12},{9,3},{1... | collective-permute-start | bytes 196616 | tf_op jit(solution)/shard_map/ppermute | solution.py:440
  10.3 0.0 collective-permute-done.2.across_ref
  10.3 0.1 pair_shards.1.refs_5_.refs_1_
  10.4 0.9 %collective-permute-start.3 = (bf16[2,32,512]{2,1,0:T(8,128)(2,1)S(1)}, bf16[2,32,512]{2,1,0:T(8,128)(2,1)S(1)}, u32[]{:S(2)}, u32[]{:S(2)}) collective-permute-start(bf16[2,32,512]{2,1,0:T(8,128)(2,1)S(1)} %get-tuple-element.22), channel_id=1, source_target_pairs={{0,6},{1,13},{2,4},{3,15},{4,2},{5,9},{6,0},{7,11},{8,14},{9,5},{1... | collective-permute-start | bytes 196616 | tf_op jit(solution)/shard_map/ppermute | solution.py:440
  11.3 0.7 %collective-permute-start.4 = (bf16[2,32,512]{2,1,0:T(8,128)(2,1)S(1)}, bf16[2,32,512]{2,1,0:T(8,128)(2,1)S(1)}, u32[]{:S(2)}, u32[]{:S(2)}) collective-permute-start(bf16[2,32,512]{2,1,0:T(8,128)(2,1)S(1)} %get-tuple-element.23), channel_id=1, source_target_pairs={{1,15},{3,13},{5,11},{7,9},{9,7},{11,5},{13,3},{15,1},{17,31},{19,... | collective-permute-start | bytes 196616 | tf_op jit(solution)/shard_map/ppermute | solution.py:440
  12.0 1.2 %collective-permute-start.6 = (bf16[2,2,32,512]{3,2,1,0:T(8,128)(2,1)S(1)}, bf16[2,2,32,512]{3,2,1,0:T(8,128)(2,1)S(1)}, u32[]{:S(2)}, u32[]{:S(2)}) collective-permute-start(bf16[2,2,32,512]{3,2,1,0:T(8,128)(2,1)S(1)} %pair_shards.1.refs_5_.refs_1_), channel_id=1, source_target_pairs={{0,4},{1,3},{2,6},{3,1},{4,0},{5,7},{6,2},{7,5},{8,12},{9,11},{10,... | collective-permute-start | bytes 393224 | tf_op jit(solution)/shard_map/ppermute | solution.py:440
  13.2 0.0 collective-permute-done.refs_0_
  13.2 0.2 collective-permute-done.1.refs_1_
  13.4 2.7 %collective-permute-done.3.refs_2_ = bf16[2,32,512]{2,1,0:T(8,128)(2,1)S(1)} collective-permute-done((bf16[2,32,512]{2,1,0:T(8,128)(2,1)S(1)}, bf16[2,32,512]{2,1,0:T(8,128)(2,1)S(1)}, u32[]{:S(2)}, u32[]{:S(2)}) %collective-permute-start.3) | collective-permute-done | bytes 65568 | tf_op jit(solution)/shard_map/ppermute | solution.py:440
  16.2 3.9 %collective-permute-start.5 = (bf16[4,2,32,512]{3,2,1,0:T(8,128)(2,1)S(1)}, bf16[4,2,32,512]{3,2,1,0:T(8,128)(2,1)S(1)}, u32[]{:S(2)}, u32[]{:S(2)}) collective-permute-start(bf16[4,2,32,512]{3,2,1,0:T(8,128)(2,1)S(1)} %pad_maximum_fusion), channel_id=1, source_target_pairs={{0,1},{1,0},{2,3},{3,2},{4,5},{5,4},{6,7},{7,6},{8,9},{9,8},{10,11... | collective-permute-start | bytes 786440 | tf_op jit(solution)/shard_map/ppermute | solution.py:483
  20.1 0.0 collective-permute-done.6.refs_2_
  20.1 0.0 copy-start.2
  20.1 1.6 %collective-permute-start.7 = (bf16[4,2,32,512]{3,2,1,0:T(8,128)(2,1)S(1)}, bf16[4,2,32,512]{3,2,1,0:T(8,128)(2,1)S(1)}, u32[]{:S(2)}, u32[]{:S(2)}) collective-permute-start(bf16[4,2,32,512]{3,2,1,0:T(8,128)(2,1)S(1)} %pad_maximum_fusion.1), channel_id=1, source_target_pairs={{0,2},{1,5},{2,0},{3,7},{4,6},{5,1},{6,4},{7,3},{8,10},{9,13},{10,... | collective-permute-start | bytes 786440 | tf_op jit(solution)/shard_map/ppermute | solution.py:440
  21.7 3.1 %load_tables.1 = (bf16[1024,512]{1,0:T(8,128)(2,1)S(1)}, bf16[1024,512]{1,0:T(8,128)(2,1)S(1)}, bf16[4,256,1024]{2,1,0:T(8,128)(2,1)S(1)}, bf16[2,256,512]{2,1,0:T(8,128)(2,1)S(1)}, f32[2,512,512]{2,1,0:T(8,128)S(1)}) custom-call(bf16[1024,512]{1,0:T(8,128)(2,1)} %constant.10.clone.refs_0_, bf16[1024,512]{1,0:T(8,128)(2,1)} %constant.11.clone.refs_1_, ...), custom_call_target="tpu_custom_call" | custom-call | bytes 12582912 | tf_op jit(solution)/shard_map/load_tables/pallas_call | solution.py:152
  24.7 0.0 collective-permute-done.5.refs_4_
  24.8 0.0 copy-start.3
  24.8 2.5 %forward.1.refs_0_ = f32[512,512]{1,0:T(8,128)S(1)} custom-call(bf16[2,32,512]{2,1,0:T(8,128)(2,1)S(1)} %collective-permute-done.refs_0_, bf16[2,32,512]{2,1,0:T(8,128)(2,1)S(1)} %collective-permute-done.1.refs_1_, bf16[2,32,512]{2,1,0:T(8,128)(2,1)S(1)} %collective-permute-done.3.refs_2_, bf16[2,32,512]{2,1,0:T(8,128)(2,1)S(1)} %collective-permute-done.4.refs_3_, ...), custom_call_target="tpu_custom_call" | custom-call | flops 1073741824 | bytes 6291456 | tf_op jit(solution)/shard_map/forward/pallas_call | solution.py:205
  27.3 0.0 collective-permute-done.7.refs_3_
  27.3 7.4 %inverse.1 = (bf16[1,1,131072]{2,1,0:T(2,128)(2,1)}, bf16[1,1,131072]{2,1,0:T(2,128)(2,1)}, f32[1,1]{1,0:T(1,128)}) custom-call(f32[512,512]{1,0:T(8,128)S(1)} %forward.1.refs_0_, bf16[2,2,32,512]{3,2,1,0:T(8,128)(2,1)S(1)} %pair_shards.1.refs_5_.refs_1_, bf16[2,2,32,512]{3,2,1,0:T(8,128)(2,1)S(1)} %collective-permute-done.6.refs_2_, ...), custom_call_target="tpu_custom_call" | custom-call | tf_op jit(solution)/shard_map/inverse/pallas_call | solution.py:408
  (7 shorter events, 0.1 us)
Async XLA Ops:
  0.6 9.7 %collective-permute-start.2 = (bf16[1,2,16384]{2,1,0:T(2,128)(2,1)}, bf16[1,2,16384]{2,1,0:T(2,128)(2,1)S(1)}, u32[]{:S(2)}, u32[]{:S(2)}) collective-permute-start(bf16[1,2,16384]{2,1,0:T(2,128)(2,1)} %shard_ref.1), channel_id=1, source_target_pairs={{0,8},{1,9},{2,10},{3,11},{4,12},{5,13},{6,14},{7,15},{8,0},{9,1},... | collective-permute-start | bytes 196616 | tf_op jit(solution)/shard_map/ppermute | solution.py:440
  4.7 0.9 %copy-start = (bf16[8,16384]{1,0:T(8,128)(2,1)S(1)}, bf16[8,16384]{1,0:T(8,128)(2,1)}, u32[]{:S(2)}) copy-start(bf16[8,16384]{1,0:T(8,128)(2,1)} %frames_ref.1) | copy-start | bytes 786436
  5.7 0.8 %copy-start.1 = (bf16[1,2,16384]{2,1,0:T(2,128)(2,1)S(1)}, bf16[1,2,16384]{2,1,0:T(2,128)(2,1)}, u32[]{:S(2)}) copy-start(bf16[1,2,16384]{2,1,0:T(2,128)(2,1)} %shard_ref.1) | copy-start | bytes 196612
  7.2 6.0 %collective-permute-start = (bf16[2,32,512]{2,1,0:T(8,128)(2,1)S(1)}, bf16[2,32,512]{2,1,0:T(8,128)(2,1)S(1)}, u32[]{:S(2)}, u32[]{:S(2)}) collective-permute-start(bf16[2,32,512]{2,1,0:T(8,128)(2,1)S(1)} %get-tuple-element.17), channel_id=1, source_target_pairs={{0,2},{1,9},{2,0},{3,11},{4,6},{5,13},{6,4},{7,15},{8,10},{9,1},{1... | collective-permute-start | bytes 196616 | tf_op jit(solution)/shard_map/ppermute | solution.py:440
  8.7 4.7 %collective-permute-start.1 = (bf16[2,32,512]{2,1,0:T(8,128)(2,1)S(1)}, bf16[2,32,512]{2,1,0:T(8,128)(2,1)S(1)}, u32[]{:S(2)}, u32[]{:S(2)}) collective-permute-start(bf16[2,32,512]{2,1,0:T(8,128)(2,1)S(1)} %get-tuple-element.18), channel_id=1, source_target_pairs={{0,4},{1,11},{2,6},{3,9},{4,0},{5,15},{6,2},{7,13},{8,12},{9,3},{1... | collective-permute-start | bytes 196616 | tf_op jit(solution)/shard_map/ppermute | solution.py:440
  10.4 5.7 %collective-permute-start.3 = (bf16[2,32,512]{2,1,0:T(8,128)(2,1)S(1)}, bf16[2,32,512]{2,1,0:T(8,128)(2,1)S(1)}, u32[]{:S(2)}, u32[]{:S(2)}) collective-permute-start(bf16[2,32,512]{2,1,0:T(8,128)(2,1)S(1)} %get-tuple-element.22), channel_id=1, source_target_pairs={{0,6},{1,13},{2,4},{3,15},{4,2},{5,9},{6,0},{7,11},{8,14},{9,5},{1... | collective-permute-start | bytes 196616 | tf_op jit(solution)/shard_map/ppermute | solution.py:440
  11.3 4.8 %collective-permute-start.4 = (bf16[2,32,512]{2,1,0:T(8,128)(2,1)S(1)}, bf16[2,32,512]{2,1,0:T(8,128)(2,1)S(1)}, u32[]{:S(2)}, u32[]{:S(2)}) collective-permute-start(bf16[2,32,512]{2,1,0:T(8,128)(2,1)S(1)} %get-tuple-element.23), channel_id=1, source_target_pairs={{1,15},{3,13},{5,11},{7,9},{9,7},{11,5},{13,3},{15,1},{17,31},{19,... | collective-permute-start | bytes 196616 | tf_op jit(solution)/shard_map/ppermute | solution.py:440
  12.0 8.1 %collective-permute-start.6 = (bf16[2,2,32,512]{3,2,1,0:T(8,128)(2,1)S(1)}, bf16[2,2,32,512]{3,2,1,0:T(8,128)(2,1)S(1)}, u32[]{:S(2)}, u32[]{:S(2)}) collective-permute-start(bf16[2,2,32,512]{3,2,1,0:T(8,128)(2,1)S(1)} %pair_shards.1.refs_5_.refs_1_), channel_id=1, source_target_pairs={{0,4},{1,3},{2,6},{3,1},{4,0},{5,7},{6,2},{7,5},{8,12},{9,11},{10,... | collective-permute-start | bytes 393224 | tf_op jit(solution)/shard_map/ppermute | solution.py:440
  16.2 8.6 %collective-permute-start.5 = (bf16[4,2,32,512]{3,2,1,0:T(8,128)(2,1)S(1)}, bf16[4,2,32,512]{3,2,1,0:T(8,128)(2,1)S(1)}, u32[]{:S(2)}, u32[]{:S(2)}) collective-permute-start(bf16[4,2,32,512]{3,2,1,0:T(8,128)(2,1)S(1)} %pad_maximum_fusion), channel_id=1, source_target_pairs={{0,1},{1,0},{2,3},{3,2},{4,5},{5,4},{6,7},{7,6},{8,9},{9,8},{10,11... | collective-permute-start | bytes 786440 | tf_op jit(solution)/shard_map/ppermute | solution.py:483
  20.1 4.7 %copy-start.2 = (s32[8,8]{1,0:T(8,128)S(1)}, s32[8,8]{1,0:T(8,128)}, u32[]{:S(2)}) copy-start(s32[8,8]{1,0:T(8,128)} %refs_6_.1) | copy-start | bytes 772
  20.1 7.2 %collective-permute-start.7 = (bf16[4,2,32,512]{3,2,1,0:T(8,128)(2,1)S(1)}, bf16[4,2,32,512]{3,2,1,0:T(8,128)(2,1)S(1)}, u32[]{:S(2)}, u32[]{:S(2)}) collective-permute-start(bf16[4,2,32,512]{3,2,1,0:T(8,128)(2,1)S(1)} %pad_maximum_fusion.1), channel_id=1, source_target_pairs={{0,2},{1,5},{2,0},{3,7},{4,6},{5,1},{6,4},{7,3},{8,10},{9,13},{10,... | collective-permute-start | bytes 786440 | tf_op jit(solution)/shard_map/ppermute | solution.py:440
  24.8 2.6 %copy-start.3 = (s32[1,3]{1,0:T(1,128)S(1)}, s32[1,3]{1,0:T(1,128)}, u32[]{:S(2)}) copy-start(s32[1,3]{1,0:T(1,128)} %refs_4_.2) | copy-start | bytes 40

commit v3 on v2

--- a/solution.py
+++ b/solution.py
@@ -15,14 +15,16 @@
 LENGTH = SIDE * SIDE
 AXES = ("groups", "segment", "template")
 MIB = 1 << 20
+STEP = 16
 BIN_LOW = (0, 32, 96, 128)
 ROUNDS = 4
+MASKS = ((3, 2, 1, 0), (7, 6, 5, 4))
 
 
 def strain_mask(step, core):
     if isinstance(core, int):
-        return (step + 1) % ROUNDS if core == 0 else step + ROUNDS
-    return jnp.where(core == 0, (step + 1) % ROUNDS, step + ROUNDS)
+        return MASKS[core][step]
+    return jnp.where(core == 0, MASKS[0][step], MASKS[1][step])
 
 
 def turn(rows, columns, modulus):
@@ -54,10 +56,21 @@
         )
     phase_cos, phase_sin = turn(digit, digit, LENGTH)
     phase = np.stack([phase_cos, phase_sin]).astype(np.float32)
+    coarse = [x[::STEP] for x in (phase_cos, phase_sin)]
+    fine = [x[:STEP] for x in (phase_cos, phase_sin)]
+    factors = np.concatenate([*coarse, *fine]).astype(np.float32)
 
 
     narrow = [x.astype(np.float32).astype(ml_dtypes.bfloat16) for x in (first, second, np.stack(third), np.stack(fourth))]
-    return (*narrow, phase)
+    return (*narrow, phase, factors)
+
+
+def in_hbm(*arrays):
+    return [pltpu.with_memory_space_constraint(x, pltpu.HBM) for x in arrays]
+
+
+def in_vmem(*arrays):
+    return [pltpu.with_memory_space_constraint(x, pltpu.VMEM) for x in arrays]
 
 
 def spread(source, wide, count, rows):
@@ -75,11 +88,21 @@
     rows = samples // SIDE
     tiles = SIDE // 128
 
-    def body(frames_ref, shard_ref, *refs):
-        outs, unpacked, wide, narrow = refs[: ROUNDS + 1], *refs[ROUNDS + 1 :]
+    def body(frames_hbm, shard_hbm, *refs):
+        outs, (unpacked, wide, narrow, frames_ref, shard_ref, arrived) = (
+            refs[: ROUNDS + 1],
+            refs[ROUNDS + 1 :],
+        )
+        copies = [
+            pltpu.make_async_copy(frames_hbm, frames_ref, arrived.at[0]),
+            pltpu.make_async_copy(shard_hbm, shard_ref, arrived.at[1]),
+        ]
+        for copy in copies:
+            copy.start()
         segment = lax.axis_index("segment")
         core = lax.axis_index("template")
         wide[:, count * rows :, :] = jnp.zeros((tiles, rows, 128), jnp.float32)
+        copies[0].wait()
         spread(frames_ref, wide, count, rows)
         for step, out_ref in enumerate(outs):
             mask = strain_mask(step, core) if step < ROUNDS else 0
@@ -88,6 +111,7 @@
                 out_ref[:, :, tile * 128 : tile * 128 + 128] = (
                     wide[tile, pl.ds(start, 2 * rows), :].astype(jnp.bfloat16).reshape(2, rows, 128)
                 )
+        copies[1].wait()
         unpack(shard_ref, narrow, unpacked.at[0])
 
     vmem = pl.BlockSpec(memory_space=pltpu.VMEM)
@@ -95,15 +119,18 @@
         body,
         out_shape=[pltpu.VMEM((2, rows, SIDE), jnp.bfloat16)] * (ROUNDS + 1)
         + [pltpu.VMEM((1, 2, rows, SIDE), jnp.bfloat16)],
-        in_specs=[vmem, vmem],
+        in_specs=[pl.BlockSpec(memory_space=pl.ANY)] * 2,
         out_specs=[vmem] * (ROUNDS + 2),
         scratch_shapes=[
             pltpu.VMEM((tiles, (count + 1) * rows, 128), jnp.float32),
             pltpu.VMEM((tiles, 2 * rows, 128), jnp.float32),
+            pltpu.VMEM(frames.shape, frames.dtype),
+            pltpu.VMEM(shard.shape, shard.dtype),
+            pltpu.SemaphoreType.DMA((2,)),
         ],
         compiler_params=pltpu.CompilerParams(vmem_limit_bytes=4 * MIB),
         name="split_frames",
-    )(frames, shard)
+    )(*in_hbm(frames, shard))
 
 
 def unpack(shard_ref, narrow, out_ref):
@@ -156,31 +183,45 @@
         out_specs=[pl.BlockSpec(memory_space=pltpu.VMEM)] * count,
         scratch_shapes=[pltpu.SemaphoreType.DMA((count,))],
         compiler_params=pltpu.CompilerParams(vmem_limit_bytes=1 * MIB),
-        cost_estimate=pl.CostEstimate(flops=0, bytes_accessed=12 * MIB, transcendentals=0),
+        cost_estimate=pl.CostEstimate(flops=0, bytes_accessed=4 * MIB, transcendentals=0),
         name="load_tables",
-    )(*(pltpu.with_memory_space_constraint(x, pltpu.HBM) for x in arrays), after)
-
-
-def forward_body(signal, first, second, phase, spectrum, turned):
+    )(*in_hbm(*arrays), after)
+
+
+def phases(factors, first, count):
+    groups = SIDE // STEP
+    coarse_cos, coarse_sin = (
+        factors[pl.ds(kind * groups + first, count), :][:, None, :] for kind in range(2)
+    )
+    fine_cos, fine_sin = (
+        factors[2 * groups + kind * STEP : 2 * groups + (kind + 1) * STEP, :][None]
+        for kind in range(2)
+    )
+    cosine = coarse_cos * fine_cos - coarse_sin * fine_sin
+    sine = coarse_sin * fine_cos + coarse_cos * fine_sin
+    return cosine.reshape(count * STEP, SIDE), sine.reshape(count * STEP, SIDE)
+
+
+def forward_body(signal, first, second, factors, spectrum, turned):
     rows = SIDE // 2
 
-    def chunk(index, carry):
-        here = pl.ds(pl.multiple_of(index * rows, rows), rows)
-        there = pl.ds(pl.multiple_of(SIDE + index * rows, rows), rows)
+    def chunk(index):
+        here = pl.ds(index * rows, rows)
+        there = pl.ds(SIDE + index * rows, rows)
         real = jnp.dot(first[here, :], signal[...], preferred_element_type=jnp.float32)
         imag = jnp.dot(first[there, :], signal[...], preferred_element_type=jnp.float32)
-        cosine, sine = phase[0, here, :], phase[1, here, :]
+        cosine, sine = phases(factors, index * (rows // STEP), rows // STEP)
         turned[here, :SIDE] = (real * cosine + imag * sine).astype(jnp.bfloat16)
         turned[here, SIDE:] = (imag * cosine - real * sine).astype(jnp.bfloat16)
         spectrum[here, :] = jnp.dot(
             turned[here, :], second[...], preferred_element_type=jnp.float32
         )
-        return carry
-
-    lax.fori_loop(0, SIDE // rows, chunk, 0)
-
-
-def forward_received(received, other, mine, frame_slot, first, second, phase):
+
+    for index in range(SIDE // rows):
+        chunk(index)
+
+
+def forward_received(received, other, mine, frame_slot, first, second, factors):
     rows = mine.shape[1]
 
     def body(*refs):
@@ -216,10 +257,10 @@
             flops=4 * SIDE**3 * 2, bytes_accessed=6 * MIB, transcendentals=0
         ),
         name="forward",
-    )(*received, other, mine, frame_slot, first, second, phase)
-
-
-def forward_arranged(signal, first, second, phase):
+    )(*received, other, mine, frame_slot, first, *in_vmem(second), factors)
+
+
+def forward_arranged(signal, first, second, factors):
     def body(signal_ref, first_ref, second_ref, phase_ref, spectrum, turned):
         forward_body(signal_ref, first_ref, second_ref, phase_ref, spectrum, turned)
 
@@ -232,7 +273,7 @@
         scratch_shapes=[pltpu.VMEM((SIDE, 2 * SIDE), jnp.bfloat16)],
         compiler_params=pltpu.CompilerParams(vmem_limit_bytes=12 * MIB),
         name="forward",
-    )(signal, first, second, phase)
+    )(signal, first, second, factors)
 
 
 def owners_of(segment, core, doubled):
@@ -422,9 +463,9 @@
             pltpu.VMEM((4, 8, quarter), jnp.float32),
             pltpu.VMEM((2, LENGTH // 256, 128), jnp.float32),
         ],
-        compiler_params=pltpu.CompilerParams(vmem_limit_bytes=20 * MIB),
+        compiler_params=pltpu.CompilerParams(vmem_limit_bytes=16 * MIB),
         name="inverse",
-    )(spectrum, *blocks, edges, third, fourth, phase)
+    )(spectrum, *blocks, edges, *in_vmem(third, fourth, phase))
 
 
 def exchange(value, mesh_shape, mask_of):
@@ -472,24 +513,30 @@
     if staged:
         across = exchange(templates, mesh_shape, lambda core: 4)
         *outgoing, mine, unpacked = split_frames(strain_frames, templates)
-        pair = pair_shards(unpacked, across)
-        *late, pair = lax.optimization_barrier((*outgoing[2:], pair))
         received = [
             exchange(value, mesh_shape, functools.partial(strain_mask, step))
-            for step, value in enumerate([*outgoing[:2], *late])
+            for step, value in enumerate(outgoing[:3])
+        ]
+        pair = pair_shards(unpacked, across)
+        *late, pair = lax.optimization_barrier((*outgoing[3:], pair))
+        received += [
+            exchange(value, mesh_shape, functools.partial(strain_mask, step + 3))
+            for step, value in enumerate(late)
         ]
         near = exchange(pair, mesh_shape, lambda core: 2 - core)
-        first, second, third, fourth, phase = load_tables(constants, pair)
+        first, second, third, fourth, phase, factors = constants
+        first, factors = load_tables((first, factors), pair)
+        *received, first = lax.optimization_barrier((*received, first))
         other = lax.ppermute(jnp.stack(received), "template", [(0, 1), (1, 0)])
         far = exchange(jnp.concatenate([pair, near]), mesh_shape, lambda core: 1 + core)
         blocks = [pair, near, far]
-        spectrum = forward_received(received, other, mine, frame_slot, first, second, phase)
+        spectrum = forward_received(received, other, mine, frame_slot, first, second, factors)
     else:
-        first, second, third, fourth, phase = constants
+        first, second, third, fourth, phase, factors = constants
         signal = arrange_plain(strain_frames, frame_slot)
         whole = lax.all_gather(templates, "segment", axis=2, tiled=True)
         blocks = [whole.reshape(1, 2, HALF, SIDE)]
-        spectrum = forward_arranged(signal, first, second, phase)
+        spectrum = forward_arranged(signal, first, second, factors)
     return inverse(spectrum, blocks, bin_edges, third, fourth, phase, staged)
 
 

time: 34.9 us -> 31.3 us (0.90)
  local copies, waits for them, and re-layouts: 1.8 us -> 0.03 us
  starting transfers between devices: 15.5 us -> 14 us
  Pallas kernels: 13.7 us -> 12.7 us
  waiting for transfers between devices: 2.93 us -> 3.67 us
    pallas_call x1, Pallas kernels: 3.07 us -> 1.26 us  [load_tables(): pl.pallas_call(body, out_shape=[pltpu.VMEM(x.shape, x.dtype) for x in arr...]
    unnamed x8 -> x12, local copies, waits for them, and re-layouts: 1.8 us -> 0.03 us
    pallas_call x1, Pallas kernels: 0.63 us -> 1.6 us  [split_frames(): pl.pallas_call(body, out_shape=[pltpu.VMEM((2, rows, SIDE), jnp.bfloat16)...]
    ppermute x7, starting transfers between devices: 11.6 us -> 10.6 us  [exchange(): return lax.ppermute(value, AXES, pairs)]
    ppermute x1, starting transfers between devices: 3.89 us -> 3.32 us  [local(): other = lax.ppermute(jnp.stack(received), 'template', [(0, 1), (1, 0)])]
    ppermute x1, waiting for transfers between devices: 0.01 us -> 0.42 us  [local(): other = lax.ppermute(jnp.stack(received), 'template', [(0, 1), (1, 0)])]
  transfers between devices with their start and end apart: 8 -> 8, of which waited for: 2 -> 3; matrix products, arithmetic and copies ran while one was open for 0% -> 0% of each run, Pallas kernels for 18% -> 17%
where the time goes in v3:
time: 31.3 us; the launch traced here: 31.1 us
  starting transfers between devices  14 us (45%)
  Pallas kernels  12.7 us (41%)
  waiting for transfers between devices  3.67 us (12%)
  between operations  0.74 us (2%)
    ppermute x7, starting transfers between devices, exchange(): return lax.ppermute(value, AXES, pairs)  10.6 us
    pallas_call x1, Pallas kernels, inverse(): pl.pallas_call(body, out_shape=(jax.ShapeDtypeStruct((1, 1, LENGTH // 2),...  7.37 us
    ppermute x1, starting transfers between devices, local(): other = lax.ppermute(jnp.stack(received), 'template', [(0, 1), (1, 0)])  3.32 us
    ppermute x7, waiting for transfers between devices, exchange(): return lax.ppermute(value, AXES, pairs)  3.24 us
    pallas_call x1, Pallas kernels, forward_received(): pl.pallas_call(body, out_shape=pltpu.VMEM((SIDE, SIDE), jnp.float32), in_...  2.34 us
    pallas_call x1, Pallas kernels, split_frames(): pl.pallas_call(body, out_shape=[pltpu.VMEM((2, rows, SIDE), jnp.bfloat16)...  1.6 us
    pallas_call x1, Pallas kernels, load_tables(): pl.pallas_call(body, out_shape=[pltpu.VMEM(x.shape, x.dtype) for x in arr...  1.26 us
  transfers between devices with their start and end apart: 8, of which 3 were waited for; matrix products, arithmetic and copies ran while one was open for 0% of the time, Pallas kernels for 17%

profile of v3, /device:TPU:0, one launch (start us, length us, event | category | flops | bytes accessed | tf_op | source)
XLA Modules:
  0.0 31.1 jit_solution(10962581106467364907)
XLA Ops:
  0.6 0.0 copy-start.5
  0.7 4.1 %collective-permute-start.3 = (bf16[1,2,16384]{2,1,0:T(2,128)(2,1)}, bf16[1,2,16384]{2,1,0:T(2,128)(2,1)S(1)}, u32[]{:S(2)}, u32[]{:S(2)}) collective-permute-start(bf16[1,2,16384]{2,1,0:T(2,128)(2,1)} %shard_hbm.1), channel_id=1, source_target_pairs={{0,8},{1,9},{2,10},{3,11},{4,12},{5,13},{6,14},{7,15},{8,0},{9,1},... | collective-permute-start | bytes 196616 | tf_op jit(solution)/shard_map/ppermute | solution.py:481
  4.8 1.6 %split_frames.1 = (bf16[2,32,512]{2,1,0:T(8,128)(2,1)S(1)}, bf16[2,32,512]{2,1,0:T(8,128)(2,1)S(1)}, bf16[2,32,512]{2,1,0:T(8,128)(2,1)S(1)}, bf16[2,32,512]{2,1...) custom-call(bf16[8,16384]{1,0:T(8,128)(2,1)} %frames_hbm.1, ...), custom_call_target="tpu_custom_call" | custom-call | tf_op jit(solution)/shard_map/split_frames/pallas_call | solution.py:118
  6.4 2.6 %collective-permute-start = (bf16[2,32,512]{2,1,0:T(8,128)(2,1)S(1)}, bf16[2,32,512]{2,1,0:T(8,128)(2,1)S(1)}, u32[]{:S(2)}, u32[]{:S(2)}) collective-permute-start(bf16[2,32,512]{2,1,0:T(8,128)(2,1)S(1)} %get-tuple-element.18), channel_id=1, source_target_pairs={{0,6},{1,15},{2,4},{3,13},{4,2},{5,11},{6,0},{7,9},{8,14},{9,7},{1... | collective-permute-start | bytes 196616 | tf_op jit(solution)/shard_map/ppermute | solution.py:481
  8.9 0.4 %collective-permute-start.1 = (bf16[2,32,512]{2,1,0:T(8,128)(2,1)S(1)}, bf16[2,32,512]{2,1,0:T(8,128)(2,1)S(1)}, u32[]{:S(2)}, u32[]{:S(2)}) collective-permute-start(bf16[2,32,512]{2,1,0:T(8,128)(2,1)S(1)} %get-tuple-element.19), channel_id=1, source_target_pairs={{0,4},{1,13},{2,6},{3,15},{4,0},{5,9},{6,2},{7,11},{8,12},{9,5},{1... | collective-permute-start | bytes 196616 | tf_op jit(solution)/shard_map/ppermute | solution.py:481
  9.4 0.5 %collective-permute-start.2 = (bf16[2,32,512]{2,1,0:T(8,128)(2,1)S(1)}, bf16[2,32,512]{2,1,0:T(8,128)(2,1)S(1)}, u32[]{:S(2)}, u32[]{:S(2)}) collective-permute-start(bf16[2,32,512]{2,1,0:T(8,128)(2,1)S(1)} %get-tuple-element.20), channel_id=1, source_target_pairs={{0,2},{1,11},{2,0},{3,9},{4,6},{5,15},{6,4},{7,13},{8,10},{9,3},{1... | collective-permute-start | bytes 196616 | tf_op jit(solution)/shard_map/ppermute | solution.py:481
  9.9 0.0 collective-permute-done.3.across_ref
  9.9 0.1 pair_shards.1.refs_2_.refs_1_
  10.0 0.7 %collective-permute-start.4 = (bf16[2,32,512]{2,1,0:T(8,128)(2,1)S(1)}, bf16[2,32,512]{2,1,0:T(8,128)(2,1)S(1)}, u32[]{:S(2)}, u32[]{:S(2)}) collective-permute-start(bf16[2,32,512]{2,1,0:T(8,128)(2,1)S(1)} %get-tuple-element.23), channel_id=1, source_target_pairs={{1,9},{3,11},{5,13},{7,15},{9,1},{11,3},{13,5},{15,7},{17,25},{19,... | collective-permute-start | bytes 196616 | tf_op jit(solution)/shard_map/ppermute | solution.py:481
  10.7 1.6 %collective-permute-start.6 = (bf16[2,2,32,512]{3,2,1,0:T(8,128)(2,1)S(1)}, bf16[2,2,32,512]{3,2,1,0:T(8,128)(2,1)S(1)}, u32[]{:S(2)}, u32[]{:S(2)}) collective-permute-start(bf16[2,2,32,512]{3,2,1,0:T(8,128)(2,1)S(1)} %pair_shards.1.refs_2_.refs_1_), channel_id=1, source_target_pairs={{0,4},{1,3},{2,6},{3,1},{4,0},{5,7},{6,2},{7,5},{8,12},{9,11},{10,... | collective-permute-start | bytes 393224 | tf_op jit(solution)/shard_map/ppermute | solution.py:481
  12.3 1.3 %load_tables.1 = (bf16[1024,512]{1,0:T(8,128)(2,1)S(1)}, f32[96,512]{1,0:T(8,128)S(1)}) custom-call(bf16[1024,512]{1,0:T(8,128)(2,1)} %constant.12.clone.refs_0_, f32[96,512]{1,0:T(8,128)} %constant.13.clone.refs_1_, bf16[2,2,32,512]{3,2,1,0:T(8,128)(2,1)S(1)} %pair_shards.1.refs_2_.refs_1_), custom_call_target="tpu_custom_call" | custom-call | bytes 4194304 | tf_op jit(solution)/shard_map/load_tables/pallas_call | solution.py:179
  13.6 0.0 collective-permute-done.refs_0_
  13.6 0.3 collective-permute-done.1.refs_1_
  13.9 0.0 collective-permute-done.2.refs_2_
  13.9 0.0 collective-permute-done.4.refs_3_
  13.9 3.3 %collective-permute-start.5 = (bf16[4,2,32,512]{3,2,1,0:T(8,128)(2,1)S(1)}, bf16[4,2,32,512]{3,2,1,0:T(8,128)(2,1)S(1)}, u32[]{:S(2)}, u32[]{:S(2)}) collective-permute-start(bf16[4,2,32,512]{3,2,1,0:T(8,128)(2,1)S(1)} %pad_maximum_fusion), channel_id=1, source_target_pairs={{0,1},{1,0},{2,3},{3,2},{4,5},{5,4},{6,7},{7,6},{8,9},{9,8},{10,11... | collective-permute-start | bytes 786440 | tf_op jit(solution)/shard_map/ppermute | solution.py:530
  17.2 0.0 collective-permute-done.6.refs_2_
  17.3 0.0 copy-start
  17.3 0.0 copy-start.3
  17.3 0.7 %collective-permute-start.7 = (bf16[4,2,32,512]{3,2,1,0:T(8,128)(2,1)S(1)}, bf16[4,2,32,512]{3,2,1,0:T(8,128)(2,1)S(1)}, u32[]{:S(2)}, u32[]{:S(2)}) collective-permute-start(bf16[4,2,32,512]{3,2,1,0:T(8,128)(2,1)S(1)} %pad_maximum_fusion.1), channel_id=1, source_target_pairs={{0,2},{1,5},{2,0},{3,7},{4,6},{5,1},{6,4},{7,3},{8,10},{9,13},{10,... | collective-permute-start | bytes 786440 | tf_op jit(solution)/shard_map/ppermute | solution.py:481
  18.0 0.4 %collective-permute-done.5.refs_4_ = bf16[4,2,32,512]{3,2,1,0:T(8,128)(2,1)S(1)} collective-permute-done((bf16[4,2,32,512]{3,2,1,0:T(8,128)(2,1)S(1)}, bf16[4,2,32,512]{3,2,1,0:T(8,128)(2,1)S(1)}, u32[]{:S(2)}, u32[]{:S(2)}) %collective-permute-start.5) | collective-permute-done | bytes 262176 | tf_op jit(solution)/shard_map/ppermute | solution.py:530
  18.4 2.3 %forward.1.refs_0_ = f32[512,512]{1,0:T(8,128)S(1)} custom-call(bf16[2,32,512]{2,1,0:T(8,128)(2,1)S(1)} %collective-permute-done.refs_0_, bf16[2,32,512]{2,1,0:T(8,128)(2,1)S(1)} %collective-permute-done.1.refs_1_, bf16[2,32,512]{2,1,0:T(8,128)(2,1)S(1)} %collective-permute-done.2.refs_2_, bf16[2,32,512]{2,1,0:T(8,128)(2,1)S(1)} %collective-permute-done.4.refs_3_, ...), custom_call_target="tpu_custom_call" | custom-call | flops 1073741824 | bytes 6291456 | tf_op jit(solution)/shard_map/forward/pallas_call | solution.py:246
  20.8 3.0 %collective-permute-done.7.refs_3_ = bf16[4,2,32,512]{3,2,1,0:T(8,128)(2,1)S(1)} collective-permute-done((bf16[4,2,32,512]{3,2,1,0:T(8,128)(2,1)S(1)}, bf16[4,2,32,512]{3,2,1,0:T(8,128)(2,1)S(1)}, u32[]{:S(2)}, u32[]{:S(2)}) %collective-permute-start.7) | collective-permute-done | bytes 262176 | tf_op jit(solution)/shard_map/ppermute | solution.py:481
  23.8 7.4 %inverse.1 = (bf16[1,1,131072]{2,1,0:T(2,128)(2,1)}, bf16[1,1,131072]{2,1,0:T(2,128)(2,1)}, f32[1,1]{1,0:T(1,128)}) custom-call(f32[512,512]{1,0:T(8,128)S(1)} %forward.1.refs_0_, bf16[2,2,32,512]{3,2,1,0:T(8,128)(2,1)S(1)} %pair_shards.1.refs_2_.refs_1_, bf16[2,2,32,512]{3,2,1,0:T(8,128)(2,1)S(1)} %collective-permute-done.6.refs_2_, ...), custom_call_target="tpu_custom_call" | custom-call | tf_op jit(solution)/shard_map/inverse/pallas_call | solution.py:449
  (11 shorter events, 0.1 us)
Async XLA Ops:
  0.6 17.8 %copy-start.5 = (bf16[1024,512]{1,0:T(8,128)(2,1)S(1)}, bf16[1024,512]{1,0:T(8,128)(2,1)}, u32[]{:S(2)}) copy-start(bf16[1024,512]{1,0:T(8,128)(2,1)} %constant.14.clone.refs_8_) | copy-start | bytes 3145732
  0.6 17.8 %copy-start.4 = (s32[8,8]{1,0:T(8,128)S(1)}, s32[8,8]{1,0:T(8,128)}, u32[]{:S(2)}) copy-start(s32[8,8]{1,0:T(8,128)} %refs_6_.2) | copy-start | bytes 772
  0.7 9.3 %collective-permute-start.3 = (bf16[1,2,16384]{2,1,0:T(2,128)(2,1)}, bf16[1,2,16384]{2,1,0:T(2,128)(2,1)S(1)}, u32[]{:S(2)}, u32[]{:S(2)}) collective-permute-start(bf16[1,2,16384]{2,1,0:T(2,128)(2,1)} %shard_hbm.1), channel_id=1, source_target_pairs={{0,8},{1,9},{2,10},{3,11},{4,12},{5,13},{6,14},{7,15},{8,0},{9,1},... | collective-permute-start | bytes 196616 | tf_op jit(solution)/shard_map/ppermute | solution.py:481
  6.4 7.3 %collective-permute-start = (bf16[2,32,512]{2,1,0:T(8,128)(2,1)S(1)}, bf16[2,32,512]{2,1,0:T(8,128)(2,1)S(1)}, u32[]{:S(2)}, u32[]{:S(2)}) collective-permute-start(bf16[2,32,512]{2,1,0:T(8,128)(2,1)S(1)} %get-tuple-element.18), channel_id=1, source_target_pairs={{0,6},{1,15},{2,4},{3,13},{4,2},{5,11},{6,0},{7,9},{8,14},{9,7},{1... | collective-permute-start | bytes 196616 | tf_op jit(solution)/shard_map/ppermute | solution.py:481
  8.9 4.9 %collective-permute-start.1 = (bf16[2,32,512]{2,1,0:T(8,128)(2,1)S(1)}, bf16[2,32,512]{2,1,0:T(8,128)(2,1)S(1)}, u32[]{:S(2)}, u32[]{:S(2)}) collective-permute-start(bf16[2,32,512]{2,1,0:T(8,128)(2,1)S(1)} %get-tuple-element.19), channel_id=1, source_target_pairs={{0,4},{1,13},{2,6},{3,15},{4,0},{5,9},{6,2},{7,11},{8,12},{9,5},{1... | collective-permute-start | bytes 196616 | tf_op jit(solution)/shard_map/ppermute | solution.py:481
  9.4 4.5 %collective-permute-start.2 = (bf16[2,32,512]{2,1,0:T(8,128)(2,1)S(1)}, bf16[2,32,512]{2,1,0:T(8,128)(2,1)S(1)}, u32[]{:S(2)}, u32[]{:S(2)}) collective-permute-start(bf16[2,32,512]{2,1,0:T(8,128)(2,1)S(1)} %get-tuple-element.20), channel_id=1, source_target_pairs={{0,2},{1,11},{2,0},{3,9},{4,6},{5,15},{6,4},{7,13},{8,10},{9,3},{1... | collective-permute-start | bytes 196616 | tf_op jit(solution)/shard_map/ppermute | solution.py:481
  10.0 3.8 %collective-permute-start.4 = (bf16[2,32,512]{2,1,0:T(8,128)(2,1)S(1)}, bf16[2,32,512]{2,1,0:T(8,128)(2,1)S(1)}, u32[]{:S(2)}, u32[]{:S(2)}) collective-permute-start(bf16[2,32,512]{2,1,0:T(8,128)(2,1)S(1)} %get-tuple-element.23), channel_id=1, source_target_pairs={{1,9},{3,11},{5,13},{7,15},{9,1},{11,3},{13,5},{15,7},{17,25},{19,... | collective-permute-start | bytes 196616 | tf_op jit(solution)/shard_map/ppermute | solution.py:481
  10.7 6.5 %collective-permute-start.6 = (bf16[2,2,32,512]{3,2,1,0:T(8,128)(2,1)S(1)}, bf16[2,2,32,512]{3,2,1,0:T(8,128)(2,1)S(1)}, u32[]{:S(2)}, u32[]{:S(2)}) collective-permute-start(bf16[2,2,32,512]{3,2,1,0:T(8,128)(2,1)S(1)} %pair_shards.1.refs_2_.refs_1_), channel_id=1, source_target_pairs={{0,4},{1,3},{2,6},{3,1},{4,0},{5,7},{6,2},{7,5},{8,12},{9,11},{10,... | collective-permute-start | bytes 393224 | tf_op jit(solution)/shard_map/ppermute | solution.py:481
  13.9 9.9 %copy-start.2 = (bf16[2,256,512]{2,1,0:T(8,128)(2,1)S(1)}, bf16[2,256,512]{2,1,0:T(8,128)(2,1)}, u32[]{:S(2)}) copy-start(bf16[2,256,512]{2,1,0:T(8,128)(2,1)} %constant.16.clone.refs_6_) | copy-start | bytes 1572868
  13.9 4.5 %collective-permute-start.5 = (bf16[4,2,32,512]{3,2,1,0:T(8,128)(2,1)S(1)}, bf16[4,2,32,512]{3,2,1,0:T(8,128)(2,1)S(1)}, u32[]{:S(2)}, u32[]{:S(2)}) collective-permute-start(bf16[4,2,32,512]{3,2,1,0:T(8,128)(2,1)S(1)} %pad_maximum_fusion), channel_id=1, source_target_pairs={{0,1},{1,0},{2,3},{3,2},{4,5},{5,4},{6,7},{7,6},{8,9},{9,8},{10,11... | collective-permute-start | bytes 786440 | tf_op jit(solution)/shard_map/ppermute | solution.py:530
  17.3 6.5 %copy-start.1 = (f32[2,512,512]{2,1,0:T(8,128)S(1)}, f32[2,512,512]{2,1,0:T(8,128)}, u32[]{:S(2)}) copy-start(f32[2,512,512]{2,1,0:T(8,128)} %constant.17.clone.refs_7_) | copy-start | bytes 6291460
  17.3 6.5 %copy-start = (bf16[4,256,1024]{2,1,0:T(8,128)(2,1)S(1)}, bf16[4,256,1024]{2,1,0:T(8,128)(2,1)}, u32[]{:S(2)}) copy-start(bf16[4,256,1024]{2,1,0:T(8,128)(2,1)} %constant.15.clone.refs_5_) | copy-start | bytes 6291460
  17.3 6.5 %copy-start.3 = (s32[1,3]{1,0:T(1,128)S(1)}, s32[1,3]{1,0:T(1,128)}, u32[]{:S(2)}) copy-start(s32[1,3]{1,0:T(1,128)} %refs_4_.1) | copy-start | bytes 40
  17.3 6.4 %collective-permute-start.7 = (bf16[4,2,32,512]{3,2,1,0:T(8,128)(2,1)S(1)}, bf16[4,2,32,512]{3,2,1,0:T(8,128)(2,1)S(1)}, u32[]{:S(2)}, u32[]{:S(2)}) collective-permute-start(bf16[4,2,32,512]{3,2,1,0:T(8,128)(2,1)S(1)} %pad_maximum_fusion.1), channel_id=1, source_target_pairs={{0,2},{1,5},{2,0},{3,7},{4,6},{5,1},{6,4},{7,3},{8,10},{9,13},{10,... | collective-permute-start | bytes 786440 | tf_op jit(solution)/shard_map/ppermute | solution.py:481

commit v4 on v3

--- a/solution.py
+++ b/solution.py
@@ -18,7 +18,7 @@
 STEP = 16
 BIN_LOW = (0, 32, 96, 128)
 ROUNDS = 4
-MASKS = ((3, 2, 1, 0), (7, 6, 5, 4))
+MASKS = ((7, 2, 1, 0), (3, 6, 5, 4))
 
 
 def strain_mask(step, core):
@@ -43,19 +43,19 @@
     column = np.arange(HALF // 2)
     for start in BIN_LOW:
         chosen = np.where(column >= start, column, column + HALF // 2)
-        third.append(
-            np.block([[cosine[chosen], sine[chosen]], [-sine[chosen], cosine[chosen]]])
-        )
+        real = np.concatenate([cosine[chosen], -sine[chosen]])
+        imag = np.concatenate([sine[chosen], cosine[chosen]])
+        tiles = np.stack([real, imag], axis=1).reshape(HALF, 2, SIDE // 128, 128)
+        third.append(tiles.swapaxes(1, 2).reshape(HALF, 2 * SIDE))
     fourth = []
     for parity in range(2):
         kept = slice(HALF // 2 + parity, HALF // 2 + HALF, 2)
-        fourth.append(
-            np.block(
-                [[cosine[kept, low], -sine[kept, low]], [sine[kept, low], cosine[kept, low]]]
-            )
-        )
+        real = np.concatenate([cosine[kept, low], -sine[kept, low]], axis=1)
+        imag = np.concatenate([sine[kept, low], cosine[kept, low]], axis=1)
+        pairs = np.stack([real.reshape(-1, 8, SIDE), imag.reshape(-1, 8, SIDE)], axis=1)
+        fourth.append(pairs.reshape(HALF, SIDE))
     phase_cos, phase_sin = turn(digit, digit, LENGTH)
-    phase = np.stack([phase_cos, phase_sin]).astype(np.float32)
+    phase = np.stack([phase_cos, phase_sin]).astype(np.float32).astype(ml_dtypes.bfloat16)
     coarse = [x[::STEP] for x in (phase_cos, phase_sin)]
     fine = [x[:STEP] for x in (phase_cos, phase_sin)]
     factors = np.concatenate([*coarse, *fine]).astype(np.float32)
@@ -288,13 +288,12 @@
     n_blocks = len(blocks)
     shard = blocks[0].shape[2]
     quarter = HALF // 2
-    wide = SIDE // 2
 
     def body(*refs):
         spectrum_ref, block_refs = refs[0], refs[1 : 1 + n_blocks]
         edge_ref, third_ref, fourth_ref, phase_ref = refs[1 + n_blocks : 5 + n_blocks]
         snr_ref, chisq_ref, peak_ref = refs[5 + n_blocks : 8 + n_blocks]
-        gathered, flipped, masked, turned, sums, series = refs[8 + n_blocks :]
+        gathered, flipped, masked, turned, sums = refs[8 + n_blocks :]
         segment = lax.axis_index("segment")
         core = lax.axis_index("template")
         for block, owners in zip(block_refs, owners_of(segment, core, doubled), strict=True):
@@ -304,12 +303,14 @@
                     gathered[part, here, :] = block[place, part]
         for part in range(2):
             flipped[:, part * HALF : (part + 1) * HALF] = gathered[part].T
-        edge = [edge_ref[0, number] for number in range(3)]
+        edge = [edge_ref[:, number : number + 1] for number in range(3)]
         sums[...] = jnp.zeros_like(sums)
-        step = 32
-
-        def correlate(index, carry):
-            here = pl.ds(pl.multiple_of(index * step, step), step)
+        step = 16
+
+        def correlate(index):
+            here = slice(index * step, (index + 1) * step)
+            half, place = index // (HALF // step), index % (HALF // step)
+            there = slice((2 * place + half) * step, (2 * place + half + 1) * step)
             spec_real = [spectrum_ref[here, q * quarter : (q + 1) * quarter] for q in range(2)]
             spec_imag = [spectrum_ref[here, (q + 2) * quarter : (q + 3) * quarter] for q in range(2)]
             temp_real = [
@@ -359,59 +360,64 @@
                         second_half, power[1], zero
                     )
                 for part in range(2):
-                    masked[number, here, part * quarter : (part + 1) * quarter] = chosen[
+                    masked[number, there, part * quarter : (part + 1) * quarter] = chosen[
                         part
                     ].astype(jnp.bfloat16)
                 folded = strength[0:8]
                 for start in range(8, step, 8):
                     folded = folded + strength[start : start + 8]
                 sums[number] += folded
-            return carry
-
-        lax.fori_loop(0, SIDE // step, correlate, 0)
-
-        def first_pass(number, carry):
-            for tile in range(SIDE // wide):
-                here = slice(tile * wide, (tile + 1) * wide)
-                there = slice(SIDE + tile * wide, SIDE + (tile + 1) * wide)
-                real = jnp.dot(
-                    masked[number], third_ref[number, :, here], preferred_element_type=jnp.float32
+
+        for index in range(SIDE // step):
+            correlate(index)
+
+        def first_pass(number, tile):
+            product = jnp.dot(
+                masked[number],
+                third_ref[number, :, 2 * tile * 128 : 2 * (tile + 1) * 128],
+                preferred_element_type=jnp.float32,
+            ).reshape(HALF // step, 2, step, 2 * 128)
+            lanes = slice(tile * 128, (tile + 1) * 128)
+            real, imag = [], []
+            for half in range(2):
+                old_real, old_imag = (
+                    product[:, half, :, part * 128 : (part + 1) * 128].astype(jnp.bfloat16)
+                    for part in range(2)
                 )
-                imag = jnp.dot(
-                    masked[number], third_ref[number, :, there], preferred_element_type=jnp.float32
+                cosine, sine = (
+                    phase_ref[kind, half * HALF : (half + 1) * HALF, lanes].reshape(
+                        HALF // step, step, 128
+                    )
+                    for kind in range(2)
                 )
-                cosine, sine = phase_ref[0, :, here], phase_ref[1, :, here]
-                new_real = real * cosine - imag * sine
-                new_imag = real * sine + imag * cosine
-                for part, value in enumerate((new_real, new_imag)):
-                    rows = slice(part * HALF, (part + 1) * HALF)
-                    upper, lower = value[:HALF], value[HALF:]
-                    turned[number, 0, rows, here] = (upper + lower).astype(jnp.bfloat16)
-                    turned[number, 1, rows, here] = (upper - lower).astype(jnp.bfloat16)
-            return carry
-
-        lax.fori_loop(0, 4, first_pass, 0, unroll=True)
+                real.append(old_real * cosine - old_imag * sine)
+                imag.append(old_real * sine + old_imag * cosine)
+            for part, (upper, lower) in enumerate((real, imag)):
+                rows = slice(part * HALF, (part + 1) * HALF)
+                columns = slice(number * 128, (number + 1) * 128)
+                for parity, value in enumerate((upper + lower, upper - lower)):
+                    turned[parity, tile, rows, columns] = value.reshape(HALF, 128)
+
+        for number in range(4):
+            for tile in range(SIDE // 128):
+                first_pass(number, tile)
 
         bin_power = [jnp.sum(sums[number]) for number in range(4)]
         total = (bin_power[0] + bin_power[1]) + (bin_power[2] + bin_power[3])
-        total_row = jnp.full((1, wide), total, jnp.float32)
-        shares = [jnp.full((1, wide), bin_power[number], jnp.float32) / total_row for number in range(4)]
+        total_row = jnp.full((1, 128), total, jnp.float32)
+        shares = [
+            jnp.full((1, 128), bin_power[number], jnp.float32) / total_row for number in range(4)
+        ]
         scale = (1.0 / LENGTH) / total_row
 
-        def second_pass(index, parity):
-            columns = slice(index * wide, (index + 1) * wide)
-            return [
-                jnp.dot(
-                    fourth_ref[parity],
-                    turned[number, parity, :, columns],
-                    preferred_element_type=jnp.float32,
-                )
-                for number in range(4)
-            ]
-
-        def finish(index, parity, pieces):
-            real = [piece[:quarter] for piece in pieces]
-            imag = [piece[quarter:] for piece in pieces]
+        def second_pass(tile, parity):
+            product = jnp.dot(
+                fourth_ref[parity], turned[parity, tile], preferred_element_type=jnp.float32
+            ).reshape(quarter // 8, 2, 8, 4 * 128)
+            real, imag = (
+                [product[:, part, :, number * 128 : (number + 1) * 128] for number in range(4)]
+                for part in range(2)
+            )
             sum_real = (real[0] + real[1]) + (real[2] + real[3])
             sum_imag = (imag[0] + imag[1]) + (imag[2] + imag[3])
             snr = jnp.sqrt((sum_real * sum_real + sum_imag * sum_imag) * scale)
@@ -426,23 +432,19 @@
             inner = 0.5 + 0.5 * (reduced * reduced * reduced)
             weighted = snr * jnp.exp2(jnp.log2(inner) * (-1.0 / 6.0))
             newsnr = jnp.where(reduced > 1.0, weighted, snr)
-            for tile in range(wide // 128):
-                lanes = slice(tile * 128, (tile + 1) * 128)
-                start = parity * (SIDE // 128) + index * (wide // 128) + tile
-                rows = pl.ds(start, quarter, stride=2 * SIDE // 128)
-                series[0, rows, :] = snr[:, lanes]
-                series[1, rows, :] = chisq[:, lanes]
-            return jnp.max(newsnr, axis=0, keepdims=True)
-
-        peak = jnp.zeros((1, wide), jnp.float32)
-        steps = [(index, parity) for index in range(SIDE // wide) for parity in range(2)]
-        pieces = second_pass(*steps[0])
-        for place, step in enumerate(steps):
-            ahead = second_pass(*steps[place + 1]) if place + 1 < len(steps) else None
-            peak = jnp.maximum(peak, finish(*step, pieces))
-            pieces = ahead
-        for kind, out_ref in enumerate((snr_ref, chisq_ref)):
-            out_ref[0] = series[kind].reshape(1, LENGTH // 2).astype(jnp.bfloat16)
+            for kind, value in enumerate((snr, chisq)):
+                rows = value.reshape(quarter, 128)
+                for row in range(quarter):
+                    place = (row * 2 * (SIDE // 128) + parity * (SIDE // 128) + tile) * 128
+                    (snr_ref, chisq_ref)[kind][0, :, place : place + 128] = rows[
+                        row : row + 1
+                    ].astype(jnp.bfloat16)
+            return jnp.max(newsnr.reshape(quarter, 128), axis=0, keepdims=True)
+
+        peak = jnp.zeros((1, 128), jnp.float32)
+        for tile in range(SIDE // 128):
+            for parity in range(2):
+                peak = jnp.maximum(peak, second_pass(tile, parity))
         peak_ref[...] = jnp.max(peak, axis=1, keepdims=True)
 
     vmem = pl.BlockSpec(memory_space=pltpu.VMEM)
@@ -453,19 +455,18 @@
             jax.ShapeDtypeStruct((1, 1, LENGTH // 2), jnp.bfloat16),
             jax.ShapeDtypeStruct((1, 1), jnp.float32),
         ),
-        in_specs=[vmem] * (1 + n_blocks) + [pl.BlockSpec(memory_space=pltpu.SMEM)] + [vmem] * 3,
+        in_specs=[vmem] * (5 + n_blocks),
         out_specs=(vmem, vmem, vmem),
         scratch_shapes=[
             pltpu.VMEM((2, HALF, SIDE), jnp.bfloat16),
             pltpu.VMEM((SIDE, SIDE), jnp.bfloat16),
             pltpu.VMEM((4, SIDE, HALF), jnp.bfloat16),
-            pltpu.VMEM((4, 2, SIDE, SIDE), jnp.bfloat16),
+            pltpu.VMEM((2, SIDE // 128, SIDE, 4 * 128), jnp.bfloat16),
             pltpu.VMEM((4, 8, quarter), jnp.float32),
-            pltpu.VMEM((2, LENGTH // 256, 128), jnp.float32),
         ],
         compiler_params=pltpu.CompilerParams(vmem_limit_bytes=16 * MIB),
         name="inverse",
-    )(spectrum, *blocks, edges, *in_vmem(third, fourth, phase))
+    )(spectrum, *blocks, *in_vmem(edges, third, fourth, phase))
 
 
 def exchange(value, mesh_shape, mask_of):
@@ -515,14 +516,9 @@
         *outgoing, mine, unpacked = split_frames(strain_frames, templates)
         received = [
             exchange(value, mesh_shape, functools.partial(strain_mask, step))
-            for step, value in enumerate(outgoing[:3])
+            for step, value in enumerate(outgoing)
         ]
         pair = pair_shards(unpacked, across)
-        *late, pair = lax.optimization_barrier((*outgoing[3:], pair))
-        received += [
-            exchange(value, mesh_shape, functools.partial(strain_mask, step + 3))
-            for step, value in enumerate(late)
-        ]
         near = exchange(pair, mesh_shape, lambda core: 2 - core)
         first, second, third, fourth, phase, factors = constants
         first, factors = load_tables((first, factors), pair)

time: 31.3 us -> 28.8 us (0.920)
  Pallas kernels: 12.7 us -> 10.6 us
  starting transfers between devices: 14 us -> 12 us
  waiting for transfers between devices: 3.67 us -> 5.15 us
    ppermute x1, starting transfers between devices: 3.32 us -> 1.22 us  [local(): other = lax.ppermute(jnp.stack(received), 'template', [(0, 1), (1, 0)])]
    pallas_call x1, Pallas kernels: 7.37 us -> 5.3 us  [inverse(): pl.pallas_call(body, out_shape=(jax.ShapeDtypeStruct((1, 1, LENGTH // 2),...]
    ppermute x7, waiting for transfers between devices: 3.24 us -> 5.15 us  [exchange(): return lax.ppermute(value, AXES, pairs)]
    ppermute x1, waiting for transfers between devices: 0.42 us -> 0.01 us  [local(): other = lax.ppermute(jnp.stack(received), 'template', [(0, 1), (1, 0)])]
  transfers between devices with their start and end apart: 8 -> 8, of which waited for: 3 -> 4; matrix products, arithmetic and copies ran while one was open for 0% -> 0% of each run, Pallas kernels for 17% -> 19%
where the time goes in v4:
time: 28.8 us; the launch traced here: 28.6 us
  starting transfers between devices  12 us (42%)
  Pallas kernels  10.6 us (37%)
  waiting for transfers between devices  5.15 us (18%)
  between operations  0.76 us (3%)
    ppermute x7, starting transfers between devices, exchange(): return lax.ppermute(value, AXES, pairs)  10.8 us
    pallas_call x1, Pallas kernels, inverse(): pl.pallas_call(body, out_shape=(jax.ShapeDtypeStruct((1, 1, LENGTH // 2),...  5.3 us
    ppermute x7, waiting for transfers between devices, exchange(): return lax.ppermute(value, AXES, pairs)  5.15 us
    pallas_call x1, Pallas kernels, forward_received(): pl.pallas_call(body, out_shape=pltpu.VMEM((SIDE, SIDE), jnp.float32), in_...  2.35 us
    pallas_call x1, Pallas kernels, split_frames(): pl.pallas_call(body, out_shape=[pltpu.VMEM((2, rows, SIDE), jnp.bfloat16)...  1.6 us
    pallas_call x1, Pallas kernels, load_tables(): pl.pallas_call(body, out_shape=[pltpu.VMEM(x.shape, x.dtype) for x in arr...  1.26 us
    ppermute x1, starting transfers between devices, local(): other = lax.ppermute(jnp.stack(received), 'template', [(0, 1), (1, 0)])  1.22 us
  transfers between devices with their start and end apart: 8, of which 4 were waited for; matrix products, arithmetic and copies ran while one was open for 0% of the time, Pallas kernels for 19%

profile of v4, /device:TPU:0, one launch (start us, length us, event | category | flops | bytes accessed | tf_op | source)
XLA Modules:
  0.0 28.6 jit_solution(4963121265700354047)
XLA Ops:
  0.6 0.0 copy-start.5
  0.7 4.1 %collective-permute-start.4 = (bf16[1,2,16384]{2,1,0:T(2,128)(2,1)}, bf16[1,2,16384]{2,1,0:T(2,128)(2,1)S(1)}, u32[]{:S(2)}, u32[]{:S(2)}) collective-permute-start(bf16[1,2,16384]{2,1,0:T(2,128)(2,1)} %shard_hbm.1), channel_id=1, source_target_pairs={{0,8},{1,9},{2,10},{3,11},{4,12},{5,13},{6,14},{7,15},{8,0},{9,1},... | collective-permute-start | bytes 196616 | tf_op jit(solution)/shard_map/ppermute | solution.py:482
  4.8 1.6 %split_frames.1 = (bf16[2,32,512]{2,1,0:T(8,128)(2,1)S(1)}, bf16[2,32,512]{2,1,0:T(8,128)(2,1)S(1)}, bf16[2,32,512]{2,1,0:T(8,128)(2,1)S(1)}, bf16[2,32,512]{2,1...) custom-call(bf16[8,16384]{1,0:T(8,128)(2,1)} %frames_hbm.1, ...), custom_call_target="tpu_custom_call" | custom-call | tf_op jit(solution)/shard_map/split_frames/pallas_call | solution.py:118
  6.4 2.3 %collective-permute-start = (bf16[2,32,512]{2,1,0:T(8,128)(2,1)S(1)}, bf16[2,32,512]{2,1,0:T(8,128)(2,1)S(1)}, u32[]{:S(2)}, u32[]{:S(2)}) collective-permute-start(bf16[2,32,512]{2,1,0:T(8,128)(2,1)S(1)} %get-tuple-element.16), channel_id=1, source_target_pairs={{0,14},{1,7},{2,12},{3,5},{4,10},{5,3},{6,8},{7,1},{8,6},{9,15},{1... | collective-permute-start | bytes 196616 | tf_op jit(solution)/shard_map/ppermute | solution.py:482
  8.7 0.0 collective-permute-start.1
  8.7 0.9 %collective-permute-start.2 = (bf16[2,32,512]{2,1,0:T(8,128)(2,1)S(1)}, bf16[2,32,512]{2,1,0:T(8,128)(2,1)S(1)}, u32[]{:S(2)}, u32[]{:S(2)}) collective-permute-start(bf16[2,32,512]{2,1,0:T(8,128)(2,1)S(1)} %get-tuple-element.18), channel_id=1, source_target_pairs={{0,2},{1,11},{2,0},{3,9},{4,6},{5,15},{6,4},{7,13},{8,10},{9,3},{1... | collective-permute-start | bytes 196616 | tf_op jit(solution)/shard_map/ppermute | solution.py:482
  9.6 0.7 %collective-permute-start.3 = (bf16[2,32,512]{2,1,0:T(8,128)(2,1)S(1)}, bf16[2,32,512]{2,1,0:T(8,128)(2,1)S(1)}, u32[]{:S(2)}, u32[]{:S(2)}) collective-permute-start(bf16[2,32,512]{2,1,0:T(8,128)(2,1)S(1)} %get-tuple-element.19), channel_id=1, source_target_pairs={{1,9},{3,11},{5,13},{7,15},{9,1},{11,3},{13,5},{15,7},{17,25},{19,... | collective-permute-start | bytes 196616 | tf_op jit(solution)/shard_map/ppermute | solution.py:482
  10.2 0.0 collective-permute-done.4.across_ref
  10.2 0.1 pair_shards.1.refs_2_.refs_1_
  10.4 1.8 %collective-permute-start.6 = (bf16[2,2,32,512]{3,2,1,0:T(8,128)(2,1)S(1)}, bf16[2,2,32,512]{3,2,1,0:T(8,128)(2,1)S(1)}, u32[]{:S(2)}, u32[]{:S(2)}) collective-permute-start(bf16[2,2,32,512]{3,2,1,0:T(8,128)(2,1)S(1)} %pair_shards.1.refs_2_.refs_1_), channel_id=1, source_target_pairs={{0,4},{1,3},{2,6},{3,1},{4,0},{5,7},{6,2},{7,5},{8,12},{9,11},{10,... | collective-permute-start | bytes 393224 | tf_op jit(solution)/shard_map/ppermute | solution.py:482
  12.1 1.3 %load_tables.1 = (bf16[1024,512]{1,0:T(8,128)(2,1)S(1)}, f32[96,512]{1,0:T(8,128)S(1)}) custom-call(bf16[1024,512]{1,0:T(8,128)(2,1)} %constant.12.clone.refs_0_, f32[96,512]{1,0:T(8,128)} %constant.13.clone.refs_1_, bf16[2,2,32,512]{3,2,1,0:T(8,128)(2,1)S(1)} %pair_shards.1.refs_2_.refs_1_), custom_call_target="tpu_custom_call" | custom-call | bytes 4194304 | tf_op jit(solution)/shard_map/load_tables/pallas_call | solution.py:179
  13.4 0.8 %collective-permute-done.refs_0_ = bf16[2,32,512]{2,1,0:T(8,128)(2,1)S(1)} collective-permute-done((bf16[2,32,512]{2,1,0:T(8,128)(2,1)S(1)}, bf16[2,32,512]{2,1,0:T(8,128)(2,1)S(1)}, u32[]{:S(2)}, u32[]{:S(2)}) %collective-permute-start) | collective-permute-done | bytes 65568 | tf_op jit(solution)/shard_map/ppermute | solution.py:482
  14.2 0.4 %collective-permute-done.1.refs_1_ = bf16[2,32,512]{2,1,0:T(8,128)(2,1)S(1)} collective-permute-done((bf16[2,32,512]{2,1,0:T(8,128)(2,1)S(1)}, bf16[2,32,512]{2,1,0:T(8,128)(2,1)S(1)}, u32[]{:S(2)}, u32[]{:S(2)}) %collective-permute-start.1) | collective-permute-done | bytes 65568 | tf_op jit(solution)/shard_map/ppermute | solution.py:482
  14.7 1.2 %collective-permute-start.5 = (bf16[4,2,32,512]{3,2,1,0:T(8,128)(2,1)S(1)}, bf16[4,2,32,512]{3,2,1,0:T(8,128)(2,1)S(1)}, u32[]{:S(2)}, u32[]{:S(2)}) collective-permute-start(bf16[4,2,32,512]{3,2,1,0:T(8,128)(2,1)S(1)} %pad_maximum_fusion), channel_id=1, source_target_pairs={{0,1},{1,0},{2,3},{3,2},{4,5},{5,4},{6,7},{7,6},{8,9},{9,8},{10,11... | collective-permute-start | bytes 786440 | tf_op jit(solution)/shard_map/ppermute | solution.py:526
  15.9 0.8 %collective-permute-done.6.refs_2_ = bf16[2,2,32,512]{3,2,1,0:T(8,128)(2,1)S(1)} collective-permute-done((bf16[2,2,32,512]{3,2,1,0:T(8,128)(2,1)S(1)}, bf16[2,2,32,512]{3,2,1,0:T(8,128)(2,1)S(1)}, u32[]{:S(2)}, u32[]{:S(2)}) %collective-permute-start.6) | collective-permute-done | bytes 131104 | tf_op jit(solution)/shard_map/ppermute | solution.py:482
  16.8 0.0 copy-start
  16.8 0.0 copy-start.1
  16.8 0.0 copy-start.2
  16.8 0.0 copy-start.3
  16.8 1.0 %collective-permute-start.7 = (bf16[4,2,32,512]{3,2,1,0:T(8,128)(2,1)S(1)}, bf16[4,2,32,512]{3,2,1,0:T(8,128)(2,1)S(1)}, u32[]{:S(2)}, u32[]{:S(2)}) collective-permute-start(bf16[4,2,32,512]{3,2,1,0:T(8,128)(2,1)S(1)} %pad_maximum_fusion.1), channel_id=1, source_target_pairs={{0,2},{1,5},{2,0},{3,7},{4,6},{5,1},{6,4},{7,3},{8,10},{9,13},{10,... | collective-permute-start | bytes 786440 | tf_op jit(solution)/shard_map/ppermute | solution.py:482
  17.9 0.0 collective-permute-done.5.refs_4_
  17.9 2.3 %forward.1.refs_0_ = f32[512,512]{1,0:T(8,128)S(1)} custom-call(bf16[2,32,512]{2,1,0:T(8,128)(2,1)S(1)} %collective-permute-done.refs_0_, bf16[2,32,512]{2,1,0:T(8,128)(2,1)S(1)} %collective-permute-done.1.refs_1_, bf16[2,32,512]{2,1,0:T(8,128)(2,1)S(1)} %collective-permute-done.2.refs_2_, bf16[2,32,512]{2,1,0:T(8,128)(2,1)S(1)} %collective-permute-done.3.refs_3_, ...), custom_call_target="tpu_custom_call" | custom-call | flops 1073741824 | bytes 6291456 | tf_op jit(solution)/shard_map/forward/pallas_call | solution.py:246
  20.2 3.0 %collective-permute-done.7.refs_3_ = bf16[4,2,32,512]{3,2,1,0:T(8,128)(2,1)S(1)} collective-permute-done((bf16[4,2,32,512]{3,2,1,0:T(8,128)(2,1)S(1)}, bf16[4,2,32,512]{3,2,1,0:T(8,128)(2,1)S(1)}, u32[]{:S(2)}, u32[]{:S(2)}) %collective-permute-start.7) | collective-permute-done | bytes 262176 | tf_op jit(solution)/shard_map/ppermute | solution.py:482
  23.3 5.3 %inverse.1 = (bf16[1,1,131072]{2,1,0:T(2,128)(2,1)}, bf16[1,1,131072]{2,1,0:T(2,128)(2,1)}, f32[1,1]{1,0:T(1,128)}) custom-call(f32[512,512]{1,0:T(8,128)S(1)} %forward.1.refs_0_, bf16[2,2,32,512]{3,2,1,0:T(8,128)(2,1)S(1)} %pair_shards.1.refs_2_.refs_1_, bf16[2,2,32,512]{3,2,1,0:T(8,128)(2,1)S(1)} %collective-permute-done.6.refs_2_, ...), custom_call_target="tpu_custom_call" | custom-call | tf_op jit(solution)/shard_map/inverse/pallas_call | solution.py:451
  (11 shorter events, 0.1 us)
Async XLA Ops:
  0.6 17.3 %copy-start.5 = (bf16[1024,512]{1,0:T(8,128)(2,1)S(1)}, bf16[1024,512]{1,0:T(8,128)(2,1)}, u32[]{:S(2)}) copy-start(bf16[1024,512]{1,0:T(8,128)(2,1)} %constant.14.clone.refs_8_) | copy-start | bytes 3145732
  0.6 17.2 %copy-start.4 = (s32[8,8]{1,0:T(8,128)S(1)}, s32[8,8]{1,0:T(8,128)}, u32[]{:S(2)}) copy-start(s32[8,8]{1,0:T(8,128)} %refs_6_.2) | copy-start | bytes 772
  0.7 9.6 %collective-permute-start.4 = (bf16[1,2,16384]{2,1,0:T(2,128)(2,1)}, bf16[1,2,16384]{2,1,0:T(2,128)(2,1)S(1)}, u32[]{:S(2)}, u32[]{:S(2)}) collective-permute-start(bf16[1,2,16384]{2,1,0:T(2,128)(2,1)} %shard_hbm.1), channel_id=1, source_target_pairs={{0,8},{1,9},{2,10},{3,11},{4,12},{5,13},{6,14},{7,15},{8,0},{9,1},... | collective-permute-start | bytes 196616 | tf_op jit(solution)/shard_map/ppermute | solution.py:482
  6.4 7.8 %collective-permute-start = (bf16[2,32,512]{2,1,0:T(8,128)(2,1)S(1)}, bf16[2,32,512]{2,1,0:T(8,128)(2,1)S(1)}, u32[]{:S(2)}, u32[]{:S(2)}) collective-permute-start(bf16[2,32,512]{2,1,0:T(8,128)(2,1)S(1)} %get-tuple-element.16), channel_id=1, source_target_pairs={{0,14},{1,7},{2,12},{3,5},{4,10},{5,3},{6,8},{7,1},{8,6},{9,15},{1... | collective-permute-start | bytes 196616 | tf_op jit(solution)/shard_map/ppermute | solution.py:482
  8.7 5.9 %collective-permute-start.1 = (bf16[2,32,512]{2,1,0:T(8,128)(2,1)S(1)}, bf16[2,32,512]{2,1,0:T(8,128)(2,1)S(1)}, u32[]{:S(2)}, u32[]{:S(2)}) collective-permute-start(bf16[2,32,512]{2,1,0:T(8,128)(2,1)S(1)} %get-tuple-element.17), channel_id=1, source_target_pairs={{0,4},{1,13},{2,6},{3,15},{4,0},{5,9},{6,2},{7,11},{8,12},{9,5},{1... | collective-permute-start | bytes 196616 | tf_op jit(solution)/shard_map/ppermute | solution.py:482
  8.7 5.9 %collective-permute-start.2 = (bf16[2,32,512]{2,1,0:T(8,128)(2,1)S(1)}, bf16[2,32,512]{2,1,0:T(8,128)(2,1)S(1)}, u32[]{:S(2)}, u32[]{:S(2)}) collective-permute-start(bf16[2,32,512]{2,1,0:T(8,128)(2,1)S(1)} %get-tuple-element.18), channel_id=1, source_target_pairs={{0,2},{1,11},{2,0},{3,9},{4,6},{5,15},{6,4},{7,13},{8,10},{9,3},{1... | collective-permute-start | bytes 196616 | tf_op jit(solution)/shard_map/ppermute | solution.py:482
  9.6 5.1 %collective-permute-start.3 = (bf16[2,32,512]{2,1,0:T(8,128)(2,1)S(1)}, bf16[2,32,512]{2,1,0:T(8,128)(2,1)S(1)}, u32[]{:S(2)}, u32[]{:S(2)}) collective-permute-start(bf16[2,32,512]{2,1,0:T(8,128)(2,1)S(1)} %get-tuple-element.19), channel_id=1, source_target_pairs={{1,9},{3,11},{5,13},{7,15},{9,1},{11,3},{13,5},{15,7},{17,25},{19,... | collective-permute-start | bytes 196616 | tf_op jit(solution)/shard_map/ppermute | solution.py:482
  10.4 6.4 %collective-permute-start.6 = (bf16[2,2,32,512]{3,2,1,0:T(8,128)(2,1)S(1)}, bf16[2,2,32,512]{3,2,1,0:T(8,128)(2,1)S(1)}, u32[]{:S(2)}, u32[]{:S(2)}) collective-permute-start(bf16[2,2,32,512]{3,2,1,0:T(8,128)(2,1)S(1)} %pair_shards.1.refs_2_.refs_1_), channel_id=1, source_target_pairs={{0,4},{1,3},{2,6},{3,1},{4,0},{5,7},{6,2},{7,5},{8,12},{9,11},{10,... | collective-permute-start | bytes 393224 | tf_op jit(solution)/shard_map/ppermute | solution.py:482
  14.7 3.2 %collective-permute-start.5 = (bf16[4,2,32,512]{3,2,1,0:T(8,128)(2,1)S(1)}, bf16[4,2,32,512]{3,2,1,0:T(8,128)(2,1)S(1)}, u32[]{:S(2)}, u32[]{:S(2)}) collective-permute-start(bf16[4,2,32,512]{3,2,1,0:T(8,128)(2,1)S(1)} %pad_maximum_fusion), channel_id=1, source_target_pairs={{0,1},{1,0},{2,3},{3,2},{4,5},{5,4},{6,7},{7,6},{8,9},{9,8},{10,11... | collective-permute-start | bytes 786440 | tf_op jit(solution)/shard_map/ppermute | solution.py:526
  16.8 6.5 %copy-start = (bf16[4,256,1024]{2,1,0:T(8,128)(2,1)S(1)}, bf16[4,256,1024]{2,1,0:T(8,128)(2,1)}, u32[]{:S(2)}) copy-start(bf16[4,256,1024]{2,1,0:T(8,128)(2,1)} %constant.15.clone.refs_5_) | copy-start | bytes 6291460
  16.8 6.5 %copy-start.1 = (bf16[2,512,512]{2,1,0:T(8,128)(2,1)S(1)}, bf16[2,512,512]{2,1,0:T(8,128)(2,1)}, u32[]{:S(2)}) copy-start(bf16[2,512,512]{2,1,0:T(8,128)(2,1)} %constant.17.clone.refs_7_) | copy-start | bytes 3145732
  16.8 6.5 %copy-start.2 = (bf16[2,256,512]{2,1,0:T(8,128)(2,1)S(1)}, bf16[2,256,512]{2,1,0:T(8,128)(2,1)}, u32[]{:S(2)}) copy-start(bf16[2,256,512]{2,1,0:T(8,128)(2,1)} %constant.16.clone.refs_6_) | copy-start | bytes 1572868
  16.8 6.5 %copy-start.3 = (s32[1,3]{1,0:T(1,128)S(1)}, s32[1,3]{1,0:T(1,128)}, u32[]{:S(2)}) copy-start(s32[1,3]{1,0:T(1,128)} %refs_4_.1) | copy-start | bytes 40
  16.8 6.4 %collective-permute-start.7 = (bf16[4,2,32,512]{3,2,1,0:T(8,128)(2,1)S(1)}, bf16[4,2,32,512]{3,2,1,0:T(8,128)(2,1)S(1)}, u32[]{:S(2)}, u32[]{:S(2)}) collective-permute-start(bf16[4,2,32,512]{3,2,1,0:T(8,128)(2,1)S(1)} %pad_maximum_fusion.1), channel_id=1, source_target_pairs={{0,2},{1,5},{2,0},{3,7},{4,6},{5,1},{6,4},{7,3},{8,10},{9,13},{10,... | collective-permute-start | bytes 786440 | tf_op jit(solution)/shard_map/ppermute | solution.py:482

commit v5 on v4

--- a/solution.py
+++ b/solution.py
@@ -15,6 +15,7 @@
 LENGTH = SIDE * SIDE
 AXES = ("groups", "segment", "template")
 MIB = 1 << 20
+TINY = float(np.finfo(np.float32).tiny)
 STEP = 16
 BIN_LOW = (0, 32, 96, 128)
 ROUNDS = 4
@@ -183,7 +184,6 @@
         out_specs=[pl.BlockSpec(memory_space=pltpu.VMEM)] * count,
         scratch_shapes=[pltpu.SemaphoreType.DMA((count,))],
         compiler_params=pltpu.CompilerParams(vmem_limit_bytes=1 * MIB),
-        cost_estimate=pl.CostEstimate(flops=0, bytes_accessed=4 * MIB, transcendentals=0),
         name="load_tables",
     )(*in_hbm(*arrays), after)
 
@@ -279,7 +279,7 @@
 def owners_of(segment, core, doubled):
     if not doubled:
         return [[0]]
-    near, far = 2 - core, 1 + core
+    near, far = 1 + core, 2 - core
     masks = [[0, 4], [near, near ^ 4], [far, far ^ 4, far ^ near, far ^ near ^ 4]]
     return [[segment ^ mask for mask in block] for block in masks]
 
@@ -420,7 +420,8 @@
             )
             sum_real = (real[0] + real[1]) + (real[2] + real[3])
             sum_imag = (imag[0] + imag[1]) + (imag[2] + imag[3])
-            snr = jnp.sqrt((sum_real * sum_real + sum_imag * sum_imag) * scale)
+            square = (sum_real * sum_real + sum_imag * sum_imag) * scale
+            snr = square * lax.rsqrt(jnp.maximum(square, TINY))
             chisq = None
             for number in range(4):
                 diff_real = real[number] - shares[number] * sum_real
@@ -429,9 +430,9 @@
                 chisq = term if chisq is None else chisq + term
             chisq = chisq * scale
             reduced = chisq * (1.0 / 6.0)
+            reduced = jnp.maximum(reduced, 1.0)
             inner = 0.5 + 0.5 * (reduced * reduced * reduced)
-            weighted = snr * jnp.exp2(jnp.log2(inner) * (-1.0 / 6.0))
-            newsnr = jnp.where(reduced > 1.0, weighted, snr)
+            newsnr = snr * jnp.exp2(jnp.log2(inner) * (-1.0 / 6.0))
             for kind, value in enumerate((snr, chisq)):
                 rows = value.reshape(quarter, 128)
                 for row in range(quarter):
@@ -519,12 +520,12 @@
             for step, value in enumerate(outgoing)
         ]
         pair = pair_shards(unpacked, across)
-        near = exchange(pair, mesh_shape, lambda core: 2 - core)
+        near = exchange(pair, mesh_shape, lambda core: 1 + core)
         first, second, third, fourth, phase, factors = constants
         first, factors = load_tables((first, factors), pair)
         *received, first = lax.optimization_barrier((*received, first))
         other = lax.ppermute(jnp.stack(received), "template", [(0, 1), (1, 0)])
-        far = exchange(jnp.concatenate([pair, near]), mesh_shape, lambda core: 1 + core)
+        far = exchange(jnp.concatenate([pair, near]), mesh_shape, lambda core: 2 - core)
         blocks = [pair, near, far]
         spectrum = forward_received(received, other, mine, frame_slot, first, second, factors)
     else:

time: 28.8 us -> 28.1 us (0.976)
  waiting for transfers between devices: 5.15 us -> 4.22 us
  starting transfers between devices: 12 us -> 12.3 us
    ppermute x7, waiting for transfers between devices: 5.15 us -> 4.22 us  [exchange(): return lax.ppermute(value, AXES, pairs)]
    ppermute x7, starting transfers between devices: 10.8 us -> 11.1 us  [exchange(): return lax.ppermute(value, AXES, pairs)]
where the time goes in v5:
time: 28.1 us; the launch traced here: 27.9 us
  starting transfers between devices  12.3 us (44%)
  Pallas kernels  10.5 us (37%)
  waiting for transfers between devices  4.22 us (15%)
  between operations  0.76 us (3%)
    ppermute x7, starting transfers between devices, exchange(): return lax.ppermute(value, AXES, pairs)  11.1 us
    pallas_call x1, Pallas kernels, inverse(): pl.pallas_call(body, out_shape=(jax.ShapeDtypeStruct((1, 1, LENGTH // 2),...  5.19 us
    ppermute x7, waiting for transfers between devices, exchange(): return lax.ppermute(value, AXES, pairs)  4.22 us
    pallas_call x1, Pallas kernels, forward_received(): pl.pallas_call(body, out_shape=pltpu.VMEM((SIDE, SIDE), jnp.float32), in_...  2.35 us
    pallas_call x1, Pallas kernels, split_frames(): pl.pallas_call(body, out_shape=[pltpu.VMEM((2, rows, SIDE), jnp.bfloat16)...  1.6 us
    pallas_call x1, Pallas kernels, load_tables(): pl.pallas_call(body, out_shape=[pltpu.VMEM(x.shape, x.dtype) for x in arr...  1.26 us
    ppermute x1, starting transfers between devices, local(): other = lax.ppermute(jnp.stack(received), 'template', [(0, 1), (1, 0)])  1.22 us
  transfers between devices with their start and end apart: 8, of which 4 were waited for; matrix products, arithmetic and copies ran while one was open for 0% of the time, Pallas kernels for 19%

profile of v5, /device:TPU:0, one launch (start us, length us, event | category | flops | bytes accessed | tf_op | source)
XLA Modules:
  0.0 27.9 jit_solution(11997322813523159710)
XLA Ops:
  0.6 0.0 copy-start.5
  0.7 4.1 %collective-permute-start.4 = (bf16[1,2,16384]{2,1,0:T(2,128)(2,1)}, bf16[1,2,16384]{2,1,0:T(2,128)(2,1)S(1)}, u32[]{:S(2)}, u32[]{:S(2)}) collective-permute-start(bf16[1,2,16384]{2,1,0:T(2,128)(2,1)} %shard_hbm.1), channel_id=1, source_target_pairs={{0,8},{1,9},{2,10},{3,11},{4,12},{5,13},{6,14},{7,15},{8,0},{9,1},... | collective-permute-start | bytes 196616 | tf_op jit(solution)/shard_map/ppermute | solution.py:483
  4.8 1.6 %split_frames.1 = (bf16[2,32,512]{2,1,0:T(8,128)(2,1)S(1)}, bf16[2,32,512]{2,1,0:T(8,128)(2,1)S(1)}, bf16[2,32,512]{2,1,0:T(8,128)(2,1)S(1)}, bf16[2,32,512]{2,1...) custom-call(bf16[8,16384]{1,0:T(8,128)(2,1)} %frames_hbm.1, ...), custom_call_target="tpu_custom_call" | custom-call | tf_op jit(solution)/shard_map/split_frames/pallas_call | solution.py:119
  6.4 2.3 %collective-permute-start = (bf16[2,32,512]{2,1,0:T(8,128)(2,1)S(1)}, bf16[2,32,512]{2,1,0:T(8,128)(2,1)S(1)}, u32[]{:S(2)}, u32[]{:S(2)}) collective-permute-start(bf16[2,32,512]{2,1,0:T(8,128)(2,1)S(1)} %get-tuple-element.16), channel_id=1, source_target_pairs={{0,14},{1,7},{2,12},{3,5},{4,10},{5,3},{6,8},{7,1},{8,6},{9,15},{1... | collective-permute-start | bytes 196616 | tf_op jit(solution)/shard_map/ppermute | solution.py:483
  8.7 0.0 collective-permute-start.1
  8.7 0.9 %collective-permute-start.2 = (bf16[2,32,512]{2,1,0:T(8,128)(2,1)S(1)}, bf16[2,32,512]{2,1,0:T(8,128)(2,1)S(1)}, u32[]{:S(2)}, u32[]{:S(2)}) collective-permute-start(bf16[2,32,512]{2,1,0:T(8,128)(2,1)S(1)} %get-tuple-element.18), channel_id=1, source_target_pairs={{0,2},{1,11},{2,0},{3,9},{4,6},{5,15},{6,4},{7,13},{8,10},{9,3},{1... | collective-permute-start | bytes 196616 | tf_op jit(solution)/shard_map/ppermute | solution.py:483
  9.6 0.7 %collective-permute-start.3 = (bf16[2,32,512]{2,1,0:T(8,128)(2,1)S(1)}, bf16[2,32,512]{2,1,0:T(8,128)(2,1)S(1)}, u32[]{:S(2)}, u32[]{:S(2)}) collective-permute-start(bf16[2,32,512]{2,1,0:T(8,128)(2,1)S(1)} %get-tuple-element.19), channel_id=1, source_target_pairs={{1,9},{3,11},{5,13},{7,15},{9,1},{11,3},{13,5},{15,7},{17,25},{19,... | collective-permute-start | bytes 196616 | tf_op jit(solution)/shard_map/ppermute | solution.py:483
  10.2 0.1 pair_shards.1.refs_2_.refs_1_
  10.4 1.2 %collective-permute-start.6 = (bf16[2,2,32,512]{3,2,1,0:T(8,128)(2,1)S(1)}, bf16[2,2,32,512]{3,2,1,0:T(8,128)(2,1)S(1)}, u32[]{:S(2)}, u32[]{:S(2)}) collective-permute-start(bf16[2,2,32,512]{3,2,1,0:T(8,128)(2,1)S(1)} %pair_shards.1.refs_2_.refs_1_), channel_id=1, source_target_pairs={{0,2},{1,5},{2,0},{3,7},{4,6},{5,1},{6,4},{7,3},{8,10},{9,13},{10,... | collective-permute-start | bytes 393224 | tf_op jit(solution)/shard_map/ppermute | solution.py:483
  11.6 1.3 %load_tables.1 = (bf16[1024,512]{1,0:T(8,128)(2,1)S(1)}, f32[96,512]{1,0:T(8,128)S(1)}) custom-call(bf16[1024,512]{1,0:T(8,128)(2,1)} %constant.12.clone.refs_0_, f32[96,512]{1,0:T(8,128)} %constant.13.clone.refs_1_, bf16[2,2,32,512]{3,2,1,0:T(8,128)(2,1)S(1)} %pair_shards.1.refs_2_.refs_1_), custom_call_target="tpu_custom_call" | custom-call | tf_op jit(solution)/shard_map/load_tables/pallas_call | solution.py:180
  12.8 1.4 %collective-permute-done.refs_0_ = bf16[2,32,512]{2,1,0:T(8,128)(2,1)S(1)} collective-permute-done((bf16[2,32,512]{2,1,0:T(8,128)(2,1)S(1)}, bf16[2,32,512]{2,1,0:T(8,128)(2,1)S(1)}, u32[]{:S(2)}, u32[]{:S(2)}) %collective-permute-start) | collective-permute-done | bytes 65568 | tf_op jit(solution)/shard_map/ppermute | solution.py:483
  14.2 0.4 %collective-permute-done.1.refs_1_ = bf16[2,32,512]{2,1,0:T(8,128)(2,1)S(1)} collective-permute-done((bf16[2,32,512]{2,1,0:T(8,128)(2,1)S(1)}, bf16[2,32,512]{2,1,0:T(8,128)(2,1)S(1)}, u32[]{:S(2)}, u32[]{:S(2)}) %collective-permute-start.1) | collective-permute-done | bytes 65568 | tf_op jit(solution)/shard_map/ppermute | solution.py:483
  14.7 0.0 collective-permute-done.2.refs_2_
  14.7 0.0 collective-permute-done.3.refs_3_
  14.7 1.2 %collective-permute-start.5 = (bf16[4,2,32,512]{3,2,1,0:T(8,128)(2,1)S(1)}, bf16[4,2,32,512]{3,2,1,0:T(8,128)(2,1)S(1)}, u32[]{:S(2)}, u32[]{:S(2)}) collective-permute-start(bf16[4,2,32,512]{3,2,1,0:T(8,128)(2,1)S(1)} %pad_maximum_fusion), channel_id=1, source_target_pairs={{0,1},{1,0},{2,3},{3,2},{4,5},{5,4},{6,7},{7,6},{8,9},{9,8},{10,11... | collective-permute-start | bytes 786440 | tf_op jit(solution)/shard_map/ppermute | solution.py:527
  15.9 0.2 collective-permute-done.6.refs_2_
  16.2 0.0 copy-start
  16.2 0.0 copy-start.1
  16.2 0.0 copy-start.2
  16.2 0.0 copy-start.3
  16.2 1.9 %collective-permute-start.7 = (bf16[4,2,32,512]{3,2,1,0:T(8,128)(2,1)S(1)}, bf16[4,2,32,512]{3,2,1,0:T(8,128)(2,1)S(1)}, u32[]{:S(2)}, u32[]{:S(2)}) collective-permute-start(bf16[4,2,32,512]{3,2,1,0:T(8,128)(2,1)S(1)} %pad_maximum_fusion.1), channel_id=1, source_target_pairs={{0,4},{1,3},{2,6},{3,1},{4,0},{5,7},{6,2},{7,5},{8,12},{9,11},{10,... | collective-permute-start | bytes 786440 | tf_op jit(solution)/shard_map/ppermute | solution.py:483
  18.2 2.4 %forward.1.refs_0_ = f32[512,512]{1,0:T(8,128)S(1)} custom-call(bf16[2,32,512]{2,1,0:T(8,128)(2,1)S(1)} %collective-permute-done.refs_0_, bf16[2,32,512]{2,1,0:T(8,128)(2,1)S(1)} %collective-permute-done.1.refs_1_, bf16[2,32,512]{2,1,0:T(8,128)(2,1)S(1)} %collective-permute-done.2.refs_2_, bf16[2,32,512]{2,1,0:T(8,128)(2,1)S(1)} %collective-permute-done.3.refs_3_, ...), custom_call_target="tpu_custom_call" | custom-call | flops 1073741824 | bytes 6291456 | tf_op jit(solution)/shard_map/forward/pallas_call | solution.py:246
  20.5 2.2 %collective-permute-done.7.refs_3_ = bf16[4,2,32,512]{3,2,1,0:T(8,128)(2,1)S(1)} collective-permute-done((bf16[4,2,32,512]{3,2,1,0:T(8,128)(2,1)S(1)}, bf16[4,2,32,512]{3,2,1,0:T(8,128)(2,1)S(1)}, u32[]{:S(2)}, u32[]{:S(2)}) %collective-permute-start.7) | collective-permute-done | bytes 262176 | tf_op jit(solution)/shard_map/ppermute | solution.py:483
  22.7 5.2 %inverse.1 = (bf16[1,1,131072]{2,1,0:T(2,128)(2,1)}, bf16[1,1,131072]{2,1,0:T(2,128)(2,1)}, f32[1,1]{1,0:T(1,128)}) custom-call(f32[512,512]{1,0:T(8,128)S(1)} %forward.1.refs_0_, bf16[2,2,32,512]{3,2,1,0:T(8,128)(2,1)S(1)} %pair_shards.1.refs_2_.refs_1_, bf16[2,2,32,512]{3,2,1,0:T(8,128)(2,1)S(1)} %collective-permute-done.6.refs_2_, ...), custom_call_target="tpu_custom_call" | custom-call | tf_op jit(solution)/shard_map/inverse/pallas_call | solution.py:452
  (11 shorter events, 0.1 us)
Async XLA Ops:
  0.6 17.5 %copy-start.5 = (bf16[1024,512]{1,0:T(8,128)(2,1)S(1)}, bf16[1024,512]{1,0:T(8,128)(2,1)}, u32[]{:S(2)}) copy-start(bf16[1024,512]{1,0:T(8,128)(2,1)} %constant.14.clone.refs_8_) | copy-start | bytes 3145732
  0.6 17.5 %copy-start.4 = (s32[8,8]{1,0:T(8,128)S(1)}, s32[8,8]{1,0:T(8,128)}, u32[]{:S(2)}) copy-start(s32[8,8]{1,0:T(8,128)} %refs_6_.2) | copy-start | bytes 772
  0.7 9.6 %collective-permute-start.4 = (bf16[1,2,16384]{2,1,0:T(2,128)(2,1)}, bf16[1,2,16384]{2,1,0:T(2,128)(2,1)S(1)}, u32[]{:S(2)}, u32[]{:S(2)}) collective-permute-start(bf16[1,2,16384]{2,1,0:T(2,128)(2,1)} %shard_hbm.1), channel_id=1, source_target_pairs={{0,8},{1,9},{2,10},{3,11},{4,12},{5,13},{6,14},{7,15},{8,0},{9,1},... | collective-permute-start | bytes 196616 | tf_op jit(solution)/shard_map/ppermute | solution.py:483
  6.4 7.8 %collective-permute-start = (bf16[2,32,512]{2,1,0:T(8,128)(2,1)S(1)}, bf16[2,32,512]{2,1,0:T(8,128)(2,1)S(1)}, u32[]{:S(2)}, u32[]{:S(2)}) collective-permute-start(bf16[2,32,512]{2,1,0:T(8,128)(2,1)S(1)} %get-tuple-element.16), channel_id=1, source_target_pairs={{0,14},{1,7},{2,12},{3,5},{4,10},{5,3},{6,8},{7,1},{8,6},{9,15},{1... | collective-permute-start | bytes 196616 | tf_op jit(solution)/shard_map/ppermute | solution.py:483
  8.7 5.9 %collective-permute-start.1 = (bf16[2,32,512]{2,1,0:T(8,128)(2,1)S(1)}, bf16[2,32,512]{2,1,0:T(8,128)(2,1)S(1)}, u32[]{:S(2)}, u32[]{:S(2)}) collective-permute-start(bf16[2,32,512]{2,1,0:T(8,128)(2,1)S(1)} %get-tuple-element.17), channel_id=1, source_target_pairs={{0,4},{1,13},{2,6},{3,15},{4,0},{5,9},{6,2},{7,11},{8,12},{9,5},{1... | collective-permute-start | bytes 196616 | tf_op jit(solution)/shard_map/ppermute | solution.py:483
  8.7 5.9 %collective-permute-start.2 = (bf16[2,32,512]{2,1,0:T(8,128)(2,1)S(1)}, bf16[2,32,512]{2,1,0:T(8,128)(2,1)S(1)}, u32[]{:S(2)}, u32[]{:S(2)}) collective-permute-start(bf16[2,32,512]{2,1,0:T(8,128)(2,1)S(1)} %get-tuple-element.18), channel_id=1, source_target_pairs={{0,2},{1,11},{2,0},{3,9},{4,6},{5,15},{6,4},{7,13},{8,10},{9,3},{1... | collective-permute-start | bytes 196616 | tf_op jit(solution)/shard_map/ppermute | solution.py:483
  9.6 5.1 %collective-permute-start.3 = (bf16[2,32,512]{2,1,0:T(8,128)(2,1)S(1)}, bf16[2,32,512]{2,1,0:T(8,128)(2,1)S(1)}, u32[]{:S(2)}, u32[]{:S(2)}) collective-permute-start(bf16[2,32,512]{2,1,0:T(8,128)(2,1)S(1)} %get-tuple-element.19), channel_id=1, source_target_pairs={{1,9},{3,11},{5,13},{7,15},{9,1},{11,3},{13,5},{15,7},{17,25},{19,... | collective-permute-start | bytes 196616 | tf_op jit(solution)/shard_map/ppermute | solution.py:483
  10.4 5.8 %collective-permute-start.6 = (bf16[2,2,32,512]{3,2,1,0:T(8,128)(2,1)S(1)}, bf16[2,2,32,512]{3,2,1,0:T(8,128)(2,1)S(1)}, u32[]{:S(2)}, u32[]{:S(2)}) collective-permute-start(bf16[2,2,32,512]{3,2,1,0:T(8,128)(2,1)S(1)} %pair_shards.1.refs_2_.refs_1_), channel_id=1, source_target_pairs={{0,2},{1,5},{2,0},{3,7},{4,6},{5,1},{6,4},{7,3},{8,10},{9,13},{10,... | collective-permute-start | bytes 393224 | tf_op jit(solution)/shard_map/ppermute | solution.py:483
  14.7 3.5 %collective-permute-start.5 = (bf16[4,2,32,512]{3,2,1,0:T(8,128)(2,1)S(1)}, bf16[4,2,32,512]{3,2,1,0:T(8,128)(2,1)S(1)}, u32[]{:S(2)}, u32[]{:S(2)}) collective-permute-start(bf16[4,2,32,512]{3,2,1,0:T(8,128)(2,1)S(1)} %pad_maximum_fusion), channel_id=1, source_target_pairs={{0,1},{1,0},{2,3},{3,2},{4,5},{5,4},{6,7},{7,6},{8,9},{9,8},{10,11... | collective-permute-start | bytes 786440 | tf_op jit(solution)/shard_map/ppermute | solution.py:527
  16.2 6.5 %copy-start = (bf16[4,256,1024]{2,1,0:T(8,128)(2,1)S(1)}, bf16[4,256,1024]{2,1,0:T(8,128)(2,1)}, u32[]{:S(2)}) copy-start(bf16[4,256,1024]{2,1,0:T(8,128)(2,1)} %constant.15.clone.refs_5_) | copy-start | bytes 6291460
  16.2 6.5 %copy-start.1 = (bf16[2,512,512]{2,1,0:T(8,128)(2,1)S(1)}, bf16[2,512,512]{2,1,0:T(8,128)(2,1)}, u32[]{:S(2)}) copy-start(bf16[2,512,512]{2,1,0:T(8,128)(2,1)} %constant.17.clone.refs_7_) | copy-start | bytes 3145732
  16.2 6.5 %copy-start.2 = (bf16[2,256,512]{2,1,0:T(8,128)(2,1)S(1)}, bf16[2,256,512]{2,1,0:T(8,128)(2,1)}, u32[]{:S(2)}) copy-start(bf16[2,256,512]{2,1,0:T(8,128)(2,1)} %constant.16.clone.refs_6_) | copy-start | bytes 1572868
  16.2 6.5 %copy-start.3 = (s32[1,3]{1,0:T(1,128)S(1)}, s32[1,3]{1,0:T(1,128)}, u32[]{:S(2)}) copy-start(s32[1,3]{1,0:T(1,128)} %refs_4_.1) | copy-start | bytes 40
  16.2 6.4 %collective-permute-start.7 = (bf16[4,2,32,512]{3,2,1,0:T(8,128)(2,1)S(1)}, bf16[4,2,32,512]{3,2,1,0:T(8,128)(2,1)S(1)}, u32[]{:S(2)}, u32[]{:S(2)}) collective-permute-start(bf16[4,2,32,512]{3,2,1,0:T(8,128)(2,1)S(1)} %pad_maximum_fusion.1), channel_id=1, source_target_pairs={{0,4},{1,3},{2,6},{3,1},{4,0},{5,7},{6,2},{7,5},{8,12},{9,11},{10,... | collective-permute-start | bytes 786440 | tf_op jit(solution)/shard_map/ppermute | solution.py:483

commit v6 on v5

--- a/solution.py
+++ b/solution.py
@@ -476,10 +476,9 @@
     for group in range(groups):
         for segment in range(segments):
             for core in range(cores):
-                if mask_of(core):
-                    here = (group * segments + segment) * cores + core
-                    other = segment ^ mask_of(core)
-                    pairs.append((here, (group * segments + other) * cores + core))
+                here = (group * segments + segment) * cores + core
+                other = segment ^ mask_of(core)
+                pairs.append((here, (group * segments + other) * cores + core))
     return lax.ppermute(value, AXES, pairs)
 
 

time: 28.1 us -> 28.1 us (level)
  no operation moved by 1% of the time
where the time goes in v6:
time: 28.1 us; the launch traced here: 27.9 us
  starting transfers between devices  12.3 us (44%)
  Pallas kernels  10.5 us (37%)
  waiting for transfers between devices  4.22 us (15%)
  between operations  0.76 us (3%)
    ppermute x7, starting transfers between devices, exchange(): return lax.ppermute(value, AXES, pairs)  11.1 us
    pallas_call x1, Pallas kernels, inverse(): pl.pallas_call(body, out_shape=(jax.ShapeDtypeStruct((1, 1, LENGTH // 2),...  5.19 us
    ppermute x7, waiting for transfers between devices, exchange(): return lax.ppermute(value, AXES, pairs)  4.22 us
    pallas_call x1, Pallas kernels, forward_received(): pl.pallas_call(body, out_shape=pltpu.VMEM((SIDE, SIDE), jnp.float32), in_...  2.34 us
    pallas_call x1, Pallas kernels, split_frames(): pl.pallas_call(body, out_shape=[pltpu.VMEM((2, rows, SIDE), jnp.bfloat16)...  1.6 us
    pallas_call x1, Pallas kernels, load_tables(): pl.pallas_call(body, out_shape=[pltpu.VMEM(x.shape, x.dtype) for x in arr...  1.26 us
    ppermute x1, starting transfers between devices, local(): other = lax.ppermute(jnp.stack(received), 'template', [(0, 1), (1, 0)])  1.22 us
  transfers between devices with their start and end apart: 8, of which 4 were waited for; matrix products, arithmetic and copies ran while one was open for 0% of the time, Pallas kernels for 19%

profile of v6, /device:TPU:0, one launch (start us, length us, event | category | flops | bytes accessed | tf_op | source)
XLA Modules:
  0.0 27.9 jit_solution(13394095582028917294)
XLA Ops:
  0.6 0.0 copy-start.5
  0.7 4.1 %collective-permute-start.4 = (bf16[1,2,16384]{2,1,0:T(2,128)(2,1)}, bf16[1,2,16384]{2,1,0:T(2,128)(2,1)S(1)}, u32[]{:S(2)}, u32[]{:S(2)}) collective-permute-start(bf16[1,2,16384]{2,1,0:T(2,128)(2,1)} %shard_hbm.1), channel_id=1, source_target_pairs={{0,8},{1,9},{2,10},{3,11},{4,12},{5,13},{6,14},{7,15},{8,0},{9,1},... | collective-permute-start | bytes 196616 | tf_op jit(solution)/shard_map/ppermute | solution.py:482
  4.8 1.6 %split_frames.1 = (bf16[2,32,512]{2,1,0:T(8,128)(2,1)S(1)}, bf16[2,32,512]{2,1,0:T(8,128)(2,1)S(1)}, bf16[2,32,512]{2,1,0:T(8,128)(2,1)S(1)}, bf16[2,32,512]{2,1...) custom-call(bf16[8,16384]{1,0:T(8,128)(2,1)} %frames_hbm.1, ...), custom_call_target="tpu_custom_call" | custom-call | tf_op jit(solution)/shard_map/split_frames/pallas_call | solution.py:119
  6.4 2.3 %collective-permute-start = (bf16[2,32,512]{2,1,0:T(8,128)(2,1)S(1)}, bf16[2,32,512]{2,1,0:T(8,128)(2,1)S(1)}, u32[]{:S(2)}, u32[]{:S(2)}) collective-permute-start(bf16[2,32,512]{2,1,0:T(8,128)(2,1)S(1)} %get-tuple-element.16), channel_id=1, source_target_pairs={{0,14},{1,7},{2,12},{3,5},{4,10},{5,3},{6,8},{7,1},{8,6},{9,15},{1... | collective-permute-start | bytes 196616 | tf_op jit(solution)/shard_map/ppermute | solution.py:482
  8.7 0.0 collective-permute-start.1
  8.7 0.9 %collective-permute-start.2 = (bf16[2,32,512]{2,1,0:T(8,128)(2,1)S(1)}, bf16[2,32,512]{2,1,0:T(8,128)(2,1)S(1)}, u32[]{:S(2)}, u32[]{:S(2)}) collective-permute-start(bf16[2,32,512]{2,1,0:T(8,128)(2,1)S(1)} %get-tuple-element.18), channel_id=1, source_target_pairs={{0,2},{1,11},{2,0},{3,9},{4,6},{5,15},{6,4},{7,13},{8,10},{9,3},{1... | collective-permute-start | bytes 196616 | tf_op jit(solution)/shard_map/ppermute | solution.py:482
  9.6 0.7 %collective-permute-start.3 = (bf16[2,32,512]{2,1,0:T(8,128)(2,1)S(1)}, bf16[2,32,512]{2,1,0:T(8,128)(2,1)S(1)}, u32[]{:S(2)}, u32[]{:S(2)}) collective-permute-start(bf16[2,32,512]{2,1,0:T(8,128)(2,1)S(1)} %get-tuple-element.19), channel_id=1, source_target_pairs={{0,0},{1,9},{2,2},{3,11},{4,4},{5,13},{6,6},{7,15},{8,8},{9,1},{10... | collective-permute-start | bytes 196616 | tf_op jit(solution)/shard_map/ppermute | solution.py:482
  10.2 0.1 pair_shards.1.refs_2_.refs_1_
  10.4 1.2 %collective-permute-start.6 = (bf16[2,2,32,512]{3,2,1,0:T(8,128)(2,1)S(1)}, bf16[2,2,32,512]{3,2,1,0:T(8,128)(2,1)S(1)}, u32[]{:S(2)}, u32[]{:S(2)}) collective-permute-start(bf16[2,2,32,512]{3,2,1,0:T(8,128)(2,1)S(1)} %pair_shards.1.refs_2_.refs_1_), channel_id=1, source_target_pairs={{0,2},{1,5},{2,0},{3,7},{4,6},{5,1},{6,4},{7,3},{8,10},{9,13},{10,... | collective-permute-start | bytes 393224 | tf_op jit(solution)/shard_map/ppermute | solution.py:482
  11.6 1.3 %load_tables.1 = (bf16[1024,512]{1,0:T(8,128)(2,1)S(1)}, f32[96,512]{1,0:T(8,128)S(1)}) custom-call(bf16[1024,512]{1,0:T(8,128)(2,1)} %constant.12.clone.refs_0_, f32[96,512]{1,0:T(8,128)} %constant.13.clone.refs_1_, bf16[2,2,32,512]{3,2,1,0:T(8,128)(2,1)S(1)} %pair_shards.1.refs_2_.refs_1_), custom_call_target="tpu_custom_call" | custom-call | tf_op jit(solution)/shard_map/load_tables/pallas_call | solution.py:180
  12.8 1.4 %collective-permute-done.refs_0_ = bf16[2,32,512]{2,1,0:T(8,128)(2,1)S(1)} collective-permute-done((bf16[2,32,512]{2,1,0:T(8,128)(2,1)S(1)}, bf16[2,32,512]{2,1,0:T(8,128)(2,1)S(1)}, u32[]{:S(2)}, u32[]{:S(2)}) %collective-permute-start) | collective-permute-done | bytes 65568 | tf_op jit(solution)/shard_map/ppermute | solution.py:482
  14.2 0.4 %collective-permute-done.1.refs_1_ = bf16[2,32,512]{2,1,0:T(8,128)(2,1)S(1)} collective-permute-done((bf16[2,32,512]{2,1,0:T(8,128)(2,1)S(1)}, bf16[2,32,512]{2,1,0:T(8,128)(2,1)S(1)}, u32[]{:S(2)}, u32[]{:S(2)}) %collective-permute-start.1) | collective-permute-done | bytes 65568 | tf_op jit(solution)/shard_map/ppermute | solution.py:482
  14.7 0.0 collective-permute-done.2.refs_2_
  14.7 0.0 collective-permute-done.3.refs_3_
  14.7 1.2 %collective-permute-start.5 = (bf16[4,2,32,512]{3,2,1,0:T(8,128)(2,1)S(1)}, bf16[4,2,32,512]{3,2,1,0:T(8,128)(2,1)S(1)}, u32[]{:S(2)}, u32[]{:S(2)}) collective-permute-start(bf16[4,2,32,512]{3,2,1,0:T(8,128)(2,1)S(1)} %pad_maximum_fusion), channel_id=1, source_target_pairs={{0,1},{1,0},{2,3},{3,2},{4,5},{5,4},{6,7},{7,6},{8,9},{9,8},{10,11... | collective-permute-start | bytes 786440 | tf_op jit(solution)/shard_map/ppermute | solution.py:526
  15.9 0.2 collective-permute-done.6.refs_2_
  16.2 0.0 copy-start
  16.2 0.0 copy-start.1
  16.2 0.0 copy-start.2
  16.2 0.0 copy-start.3
  16.2 1.9 %collective-permute-start.7 = (bf16[4,2,32,512]{3,2,1,0:T(8,128)(2,1)S(1)}, bf16[4,2,32,512]{3,2,1,0:T(8,128)(2,1)S(1)}, u32[]{:S(2)}, u32[]{:S(2)}) collective-permute-start(bf16[4,2,32,512]{3,2,1,0:T(8,128)(2,1)S(1)} %pad_maximum_fusion.1), channel_id=1, source_target_pairs={{0,4},{1,3},{2,6},{3,1},{4,0},{5,7},{6,2},{7,5},{8,12},{9,11},{10,... | collective-permute-start | bytes 786440 | tf_op jit(solution)/shard_map/ppermute | solution.py:482
  18.2 2.3 %forward.1.refs_0_ = f32[512,512]{1,0:T(8,128)S(1)} custom-call(bf16[2,32,512]{2,1,0:T(8,128)(2,1)S(1)} %collective-permute-done.refs_0_, bf16[2,32,512]{2,1,0:T(8,128)(2,1)S(1)} %collective-permute-done.1.refs_1_, bf16[2,32,512]{2,1,0:T(8,128)(2,1)S(1)} %collective-permute-done.2.refs_2_, bf16[2,32,512]{2,1,0:T(8,128)(2,1)S(1)} %collective-permute-done.3.refs_3_, ...), custom_call_target="tpu_custom_call" | custom-call | flops 1073741824 | bytes 6291456 | tf_op jit(solution)/shard_map/forward/pallas_call | solution.py:246
  20.5 2.2 %collective-permute-done.7.refs_3_ = bf16[4,2,32,512]{3,2,1,0:T(8,128)(2,1)S(1)} collective-permute-done((bf16[4,2,32,512]{3,2,1,0:T(8,128)(2,1)S(1)}, bf16[4,2,32,512]{3,2,1,0:T(8,128)(2,1)S(1)}, u32[]{:S(2)}, u32[]{:S(2)}) %collective-permute-start.7) | collective-permute-done | bytes 262176 | tf_op jit(solution)/shard_map/ppermute | solution.py:482
  22.7 5.2 %inverse.1 = (bf16[1,1,131072]{2,1,0:T(2,128)(2,1)}, bf16[1,1,131072]{2,1,0:T(2,128)(2,1)}, f32[1,1]{1,0:T(1,128)}) custom-call(f32[512,512]{1,0:T(8,128)S(1)} %forward.1.refs_0_, bf16[2,2,32,512]{3,2,1,0:T(8,128)(2,1)S(1)} %pair_shards.1.refs_2_.refs_1_, bf16[2,2,32,512]{3,2,1,0:T(8,128)(2,1)S(1)} %collective-permute-done.6.refs_2_, ...), custom_call_target="tpu_custom_call" | custom-call | tf_op jit(solution)/shard_map/inverse/pallas_call | solution.py:452
  (11 shorter events, 0.1 us)
Async XLA Ops:
  0.6 17.5 %copy-start.5 = (bf16[1024,512]{1,0:T(8,128)(2,1)S(1)}, bf16[1024,512]{1,0:T(8,128)(2,1)}, u32[]{:S(2)}) copy-start(bf16[1024,512]{1,0:T(8,128)(2,1)} %constant.14.clone.refs_8_) | copy-start | bytes 3145732
  0.6 17.5 %copy-start.4 = (s32[8,8]{1,0:T(8,128)S(1)}, s32[8,8]{1,0:T(8,128)}, u32[]{:S(2)}) copy-start(s32[8,8]{1,0:T(8,128)} %refs_6_.2) | copy-start | bytes 772
  0.7 9.6 %collective-permute-start.4 = (bf16[1,2,16384]{2,1,0:T(2,128)(2,1)}, bf16[1,2,16384]{2,1,0:T(2,128)(2,1)S(1)}, u32[]{:S(2)}, u32[]{:S(2)}) collective-permute-start(bf16[1,2,16384]{2,1,0:T(2,128)(2,1)} %shard_hbm.1), channel_id=1, source_target_pairs={{0,8},{1,9},{2,10},{3,11},{4,12},{5,13},{6,14},{7,15},{8,0},{9,1},... | collective-permute-start | bytes 196616 | tf_op jit(solution)/shard_map/ppermute | solution.py:482
  6.4 7.8 %collective-permute-start = (bf16[2,32,512]{2,1,0:T(8,128)(2,1)S(1)}, bf16[2,32,512]{2,1,0:T(8,128)(2,1)S(1)}, u32[]{:S(2)}, u32[]{:S(2)}) collective-permute-start(bf16[2,32,512]{2,1,0:T(8,128)(2,1)S(1)} %get-tuple-element.16), channel_id=1, source_target_pairs={{0,14},{1,7},{2,12},{3,5},{4,10},{5,3},{6,8},{7,1},{8,6},{9,15},{1... | collective-permute-start | bytes 196616 | tf_op jit(solution)/shard_map/ppermute | solution.py:482
  8.7 5.9 %collective-permute-start.1 = (bf16[2,32,512]{2,1,0:T(8,128)(2,1)S(1)}, bf16[2,32,512]{2,1,0:T(8,128)(2,1)S(1)}, u32[]{:S(2)}, u32[]{:S(2)}) collective-permute-start(bf16[2,32,512]{2,1,0:T(8,128)(2,1)S(1)} %get-tuple-element.17), channel_id=1, source_target_pairs={{0,4},{1,13},{2,6},{3,15},{4,0},{5,9},{6,2},{7,11},{8,12},{9,5},{1... | collective-permute-start | bytes 196616 | tf_op jit(solution)/shard_map/ppermute | solution.py:482
  8.7 5.9 %collective-permute-start.2 = (bf16[2,32,512]{2,1,0:T(8,128)(2,1)S(1)}, bf16[2,32,512]{2,1,0:T(8,128)(2,1)S(1)}, u32[]{:S(2)}, u32[]{:S(2)}) collective-permute-start(bf16[2,32,512]{2,1,0:T(8,128)(2,1)S(1)} %get-tuple-element.18), channel_id=1, source_target_pairs={{0,2},{1,11},{2,0},{3,9},{4,6},{5,15},{6,4},{7,13},{8,10},{9,3},{1... | collective-permute-start | bytes 196616 | tf_op jit(solution)/shard_map/ppermute | solution.py:482
  9.6 5.1 %collective-permute-start.3 = (bf16[2,32,512]{2,1,0:T(8,128)(2,1)S(1)}, bf16[2,32,512]{2,1,0:T(8,128)(2,1)S(1)}, u32[]{:S(2)}, u32[]{:S(2)}) collective-permute-start(bf16[2,32,512]{2,1,0:T(8,128)(2,1)S(1)} %get-tuple-element.19), channel_id=1, source_target_pairs={{0,0},{1,9},{2,2},{3,11},{4,4},{5,13},{6,6},{7,15},{8,8},{9,1},{10... | collective-permute-start | bytes 196616 | tf_op jit(solution)/shard_map/ppermute | solution.py:482
  10.4 5.8 %collective-permute-start.6 = (bf16[2,2,32,512]{3,2,1,0:T(8,128)(2,1)S(1)}, bf16[2,2,32,512]{3,2,1,0:T(8,128)(2,1)S(1)}, u32[]{:S(2)}, u32[]{:S(2)}) collective-permute-start(bf16[2,2,32,512]{3,2,1,0:T(8,128)(2,1)S(1)} %pair_shards.1.refs_2_.refs_1_), channel_id=1, source_target_pairs={{0,2},{1,5},{2,0},{3,7},{4,6},{5,1},{6,4},{7,3},{8,10},{9,13},{10,... | collective-permute-start | bytes 393224 | tf_op jit(solution)/shard_map/ppermute | solution.py:482
  14.7 3.5 %collective-permute-start.5 = (bf16[4,2,32,512]{3,2,1,0:T(8,128)(2,1)S(1)}, bf16[4,2,32,512]{3,2,1,0:T(8,128)(2,1)S(1)}, u32[]{:S(2)}, u32[]{:S(2)}) collective-permute-start(bf16[4,2,32,512]{3,2,1,0:T(8,128)(2,1)S(1)} %pad_maximum_fusion), channel_id=1, source_target_pairs={{0,1},{1,0},{2,3},{3,2},{4,5},{5,4},{6,7},{7,6},{8,9},{9,8},{10,11... | collective-permute-start | bytes 786440 | tf_op jit(solution)/shard_map/ppermute | solution.py:526
  16.2 6.5 %copy-start = (bf16[4,256,1024]{2,1,0:T(8,128)(2,1)S(1)}, bf16[4,256,1024]{2,1,0:T(8,128)(2,1)}, u32[]{:S(2)}) copy-start(bf16[4,256,1024]{2,1,0:T(8,128)(2,1)} %constant.15.clone.refs_5_) | copy-start | bytes 6291460
  16.2 6.5 %copy-start.1 = (bf16[2,512,512]{2,1,0:T(8,128)(2,1)S(1)}, bf16[2,512,512]{2,1,0:T(8,128)(2,1)}, u32[]{:S(2)}) copy-start(bf16[2,512,512]{2,1,0:T(8,128)(2,1)} %constant.17.clone.refs_7_) | copy-start | bytes 3145732
  16.2 6.5 %copy-start.2 = (bf16[2,256,512]{2,1,0:T(8,128)(2,1)S(1)}, bf16[2,256,512]{2,1,0:T(8,128)(2,1)}, u32[]{:S(2)}) copy-start(bf16[2,256,512]{2,1,0:T(8,128)(2,1)} %constant.16.clone.refs_6_) | copy-start | bytes 1572868
  16.2 6.5 %copy-start.3 = (s32[1,3]{1,0:T(1,128)S(1)}, s32[1,3]{1,0:T(1,128)}, u32[]{:S(2)}) copy-start(s32[1,3]{1,0:T(1,128)} %refs_4_.1) | copy-start | bytes 40
  16.2 6.4 %collective-permute-start.7 = (bf16[4,2,32,512]{3,2,1,0:T(8,128)(2,1)S(1)}, bf16[4,2,32,512]{3,2,1,0:T(8,128)(2,1)S(1)}, u32[]{:S(2)}, u32[]{:S(2)}) collective-permute-start(bf16[4,2,32,512]{3,2,1,0:T(8,128)(2,1)S(1)} %pad_maximum_fusion.1), channel_id=1, source_target_pairs={{0,4},{1,3},{2,6},{3,1},{4,0},{5,7},{6,2},{7,5},{8,12},{9,11},{10,... | collective-permute-start | bytes 786440 | tf_op jit(solution)/shard_map/ppermute | solution.py:482
